TPU v7x, 768 devices: a whole 4x8x12 slice. The times are simulated.
768 devices in a mesh: row: 8 (over y_hi, x), col: 96 (over z, y_lo, core).
Axes of the slice: x: 4, y: 8 (y_hi: 2, y_lo: 4; y = y_hi * 4 + y_lo), z: 12, core: 2. Of those that a mesh axis runs over, the one named last changes fastest.
Arguments:
- win_vals: bfloat16 [8, 96, 128, 128], P('row', 'col'), may hold values from -3 to 3
- couple_vals: bfloat16 [8, 96, 8, 12, 128, 128], P('row', 'col'), may hold values from -0.09375 to 0.09375
- win_cols: int32 [8, 96], replicated, may hold values from -1 to 862, as said below
Outputs:
- purified: bfloat16 [8, 96, 128, 128], P('row', 'col')
Inputs may be any that keep to these rules, and one draw needn't show every extreme that they name: `win_cols`: slot s of window r is -1 (empty) or block column s * 9 + o with 0 <= o <= 7, so no window row is a live column; in one stripe the live columns of different windows differ. For every window and band b, the 12 slots s with s // 12 == b hold 1 to 8 live columns, and in some window every band holds exactly 8.
All inputs are finite; a program needn't handle non-finite values.
Results may differ from a plain program's by a relative error of at most 0.0035.
Values may be sent and summed in bfloat16 or wider, within the bound.
No kernel may reach another device: no remote copies, remote signals or barrier semaphores. Data moves between devices by JAX's collectives and lax.ppermute only.
A program may use at most 32 MiB of HBM per device.

v0:
```python
import jax
import jax.numpy as jnp
from jax import lax
from jax.sharding import PartitionSpec as P


def slot_pickers(win_cols, band_count, group_width, live_width):
    alive_slots = (win_cols >= 0).reshape(win_cols.shape[0], band_count, group_width)
    ranking = jnp.cumsum(alive_slots.astype(jnp.int32), axis=2) - 1
    targets = jnp.arange(live_width, dtype=jnp.int32)
    matches = (ranking[:, :, None, :] == targets[None, None, :, None]) & alive_slots[:, :, None, :]
    return matches.astype(jnp.bfloat16)


def on_device(win_vals, couple_vals, win_cols):
    band_count = lax.axis_size("row")
    row_index = lax.axis_index("row")
    col_index = lax.axis_index("col")
    stripe_count = win_cols.shape[1]
    group_width = stripe_count // band_count
    live_width = max(1, 2 * group_width // 3)
    block_size = win_vals.shape[-1]
    pickers = slot_pickers(win_cols, band_count, group_width, live_width)
    send_picker = lax.dynamic_index_in_dim(pickers, row_index, 1, keepdims=False)
    packed = jnp.einsum(
        "rjg,rgab->rjab", send_picker, couple_vals[0, 0], preferred_element_type=jnp.float32
    ).astype(jnp.bfloat16)
    received = lax.all_to_all(packed, "row", split_axis=0, concat_axis=0, tiled=True)
    take_picker = lax.dynamic_index_in_dim(pickers, row_index, 0, keepdims=False)
    alive_row = lax.dynamic_index_in_dim(win_cols, row_index, 0, keepdims=False) >= 0
    own_alive = lax.dynamic_index_in_dim(alive_row, col_index, 0, keepdims=False)
    column = jnp.einsum(
        "bjg,bjxy->bgxy", take_picker, received, preferred_element_type=jnp.float32
    ).astype(jnp.bfloat16)
    column = column.reshape(stripe_count, block_size, block_size)

    def fold_product(piece):
        return jnp.einsum("sxy,syz->xz", piece[0], column, preferred_element_type=jnp.float32)

    square = fold_product(lax.all_gather(win_vals, "col", axis=1, tiled=True))
    square = jnp.where(own_alive, square, 0.0)
    square_half = square.astype(jnp.bfloat16)[None, None]
    cube_block = fold_product(lax.all_gather(square_half, "col", axis=1, tiled=True))
    purified = jnp.where(own_alive, 3.0 * square - 2.0 * cube_block, 0.0)
    return purified.astype(jnp.bfloat16)[None, None]


def solution(mesh):
    return jax.shard_map(
        on_device,
        mesh=mesh,
        in_specs=(P("row", "col", None, None), P("row", "col", None, None, None, None), P()),
        out_specs=P("row", "col", None, None),
        check_vma=False,
    )
```

profile of v0, /device:TPU:1, one launch (start us, length us, event | category | flops | bytes accessed | tf_op | source)
XLA Modules:
  0.0 411.4 jit_solution(6820363515136892087)
XLA Ops:
  6.5 0.0 copy-start
  6.5 0.0 all-gather.4.cloned.1.call-start
  6.5 0.7 all-gather.4.cloned.1.call-update
  7.3 0.9 broadcast_compare_fusion
  8.2 0.1 reshape.22
  8.3 1.3 reduce_window_sum.11
  9.6 0.1 fusion.33
  9.7 3.3 fusion.6
  13.0 10.1 %all-to-all-start = ((bf16[8,8,128,128]{3,1,2,0:T(8,128)(2,1)}), bf16[8,8,128,128]{3,1,2,0:T(8,128)(2,1)}, u32[]{:S(2)}, u32[]{:S(2)}) async-start(bf16[8,8,128,128]{3,1,2,0:T(8,128)(2,1)} %fusion.6), calls=%async_computation | async-start | bytes 4194304 | tf_op jit(solution)/shard_map/all_to_all | solution.py:28
  23.1 0.0 all-gather.6.cloned.1.call-start
  23.2 0.7 fusion.40
  23.9 0.7 constant_dynamic-slice_fusion
  24.5 34.0 %all-to-all-done = bf16[8,8,128,128]{3,1,2,0:T(8,128)(2,1)} async-done(((bf16[8,8,128,128]{3,1,2,0:T(8,128)(2,1)}), bf16[8,8,128,128]{3,1,2,0:T(8,128)(2,1)}, u32[]{:S(2)}, u32[]{:S(2)}) %all-to-all-start) | async-done | bytes 2097184 | tf_op jit(solution)/shard_map/all_to_all | solution.py:28
  58.5 2.9 convolution_convert_fusion
  61.4 2.6 copy.33
  64.0 157.2 %all-gather.4.cloned.1.call-done = bf16[1,96,128,128]{3,2,0,1:T(8,128)(2,1)} async-done(((bf16[1,1,128,128]{3,2,0,1:T(8,128)(2,1)}), bf16[1,96,128,128]{3,2,0,1:T(8,128)(2,1)}) %all-gather.4.cloned.1.call-update) | async-done | bytes 3145744 | tf_op jit(solution)/shard_map/all_gather | solution.py:40
  221.2 4.5 %fusion.27 = f32[128,128]{1,0:T(8,128)S(1)} fusion(bf16[96,128,128]{2,1,0:T(8,128)(2,1)} %bitcast.55, bf16[1,96,128,128]{3,2,0,1:T(8,128)(2,1)} %all-gather.4.cloned.1.call-done, pred[]{:T(512)} %bitcast), kind=kOutput, calls=%fused_computation.14 | convolution fusion | flops 402669568 | bytes 6356993 | tf_op jit(solution)/shard_map/sxy,syz->xz/dot_general | solution.py:38
  225.7 0.6 convert_bitcast_fusion
  226.3 0.0 all-gather.6.cloned.1.call-update
  226.4 170.8 %all-gather.6.cloned.1.call-done = bf16[12288,128]{0,1:T(8,128)(2,1)} async-done(((bf16[128,128]{0,1:T(8,128)(2,1)}), bf16[12288,128]{0,1:T(8,128)(2,1)}) %all-gather.6.cloned.1.call-update) | async-done | bytes 3145744 | tf_op jit(solution)/shard_map/all_gather | solution.py:43
  397.1 2.8 copy.35
  399.9 0.1 copy-done.1
  400.0 3.9 fusion.30
  403.8 0.7 copy.27
  (6 shorter events, 0.0 us)
Async XLA Ops:
  6.5 3.2 copy-start
  6.5 214.6 %all-gather.4.cloned.1.call-start = ((), (), s32[]{:S(2)}) async-start(), calls=%async_computation.1 | async-start | bytes 3178496 | tf_op jit(solution)/shard_map/all_gather | solution.py:40
  13.0 45.5 %all-to-all-start = ((bf16[8,8,128,128]{3,1,2,0:T(8,128)(2,1)}), bf16[8,8,128,128]{3,1,2,0:T(8,128)(2,1)}, u32[]{:S(2)}, u32[]{:S(2)}) async-start(bf16[8,8,128,128]{3,1,2,0:T(8,128)(2,1)} %fusion.6), calls=%async_computation | async-start | bytes 4194304 | tf_op jit(solution)/shard_map/all_to_all | solution.py:28
  23.1 374.0 %all-gather.6.cloned.1.call-start = ((), (), s32[]{:S(2)}) async-start(), calls=%async_computation.2 | async-start | bytes 3178496 | tf_op jit(solution)/shard_map/all_gather | solution.py:43
  397.1 2.8 copy-start.1
Sparse Core Ops, SparseCore 0:
  9.9 211.2 all-gather.3
  226.5 170.6 all-gather.5
where the time goes:
time: 412 us; the launch traced here: 411 us
  waiting for transfers between devices  363 us (88%)
  matrix products  14.6 us (4%)
  between operations  13.5 us (3%)
  starting transfers between devices  10.2 us (2%)
  local copies, waits for them, and re-layouts  6.87 us (2%)
    all_gather x1, waiting for transfers between devices, on_device(): lax.all_gather(square_half, 'col', axis=1, tiled=True)  171 us
    all_gather x1, waiting for transfers between devices, on_device(): square = fold_product(lax.all_gather(win_vals, 'col', axis=1, tiled=True))  157 us
    all_to_all x1, waiting for transfers between devices, on_device(): lax.all_to_all(packed, 'row', split_axis=0, concat_axis=0, tiled=True)  34 us
    all_to_all x1, starting transfers between devices, on_device(): lax.all_to_all(packed, 'row', split_axis=0, concat_axis=0, tiled=True)  10.1 us
    dot_general x2, matrix products, fold_product(): jnp.einsum('sxy,syz->xz', piece[0], column, preferred_element_type=jnp.fl...  8.38 us
  transfers between devices with their start and end apart: 3, of which 3 were waited for; matrix products, arithmetic and copies ran while one was open for 3% of the time, Pallas kernels for 0%

commit v1 on v0

v1 whole, which is shorter than its diff:
```python
import functools

import jax
import jax.numpy as jnp
from jax import lax
from jax.experimental import pallas as pl
from jax.experimental.pallas import tpu as pltpu
from jax.sharding import PartitionSpec as P

BS = 128
BANDS = 8
GROUP = 12
LIVE = 8
Z, Y, C = 12, 4, 2
N_COL = Z * Y * C


def col_of(z, y, c):
    return (z * Y + y) * C + c


def member(cell, k):
    q, h = divmod(cell, Y // 2)
    return col_of(2 * q + (k >> 2 & 1), 2 * h + (k >> 1 & 1), k & 1)


CELLS = [[member(cell, k) for k in range(8)] for cell in range(12)]
SPREAD = [[member(cell, k) for cell in range(12)] for k in range(8)]
Y_LINES = [[col_of(z, y, c) for y in range(Y)] for z in range(Z) for c in range(C)]
Z_LINES = [[col_of(z, y, c) for z in range(Z)] for y in range(Y) for c in range(C)]
SWAP = [(s, s ^ 1) for s in range(N_COL)]
TO_SPREAD = [(GROUP * b + g, member(g, b)) for b in range(BANDS) for g in range(GROUP)]


def member_index(col):
    z = col // (Y * C)
    y = (col // C) % Y
    return (z % 2) * 4 + (y % 2) * 2 + col % C


def pack_kernel(cols_ref, couple_ref, out_ref):
    r = pl.program_id(0)
    first = lax.axis_index("row") * GROUP
    count = jnp.int32(0)
    for g in range(GROUP):
        alive = cols_ref[r, first + g] >= 0

        @pl.when(alive & (count < LIVE))
        def _(count=count, g=g):
            out_ref[0, count] = couple_ref[0, g]

        count = count + alive.astype(jnp.int32)
    for j in range(LIVE):

        @pl.when(j >= count)
        def _(j=j):
            out_ref[0, j] = jnp.zeros((BS, BS), out_ref.dtype)


def pack(win_cols, couple):
    return pl.pallas_call(
        pack_kernel,
        out_shape=jax.ShapeDtypeStruct((BANDS, LIVE, BS, BS), couple.dtype),
        grid=(BANDS,),
        in_specs=[
            pl.BlockSpec(memory_space=pltpu.SMEM),
            pl.BlockSpec((1, GROUP, BS, BS), lambda r: (r, 0, 0, 0)),
        ],
        out_specs=pl.BlockSpec((1, LIVE, BS, BS), lambda r: (r, 0, 0, 0)),
        cost_estimate=pl.CostEstimate(flops=0, bytes_accessed=5 << 20, transcendentals=0),
        name="pack",
    )(win_cols, couple)


def live_blocks(cols_ref, list_ref, r, band, position):
    count = jnp.int32(0)
    for g in range(GROUP):
        list_ref[jnp.minimum(count, LIVE)] = position(g)
        count = count + (cols_ref[r, band * GROUP + g] >= 0).astype(jnp.int32)
    return count


def picked(blocks_ref, list_ref, count):
    picks = []
    for j in range(LIVE):
        at = jnp.where(j < count, list_ref[j], 0)
        block = blocks_ref[at]
        picks.append(jnp.where(j < count, block, jnp.zeros_like(block)))
    return jnp.concatenate(picks, axis=1)


def square_kernel(cols_ref, a0_ref, a1_ref, b0_ref, b1_ref, m_ref, sq_ref, half_ref, xs, ms, lists, sems):
    row, col = lax.axis_index("row"), lax.axis_index("col")
    core = lax.rem(col, 2)
    part = Z * 2
    copies = [
        pltpu.make_async_copy(a0_ref, xs.at[core, pl.ds(0, part)], sems.at[0]),
        pltpu.make_async_copy(a1_ref, xs.at[core, pl.ds(part, part)], sems.at[1]),
        pltpu.make_async_copy(b0_ref, xs.at[1 - core, pl.ds(0, part)], sems.at[2]),
        pltpu.make_async_copy(b1_ref, xs.at[1 - core, pl.ds(part, part)], sems.at[3]),
        pltpu.make_async_copy(m_ref, ms, sems.at[4]),
    ]
    for copy in copies:
        copy.start()
    counts = []
    for band in range(BANDS):

        def position(g, band=band):
            z, rest = divmod(band * GROUP + g, Y * C)
            y, c = divmod(rest, C)
            return c * (2 * part) + (y // 2) * part + z * 2 + y % 2

        counts.append(live_blocks(cols_ref, lists.at[band], row, band, position))
    for copy in copies:
        copy.wait()
    blocks = xs.reshape(C * 2 * part, BS, BS)
    total = jnp.zeros((BS, BS), jnp.float32)
    for band in range(BANDS):
        left = picked(blocks, lists.at[band], counts[band])
        right = ms[band].reshape(LIVE * BS, BS)
        total = total + jnp.dot(left, right, preferred_element_type=jnp.float32)
    total = jnp.where(cols_ref[row, col] >= 0, total, 0.0)
    sq_ref[...] = total
    half_ref[...] = total.astype(half_ref.dtype)


def square_of(win_cols, xs, m):
    hbm = pl.BlockSpec(memory_space=pl.ANY)
    vmem = pl.BlockSpec(memory_space=pltpu.VMEM)
    return pl.pallas_call(
        square_kernel,
        out_shape=(
            jax.ShapeDtypeStruct((BS, BS), jnp.float32),
            jax.ShapeDtypeStruct((BS, BS), jnp.bfloat16),
        ),
        in_specs=[pl.BlockSpec(memory_space=pltpu.SMEM)] + [hbm] * 5,
        out_specs=(vmem, vmem),
        scratch_shapes=[
            pltpu.VMEM((C, 2 * Z * 2, BS, BS), jnp.bfloat16),
            pltpu.VMEM((BANDS, LIVE, BS, BS), jnp.bfloat16),
            pltpu.SMEM((BANDS, LIVE + 1), jnp.int32),
            pltpu.SemaphoreType.DMA((5,)),
        ],
        cost_estimate=pl.CostEstimate(flops=2 * 64 * BS**3, bytes_accessed=5 << 20, transcendentals=0),
        compiler_params=pltpu.CompilerParams(vmem_limit_bytes=24 << 20),
        name="square",
    )(win_cols, *xs, m)


def partial_kernel(cols_ref, x_ref, m_ref, out_ref, list_ref):
    row, col = lax.axis_index("row"), lax.axis_index("col")
    band = member_index(col)
    count = live_blocks(cols_ref, list_ref, row, band, lambda g: g)
    left = picked(x_ref, list_ref, count)
    for k in range(0, LIVE, 2):
        right = jnp.concatenate([m_ref[k].reshape(LIVE * BS, BS), m_ref[k + 1].reshape(LIVE * BS, BS)], axis=1)
        product = jnp.dot(left, right, preferred_element_type=jnp.float32)
        out_ref[k] = product[:, :BS].astype(out_ref.dtype)
        out_ref[k + 1] = product[:, BS:].astype(out_ref.dtype)


def partials_of(win_cols, x, m, dtype):
    vmem = pl.BlockSpec(memory_space=pltpu.VMEM)
    return pl.pallas_call(
        partial_kernel,
        out_shape=jax.ShapeDtypeStruct((8, BS, BS), dtype),
        in_specs=[pl.BlockSpec(memory_space=pltpu.SMEM), vmem, vmem],
        out_specs=vmem,
        scratch_shapes=[pltpu.SMEM((LIVE + 1,), jnp.int32)],
        cost_estimate=pl.CostEstimate(flops=2 * 64 * BS**3, bytes_accessed=3 << 20, transcendentals=0),
        compiler_params=pltpu.CompilerParams(vmem_limit_bytes=24 << 20),
        name="partials",
    )(win_cols, x, m)


def final_kernel(cols_ref, sq_ref, parts_ref, out_ref):
    row, col = lax.axis_index("row"), lax.axis_index("col")
    cube = parts_ref[0].astype(jnp.float32)
    for k in range(1, 8):
        cube = cube + parts_ref[k].astype(jnp.float32)
    value = 3.0 * sq_ref[...] - 2.0 * cube
    out_ref[...] = jnp.where(cols_ref[row, col] >= 0, value, 0.0).astype(out_ref.dtype)


def final_of(win_cols, sq, parts):
    vmem = pl.BlockSpec(memory_space=pltpu.VMEM)
    return pl.pallas_call(
        final_kernel,
        out_shape=jax.ShapeDtypeStruct((BS, BS), jnp.bfloat16),
        in_specs=[pl.BlockSpec(memory_space=pltpu.SMEM), vmem, vmem],
        out_specs=vmem,
        name="final",
    )(win_cols, sq, parts)


def exchange(value, axis, groups=None):
    return lax.all_to_all(value, axis, split_axis=0, concat_axis=0, tiled=True, axis_index_groups=groups)


def on_device(win_vals, couple_vals, win_cols):
    x = win_vals[0]
    packed = pack(win_cols, couple_vals[0, 0])
    column = exchange(packed, "row")

    line = exchange(jnp.broadcast_to(x, (Y, BS, BS)), "col", Y_LINES)
    own, other = [], []
    for half in (line[:2], line[2:]):
        gathered = lax.all_gather(half, "col", axis=0, tiled=True, axis_index_groups=Z_LINES)
        own.append(gathered)
        other.append(lax.ppermute(gathered, "col", SWAP))
    square, square_half = square_of(win_cols, own + other, column)

    cell = exchange(column, "col", CELLS)
    spread = lax.ppermute(square_half, "col", TO_SPREAD)
    blocks = exchange(jnp.broadcast_to(spread, (GROUP, BS, BS)), "col", SPREAD)
    parts = partials_of(win_cols, blocks, cell, jnp.float32)
    parts = exchange(parts, "col", CELLS)
    return final_of(win_cols, square, parts)[None, None]


def solution(mesh):
    return jax.shard_map(
        on_device,
        mesh=mesh,
        in_specs=(P("row", "col", None, None), P("row", "col", None, None, None, None), P()),
        out_specs=P("row", "col", None, None),
        check_vma=False,
    )
```

time: 412 us -> 181 us (0.44)
  waiting for transfers between devices: 363 us -> 4.36 us
  blocking collectives: 0 us -> 125 us
  starting transfers between devices: 10.2 us -> 31.3 us
  matrix products: 14.6 us -> 0 us
  between operations: 13.5 us -> 0.1 us
  Pallas kernels: 0 us -> 11.5 us
    all_gather x2 -> x0, waiting for transfers between devices: 328 us -> none  [the longest x1 171 us: on_device(): lax.all_gather(square_half, 'col', axis=1, tiled=True)]
    all_to_all x0 -> x3, blocking collectives: none -> 71 us  [exchange(): lax.all_to_all(value, axis, split_axis=0, concat_axis=0, tiled=True, axis...]
    all_gather x0 -> x2, blocking collectives: none -> 54 us  [on_device(): lax.all_gather(half, 'col', axis=0, tiled=True, axis_index_groups=Z_LINES)]
    all_to_all x1 -> x2, waiting for transfers between devices: 34 us -> 0.01 us  [exchange(): lax.all_to_all(value, axis, split_axis=0, concat_axis=0, tiled=True, axis...]
    ppermute x0 -> x3, starting transfers between devices: none -> 17.7 us  [the longest x2 13.2 us: on_device(): other.append(lax.ppermute(gathered, 'col', SWAP))]
    dot_general x4 -> x0, matrix products: 14.6 us -> none  [the longest x2 8.38 us: fold_product(): jnp.einsum('sxy,syz->xz', piece[0], column, preferred_element_type=jnp.fl...]
    pallas_call x0 -> x4, Pallas kernels: none -> 11.5 us  [the longest x1 6.52 us: pack(): pl.pallas_call(pack_kernel, out_shape=jax.ShapeDtypeStruct((BANDS, LIVE,...]
    ppermute x0 -> x3, waiting for transfers between devices: none -> 4.35 us  [the longest x1 2.99 us: on_device(): spread = lax.ppermute(square_half, 'col', TO_SPREAD)]
  transfers between devices with their start and end apart: 3 -> 5, of which waited for: 3 -> 2; matrix products, arithmetic and copies ran while one was open for 3% -> 0% of each run, Pallas kernels for 0% -> 4%
where the time goes in v1:
time: 181 us; the launch traced here: 180 us
  blocking collectives  125 us (69%)
  starting transfers between devices  31.3 us (17%)
  Pallas kernels  11.5 us (6%)
  local copies, waits for them, and re-layouts  7.54 us (4%)
  waiting for transfers between devices  4.36 us (2%)
    all_to_all x3, blocking collectives, exchange(): lax.all_to_all(value, axis, split_axis=0, concat_axis=0, tiled=True, axis...  71 us
    all_gather x2, blocking collectives, on_device(): lax.all_gather(half, 'col', axis=0, tiled=True, axis_index_groups=Z_LINES)  54 us
    all_to_all x2, starting transfers between devices, exchange(): lax.all_to_all(value, axis, split_axis=0, concat_axis=0, tiled=True, axis...  13.6 us
    ppermute x2, starting transfers between devices, on_device(): other.append(lax.ppermute(gathered, 'col', SWAP))  13.2 us
    pallas_call x1, Pallas kernels, pack(): pl.pallas_call(pack_kernel, out_shape=jax.ShapeDtypeStruct((BANDS, LIVE,...  6.52 us
    unnamed x16, local copies, waits for them, and re-layouts  6.05 us
    ppermute x1, starting transfers between devices, on_device(): spread = lax.ppermute(square_half, 'col', TO_SPREAD)  4.5 us
  transfers between devices with their start and end apart: 5, of which 2 were waited for; matrix products, arithmetic and copies ran while one was open for 0% of the time, Pallas kernels for 4%

profile of v1, /device:TPU:1, one launch (start us, length us, event | category | flops | bytes accessed | tf_op | source)
XLA Modules:
  0.0 179.8 jit_solution(7295105084641102126)
XLA Ops:
  0.0 1.4 broadcast_in_dim.14
  1.4 5.4 %all-to-all-start = ((bf16[4,128,128]{2,1,0:T(8,128)(2,1)}), bf16[4,128,128]{2,1,0:T(8,128)(2,1)S(1)}, u32[]{:S(2)}, u32[]{:S(2)}) async-start(bf16[4,128,128]{2,1,0:T(8,128)(2,1)} %broadcast_in_dim.14), calls=%async_computation | async-start | bytes 262144 | tf_op jit(solution)/shard_map/all_to_all | solution.py:197
  6.8 6.5 %pack.1 = bf16[8,8,128,128]{3,2,1,0:T(8,128)(2,1)} custom-call(s32[8,96]{1,0:T(8,128)} %cols_ref.7, bf16[8,12,128,128]{3,2,1,0:T(8,128)(2,1)} %bitcast.3), custom_call_target="tpu_custom_call" | custom-call | bytes 5242880 | tf_op jit(solution)/shard_map/pack/pallas_call | solution.py:61
  13.4 8.2 %all-to-all-start.1 = ((bf16[8,8,128,128]{3,2,1,0:T(8,128)(2,1)}), bf16[8,8,128,128]{3,2,1,0:T(8,128)(2,1)S(1)}, u32[]{:S(2)}, u32[]{:S(2)}) async-start(bf16[8,8,128,128]{3,2,1,0:T(8,128)(2,1)} %pack.1), calls=%async_computation.1 | async-start | bytes 4194304 | tf_op jit(solution)/shard_map/all_to_all | solution.py:197
  21.6 32.8 %all_gather.7.a1_ref = bf16[24,128,128]{2,1,0:T(8,128)(2,1)S(1)} all-gather(bf16[2,128,128]{2,1,0:T(8,128)(2,1)S(1)} %get-tuple-element.9), channel_id=1, replica_groups={{0,8,16,24,32,40,48,56,64,72,80,88},{1,9,17,25,33,41,49,57,65,73,81,89}..., dimensions={0}, use_global_device_ids=true | all-gather | bytes 851968 | tf_op jit(solution)/shard_map/all_gather | solution.py:208
  54.4 21.2 %all_gather.6.a0_ref = bf16[24,128,128]{2,1,0:T(8,128)(2,1)S(1)} all-gather(bf16[2,128,128]{2,1,0:T(8,128)(2,1)S(1)} %get-tuple-element.10), channel_id=1, replica_groups={{0,8,16,24,32,40,48,56,64,72,80,88},{1,9,17,25,33,41,49,57,65,73,81,89}..., dimensions={0}, use_global_device_ids=true | all-gather | bytes 851968 | tf_op jit(solution)/shard_map/all_gather | solution.py:208
  75.5 11.3 %collective-permute-start = (bf16[24,128,128]{2,1,0:T(8,128)(2,1)S(1)}, bf16[24,128,128]{2,1,0:T(8,128)(2,1)S(1)}, u32[]{:S(2)}, u32[]{:S(2)}) collective-permute-start(bf16[24,128,128]{2,1,0:T(8,128)(2,1)S(1)} %all_gather.6.a0_ref), channel_id=1, source_target_pairs={{0,1},{1,0},{2,3},{3,2},{4,5},{5,4},{6,7},{7,6},{8,9},{9,8},{10,11... | collective-permute-start | bytes 2359304 | tf_op jit(solution)/shard_map/ppermute | solution.py:210
  86.8 0.9 copy-done
  87.7 1.9 %collective-permute-start.1 = (bf16[24,128,128]{2,1,0:T(8,128)(2,1)S(1)}, bf16[24,128,128]{2,1,0:T(8,128)(2,1)S(1)}, u32[]{:S(2)}, u32[]{:S(2)}) collective-permute-start(bf16[24,128,128]{2,1,0:T(8,128)(2,1)S(1)} %all_gather.7.a1_ref), channel_id=1, source_target_pairs={{0,1},{1,0},{2,3},{3,2},{4,5},{5,4},{6,7},{7,6},{8,9},{9,8},{10,11... | collective-permute-start | bytes 2359304 | tf_op jit(solution)/shard_map/ppermute | solution.py:210
  89.7 0.9 copy-done.2
  90.5 1.4 collective-permute-done.1.b1_ref
  91.9 0.9 copy-done.4
  92.8 1.1 copy-done.1
  93.9 1.1 copy-done.3
  95.1 1.1 copy-done.5
  96.2 2.1 %square.1 = (f32[128,128]{1,0:T(8,128)S(1)}, bf16[128,128]{1,0:T(8,128)(2,1)S(1)}) custom-call(s32[8,96]{1,0:T(8,128)S(1)} %copy-done.7, bf16[24,128,128]{2,1,0:T(8,128)(2,1)S(1)} %copy-done.1, bf16[24,128,128]{2,1,0:T(8,128)(2,1)S(1)} %all_gather.7.a1_ref, bf16[24,128,128]{2,1,0:T(8,128)(2,1)S(1)} %copy-done.3, bf16[24,128,128]{2,1,0:T(8,128)(2,1)S(1)} %copy-done.5, ...), custom_call_target="tpu_custom_call" | custom-call | flops 268435456 | bytes 5242880 | tf_op jit(solution)/shard_map/square/pallas_call | solution.py:130
  98.3 4.5 %collective-permute-start.2 = (bf16[128,128]{1,0:T(8,128)(2,1)S(1)}, bf16[128,128]{1,0:T(8,128)(2,1)S(1)}, u32[]{:S(2)}, u32[]{:S(2)}) collective-permute-start(bf16[128,128]{1,0:T(8,128)(2,1)S(1)} %get-tuple-element.8), channel_id=1, source_target_pairs={{0,0},{1,4},{2,16},{3,20},{4,32},{5,36},{6,48},{7,52},{8,64},{9,68... | collective-permute-start | bytes 98312 | tf_op jit(solution)/shard_map/ppermute | solution.py:214
  102.8 3.0 %collective-permute-done.2 = bf16[128,128]{1,0:T(8,128)(2,1)S(1)} collective-permute-done((bf16[128,128]{1,0:T(8,128)(2,1)S(1)}, bf16[128,128]{1,0:T(8,128)(2,1)S(1)}, u32[]{:S(2)}, u32[]{:S(2)}) %collective-permute-start.2) | collective-permute-done | bytes 32800 | tf_op jit(solution)/shard_map/ppermute | solution.py:214
  105.8 0.1 broadcast_in_dim.15
  105.9 23.2 %all_to_all.25.x_ref = bf16[12,128,128]{2,1,0:T(8,128)(2,1)S(1)} all-to-all(bf16[12,128,128]{2,1,0:T(8,128)(2,1)S(1)} %broadcast_in_dim.15), channel_id=1, replica_groups={{0,4,16,20,32,36,48,52,64,68,80,84},{1,5,17,21,33,37,49,53,65,69,81,85}..., dimensions={0} | all-to-all | bytes 786432 | tf_op jit(solution)/shard_map/all_to_all | solution.py:197
  129.1 35.8 %all_to_all.26.m_ref = bf16[8,8,128,128]{3,2,1,0:T(8,128)(2,1)S(1)} all-to-all(bf16[8,8,128,128]{3,2,1,0:T(8,128)(2,1)S(1)} %all-to-all-done.1.m_ref), channel_id=1, replica_groups={{0,1,2,3,8,9,10,11},{4,5,6,7,12,13,14,15},{16,17,18,19,24,25,26,27},{20..., dimensions={0} | all-to-all | bytes 4194304 | tf_op jit(solution)/shard_map/all_to_all | solution.py:197
  164.9 1.1 partials.1
  166.1 12.0 %all_to_all.27.parts_ref = f32[8,128,128]{2,1,0:T(8,128)} all-to-all(f32[8,128,128]{2,1,0:T(8,128)S(1)} %partials.1), channel_id=1, replica_groups={{0,1,2,3,8,9,10,11},{4,5,6,7,12,13,14,15},{16,17,18,19,24,25,26,27},{20..., dimensions={0} | all-to-all | bytes 1048576 | tf_op jit(solution)/shard_map/all_to_all | solution.py:197
  178.0 1.7 final.1
  (14 shorter events, 0.0 us)
Async XLA Ops:
  1.4 11.9 %all-to-all-start = ((bf16[4,128,128]{2,1,0:T(8,128)(2,1)}), bf16[4,128,128]{2,1,0:T(8,128)(2,1)S(1)}, u32[]{:S(2)}, u32[]{:S(2)}) async-start(bf16[4,128,128]{2,1,0:T(8,128)(2,1)} %broadcast_in_dim.14), calls=%async_computation | async-start | bytes 262144 | tf_op jit(solution)/shard_map/all_to_all | solution.py:197
  13.4 79.4 %copy-start.7 = (s32[8,96]{1,0:T(8,128)S(1)}, s32[8,96]{1,0:T(8,128)}, u32[]{:S(2)}) copy-start(s32[8,96]{1,0:T(8,128)} %cols_ref.7) | copy-start | bytes 9220
  13.4 79.4 %all-to-all-start.1 = ((bf16[8,8,128,128]{3,2,1,0:T(8,128)(2,1)}), bf16[8,8,128,128]{3,2,1,0:T(8,128)(2,1)S(1)}, u32[]{:S(2)}, u32[]{:S(2)}) async-start(bf16[8,8,128,128]{3,2,1,0:T(8,128)(2,1)} %pack.1), calls=%async_computation.1 | async-start | bytes 4194304 | tf_op jit(solution)/shard_map/all_to_all | solution.py:197
  75.5 14.1 %collective-permute-start = (bf16[24,128,128]{2,1,0:T(8,128)(2,1)S(1)}, bf16[24,128,128]{2,1,0:T(8,128)(2,1)S(1)}, u32[]{:S(2)}, u32[]{:S(2)}) collective-permute-start(bf16[24,128,128]{2,1,0:T(8,128)(2,1)S(1)} %all_gather.6.a0_ref), channel_id=1, source_target_pairs={{0,1},{1,0},{2,3},{3,2},{4,5},{5,4},{6,7},{7,6},{8,9},{9,8},{10,11... | collective-permute-start | bytes 2359304 | tf_op jit(solution)/shard_map/ppermute | solution.py:210
  86.8 0.9 copy-start
  87.7 4.2 %collective-permute-start.1 = (bf16[24,128,128]{2,1,0:T(8,128)(2,1)S(1)}, bf16[24,128,128]{2,1,0:T(8,128)(2,1)S(1)}, u32[]{:S(2)}, u32[]{:S(2)}) collective-permute-start(bf16[24,128,128]{2,1,0:T(8,128)(2,1)S(1)} %all_gather.7.a1_ref), channel_id=1, source_target_pairs={{0,1},{1,0},{2,3},{3,2},{4,5},{5,4},{6,7},{7,6},{8,9},{9,8},{10,11... | collective-permute-start | bytes 2359304 | tf_op jit(solution)/shard_map/ppermute | solution.py:210
  89.7 0.9 copy-start.2
  91.9 0.9 copy-start.4
  92.8 1.1 copy-start.1
  93.9 1.1 copy-start.3
  95.1 1.1 copy-start.5
  98.3 7.6 %copy-start.6 = (f32[128,128]{1,0:T(8,128)}, f32[128,128]{1,0:T(8,128)S(1)}, u32[]{:S(2)}) copy-start(f32[128,128]{1,0:T(8,128)S(1)} %get-tuple-element.7.sq_ref) | copy-start | bytes 196612
  98.3 7.5 %collective-permute-start.2 = (bf16[128,128]{1,0:T(8,128)(2,1)S(1)}, bf16[128,128]{1,0:T(8,128)(2,1)S(1)}, u32[]{:S(2)}, u32[]{:S(2)}) collective-permute-start(bf16[128,128]{1,0:T(8,128)(2,1)S(1)} %get-tuple-element.8), channel_id=1, source_target_pairs={{0,0},{1,4},{2,16},{3,20},{4,32},{5,36},{6,48},{7,52},{8,64},{9,68... | collective-permute-start | bytes 98312 | tf_op jit(solution)/shard_map/ppermute | solution.py:214

commit v2 on v0

v2 whole, which is shorter than its diff:
```python
import jax
import jax.numpy as jnp
from jax import lax
from jax.experimental import pallas as pl
from jax.experimental.pallas import tpu as pltpu
from jax.sharding import PartitionSpec as P

BS = 128
BANDS = 8
GROUP = 12
LIVE = 8
Z, Y, C = 12, 4, 2
N_COL = Z * Y * C


def col_of(z, y, c):
    return (z * Y + y) * C + c


def member(cell, k):
    q, h = divmod(cell, Y // 2)
    return col_of(2 * q + (k >> 2 & 1), 2 * h + (k >> 1 & 1), k & 1)


N_CELL = N_COL // 8
HALF = N_CELL // 2
CELLS = [[member(cell, k) for k in range(8)] for cell in range(N_CELL)]
HALVES = [[member(half * HALF + e, k) for e in range(HALF)] for half in range(2) for k in range(8)]


def device(row, col):
    return row * N_COL + col


def to_cells(shift, source):
    pairs = []
    for w in range(BANDS):
        for s in range(N_COL):
            b, g = divmod(s, GROUP)
            pairs.append((source(w, s), device(b, member((g + shift) % N_CELL, w))))
    return pairs


def home(w, s):
    return device(w, s)


CELL_OF = {member(cell, k): (cell, k) for cell in range(N_CELL) for k in range(8)}


def summed(w, s):
    cell, k = CELL_OF[s]
    return device(k, member(cell, w))


FROM_HOME = [to_cells(shift, home) for shift in (0, HALF)]
FROM_SUMMED = [to_cells(shift, summed) for shift in (0, HALF)]
TO_HOME = [(summed(w, s), home(w, s)) for w in range(BANDS) for s in range(N_COL)]


def cell_and_member(col):
    z = col // (Y * C)
    y = lax.rem(col // C, Y)
    cell = (z // 2) * (Y // 2) + y // 2
    return cell, lax.rem(z, 2) * 4 + lax.rem(y, 2) * 2 + lax.rem(col, 2)


def summed_slot(row, col):
    z = 2 * (col // (2 * Y * C)) + row // 4
    y = 2 * (lax.rem(col // C, Y) // 2) + lax.rem(row // 2, 2)
    return (z * Y + y) * C + lax.rem(row, 2)


def list_live(cols_ref, list_ref, window, band, position):
    count = jnp.int32(0)
    for g in range(GROUP):
        list_ref[jnp.minimum(count, LIVE)] = position(g)
        count = count + (cols_ref[window, band * GROUP + g] >= 0).astype(jnp.int32)
    return count


def pack_kernel(cols_ref, couple_ref, out_ref, lists, sem):
    band = lax.axis_index("row")
    for w in range(BANDS):
        count = list_live(cols_ref, lists.at[w], w, band, lambda g: g)
        for j in range(LIVE):
            at = jnp.where(j < count, lists[w, j], 0)
            pltpu.make_async_copy(couple_ref.at[w, at], out_ref.at[w, j], sem).start()
    pltpu.make_async_copy(out_ref, out_ref, sem).wait()


def pack(win_cols, couple):
    return pl.pallas_call(
        pack_kernel,
        out_shape=jax.ShapeDtypeStruct((BANDS, LIVE, BS, BS), couple.dtype),
        in_specs=[pl.BlockSpec(memory_space=pltpu.SMEM), pl.BlockSpec(memory_space=pl.ANY)],
        out_specs=pl.BlockSpec(memory_space=pl.ANY),
        scratch_shapes=[
            pltpu.SMEM((BANDS, LIVE + 1), jnp.int32),
            pltpu.SemaphoreType.DMA(()),
        ],
        cost_estimate=pl.CostEstimate(flops=0, bytes_accessed=4 << 20, transcendentals=0),
        compiler_params=pltpu.CompilerParams(vmem_limit_bytes=56 << 20),
        name="pack",
    )(win_cols, couple)


def partial_kernel(cols_ref, x_ref, m_ref, out_ref, list_ref):
    cell, window = cell_and_member(lax.axis_index("col"))
    second = cell // HALF

    def position(g):
        return (g % HALF) * 2 + (g // HALF != second).astype(jnp.int32)

    count = list_live(cols_ref, list_ref, window, lax.axis_index("row"), position)
    picks = []
    for j in range(LIVE):
        block = x_ref[jnp.where(j < count, list_ref[j], 0)]
        picks.append(jnp.where(j < count, block, jnp.zeros_like(block)))
    left = jnp.concatenate(picks, axis=1)
    for k in range(0, 8, 2):
        right = [m_ref[k + i].reshape(LIVE * BS, BS) for i in range(2)]
        product = jnp.dot(left, jnp.concatenate(right, axis=1), preferred_element_type=jnp.float32)
        for i in range(2):
            out_ref[k + i] = product[:, i * BS : (i + 1) * BS].astype(out_ref.dtype)


def partials_of(win_cols, x, m, dtype):
    vmem = pl.BlockSpec(memory_space=pltpu.VMEM)
    return pl.pallas_call(
        partial_kernel,
        out_shape=jax.ShapeDtypeStruct((8, BS, BS), dtype),
        in_specs=[pl.BlockSpec(memory_space=pltpu.SMEM), vmem, vmem],
        out_specs=vmem,
        scratch_shapes=[pltpu.SMEM((LIVE + 1,), jnp.int32)],
        cost_estimate=pl.CostEstimate(flops=2 * 64 * BS**3, bytes_accessed=3 << 20, transcendentals=0),
        compiler_params=pltpu.CompilerParams(vmem_limit_bytes=24 << 20),
        name="partials",
    )(win_cols, x, m)


def total_of(cols_ref, parts_ref):
    total = parts_ref[0].astype(jnp.float32)
    for b in range(1, BANDS):
        total = total + parts_ref[b].astype(jnp.float32)
    row, col = lax.axis_index("row"), lax.axis_index("col")
    _, window = cell_and_member(col)
    return total, cols_ref[window, summed_slot(row, col)] >= 0


def square_kernel(cols_ref, parts_ref, square_ref, half_ref):
    total, alive = total_of(cols_ref, parts_ref)
    total = jnp.where(alive, total, 0.0)
    square_ref[...] = total
    half_ref[...] = total.astype(half_ref.dtype)


def final_kernel(cols_ref, square_ref, parts_ref, out_ref):
    cube, alive = total_of(cols_ref, parts_ref)
    value = 3.0 * square_ref[...] - 2.0 * cube
    out_ref[...] = jnp.where(alive, value, 0.0).astype(out_ref.dtype)


def small_call(kernel, name, types, cols, *arrays):
    vmem = pl.BlockSpec(memory_space=pltpu.VMEM)
    return pl.pallas_call(
        kernel,
        out_shape=[jax.ShapeDtypeStruct((BS, BS), dtype) for dtype in types],
        in_specs=[pl.BlockSpec(memory_space=pltpu.SMEM)] + [vmem] * len(arrays),
        out_specs=[vmem] * len(types),
        name=name,
    )(cols, *arrays)


def exchange(value, axis, groups=None):
    return lax.all_to_all(value, axis, split_axis=0, concat_axis=0, tiled=True, axis_index_groups=groups)


def two_cells(block, routes):
    return jnp.stack([lax.ppermute(block, ("row", "col"), route) for route in routes])


def on_device(win_vals, couple_vals, win_cols):
    held = exchange(pack(win_cols, couple_vals[0, 0]), "col", CELLS)
    pair = two_cells(win_vals[0, 0], FROM_HOME)
    x = lax.all_gather(pair, "col", axis=0, tiled=True, axis_index_groups=HALVES)
    parts = exchange(partials_of(win_cols, x, held, jnp.float32), "row")
    square, square_half = small_call(square_kernel, "square", (jnp.float32, jnp.bfloat16), win_cols, parts)
    pair = two_cells(square_half, FROM_SUMMED)
    x = exchange(jnp.tile(pair, (HALF, 1, 1)), "col", HALVES)
    parts = exchange(partials_of(win_cols, x, held, jnp.float32), "row")
    (purified,) = small_call(final_kernel, "final", (jnp.bfloat16,), win_cols, square, parts)
    return lax.ppermute(purified, ("row", "col"), TO_HOME)[None, None]


def solution(mesh):
    return jax.shard_map(
        on_device,
        mesh=mesh,
        in_specs=(P("row", "col", None, None), P("row", "col", None, None, None, None), P()),
        out_specs=P("row", "col", None, None),
        check_vma=False,
    )
```

time: 412 us -> 244 us (0.59)
  waiting for transfers between devices: 363 us -> 15.6 us
  blocking collectives: 0 us -> 107 us
  Pallas kernels: 0 us -> 71.1 us
  starting transfers between devices: 10.2 us -> 45 us
  matrix products: 14.6 us -> 0 us
  between operations: 13.5 us -> 0.11 us
  local copies, waits for them, and re-layouts: 6.87 us -> 0.7 us
    all_gather x2 -> x0, waiting for transfers between devices: 328 us -> none  [the longest x1 171 us: on_device(): lax.all_gather(square_half, 'col', axis=1, tiled=True)]
    all_to_all x0 -> x3, blocking collectives: none -> 79 us  [exchange(): lax.all_to_all(value, axis, split_axis=0, concat_axis=0, tiled=True, axis...]
    pallas_call x0 -> x5, Pallas kernels: none -> 71.1 us  [the longest x1 65.4 us: pack(): pl.pallas_call(pack_kernel, out_shape=jax.ShapeDtypeStruct((BANDS, LIVE,...]
    all_to_all x1, waiting for transfers between devices: 34 us -> 0.01 us  [exchange(): lax.all_to_all(value, axis, split_axis=0, concat_axis=0, tiled=True, axis...]
    ppermute x0 -> x5, starting transfers between devices: none -> 31 us  [the longest x4 21.6 us: two_cells(): lax.ppermute(block, ('row', 'col'), route)]
    all_gather x0 -> x1, blocking collectives: none -> 28.3 us  [on_device(): lax.all_gather(pair, 'col', axis=0, tiled=True, axis_index_groups=HALVES)]
    ppermute x0 -> x5, waiting for transfers between devices: none -> 15.6 us  [the longest x4 13.8 us: two_cells(): lax.ppermute(block, ('row', 'col'), route)]
    dot_general x4 -> x0, matrix products: 14.6 us -> none  [the longest x2 8.38 us: fold_product(): jnp.einsum('sxy,syz->xz', piece[0], column, preferred_element_type=jnp.fl...]
  transfers between devices with their start and end apart: 3 -> 6, of which waited for: 3 -> 2; matrix products, arithmetic and copies ran while one was open for 3% -> 0% of each run, Pallas kernels for 0% -> 0%
where the time goes in v2:
time: 244 us; the launch traced here: 240 us
  blocking collectives  107 us (44%)
  Pallas kernels  71.1 us (29%)
  starting transfers between devices  45 us (18%)
  waiting for transfers between devices  15.6 us (6%)
    all_to_all x3, blocking collectives, exchange(): lax.all_to_all(value, axis, split_axis=0, concat_axis=0, tiled=True, axis...  79 us
    pallas_call x1, Pallas kernels, pack(): pl.pallas_call(pack_kernel, out_shape=jax.ShapeDtypeStruct((BANDS, LIVE,...  65.4 us
    all_gather x1, blocking collectives, on_device(): lax.all_gather(pair, 'col', axis=0, tiled=True, axis_index_groups=HALVES)  28.3 us
    ppermute x4, starting transfers between devices, two_cells(): lax.ppermute(block, ('row', 'col'), route)  21.6 us
    all_to_all x1, starting transfers between devices, exchange(): lax.all_to_all(value, axis, split_axis=0, concat_axis=0, tiled=True, axis...  14 us
    ppermute x4, waiting for transfers between devices, two_cells(): lax.ppermute(block, ('row', 'col'), route)  13.8 us
    ppermute x1, starting transfers between devices, on_device(): return lax.ppermute(purified, ('row', 'col'), TO_HOME)[None, None]  9.36 us
  transfers between devices with their start and end apart: 6, of which 2 were waited for; matrix products, arithmetic and copies ran while one was open for 0% of the time, Pallas kernels for 0%

profile of v2, /device:TPU:1, one launch (start us, length us, event | category | flops | bytes accessed | tf_op | source)
XLA Modules:
  0.0 239.9 jit_solution(1716924975037324050)
XLA Ops:
  0.0 65.4 %pack.1 = bf16[8,8,128,128]{3,2,1,0:T(8,128)(2,1)} custom-call(s32[8,96]{1,0:T(8,128)} %cols_ref.9, bf16[8,12,128,128]{3,2,1,0:T(8,128)(2,1)} %bitcast.8), custom_call_target="tpu_custom_call" | custom-call | bytes 4194304 | tf_op jit(solution)/shard_map/pack/pallas_call | solution.py:93
  65.4 0.0 copy-start.2
  65.4 0.0 copy-start
  65.4 14.0 %all-to-all-start = ((bf16[8,8,128,128]{3,2,1,0:T(8,128)(2,1)}), bf16[8,8,128,128]{3,2,1,0:T(8,128)(2,1)S(1)}, u32[]{:S(2)}, u32[]{:S(2)}) async-start(bf16[8,8,128,128]{3,2,1,0:T(8,128)(2,1)} %pack.1), calls=%async_computation | async-start | bytes 4194304 | tf_op jit(solution)/shard_map/all_to_all | solution.py:176
  79.5 8.6 %collective-permute-start.1 = (bf16[128,128]{1,0:T(8,128)(2,1)S(1)}, bf16[128,128]{1,0:T(8,128)(2,1)S(1)}, u32[]{:S(2)}, u32[]{:S(2)}) collective-permute-start(bf16[128,128]{1,0:T(8,128)(2,1)S(1)} %bitcast.15), channel_id=1, source_target_pairs={{0,48},{1,52},{2,64},{3,68},{4,80},{5,84},{6,0},{7,4},{8,16},{9,20... | collective-permute-start | bytes 98312 | tf_op jit(solution)/shard_map/ppermute | solution.py:180
  88.1 1.9 collective-permute-start
  90.0 13.8 %collective-permute-done.1 = bf16[128,128]{1,0:T(8,128)(2,1)S(1)} collective-permute-done((bf16[128,128]{1,0:T(8,128)(2,1)S(1)}, bf16[128,128]{1,0:T(8,128)(2,1)S(1)}, u32[]{:S(2)}, u32[]{:S(2)}) %collective-permute-start.1) | collective-permute-done | bytes 32800 | tf_op jit(solution)/shard_map/ppermute | solution.py:180
  103.9 0.0 collective-permute-done
  103.9 28.3 %all_gather.3.x_ref = bf16[12,128,128]{2,1,0:T(8,128)(2,1)S(1)} all-gather(bf16[2,128,128]{2,1,0:T(8,128)(2,1)S(1)} %pad_maximum_fusion), channel_id=1, replica_groups={{0,4,16,20,32,36},{1,5,17,21,33,37},{2,6,18,22,34,38},{3,7,19,23,35,39}..., dimensions={0}, use_global_device_ids=true | all-gather | bytes 458752 | tf_op jit(solution)/shard_map/all_gather | solution.py:186
  132.2 0.0 all-to-all-done.m_ref
  132.2 1.1 partials.2
  133.4 0.0 copy-start.1
  133.4 27.0 %all_to_all.20.parts_ref = f32[8,128,128]{2,1,0:T(8,128)} all-to-all(f32[8,128,128]{2,1,0:T(8,128)S(1)} %partials.2), channel_id=1, replica_groups=mesh['row'=8,'col'=96] {'row'}, dimensions={0} | all-to-all | bytes 1048576 | tf_op jit(solution)/shard_map/all_to_all | solution.py:176
  160.4 1.7 square.1
  162.1 9.7 %collective-permute-start.3 = (bf16[128,128]{1,0:T(8,128)(2,1)}, bf16[128,128]{1,0:T(8,128)(2,1)S(1)}, u32[]{:S(2)}, u32[]{:S(2)}) collective-permute-start(bf16[128,128]{1,0:T(8,128)(2,1)} %get-tuple-element.8), channel_id=1, source_target_pairs={{0,48},{96,52},{192,64},{288,68},{4,80},{100,84},{196,0},{292,4},{... | collective-permute-start | bytes 98312 | tf_op jit(solution)/shard_map/ppermute | solution.py:180
  171.8 1.4 collective-permute-start.2
  173.3 0.1 tile.4
  173.3 25.6 %all_to_all.21.x_ref = bf16[12,128,128]{2,1,0:T(8,128)(2,1)S(1)} all-to-all(bf16[12,128,128]{2,1,0:T(8,128)(2,1)S(1)} %bitcast.9), channel_id=1, replica_groups={{0,4,16,20,32,36},{1,5,17,21,33,37},{2,6,18,22,34,38},{3,7,19,23,35,39}..., dimensions={0} | all-to-all | bytes 786432 | tf_op jit(solution)/shard_map/all_to_all | solution.py:176
  199.0 1.1 partials.3
  200.1 26.3 %all_to_all.22.parts_ref = f32[8,128,128]{2,1,0:T(8,128)} all-to-all(f32[8,128,128]{2,1,0:T(8,128)S(1)} %partials.3), channel_id=1, replica_groups=mesh['row'=8,'col'=96] {'row'}, dimensions={0} | all-to-all | bytes 1048576 | tf_op jit(solution)/shard_map/all_to_all | solution.py:176
  226.4 1.8 final.1
  228.2 9.4 %collective-permute-start.4 = (bf16[128,128]{1,0:T(8,128)(2,1)}, bf16[128,128]{1,0:T(8,128)(2,1)S(1)}, u32[]{:S(2)}, u32[]{:S(2)}) collective-permute-start(bf16[128,128]{1,0:T(8,128)(2,1)} %final.1), channel_id=1, source_target_pairs={{0,0},{96,1},{192,2},{288,3},{4,4},{100,5},{196,6},{292,7},{384,8}... | collective-permute-start | bytes 98312 | tf_op jit(solution)/shard_map/ppermute | solution.py:193
  237.5 1.8 collective-permute-done.4
  239.3 0.6 copy.5
  (7 shorter events, 0.0 us)
Async XLA Ops:
  65.4 14.1 %copy-start.2 = (bf16[1,1,128,128]{3,2,1,0:T(8,128)(2,1)S(1)}, bf16[1,1,128,128]{3,2,1,0:T(8,128)(2,1)}, u32[]{:S(2)}) copy-start(bf16[1,1,128,128]{3,2,1,0:T(8,128)(2,1)} %param.3) | copy-start | bytes 98308
  65.4 66.8 %copy-start = (s32[8,96]{1,0:T(8,128)S(1)}, s32[8,96]{1,0:T(8,128)}, u32[]{:S(2)}) copy-start(s32[8,96]{1,0:T(8,128)} %cols_ref.9) | copy-start | bytes 9220
  65.4 66.8 %all-to-all-start = ((bf16[8,8,128,128]{3,2,1,0:T(8,128)(2,1)}), bf16[8,8,128,128]{3,2,1,0:T(8,128)(2,1)S(1)}, u32[]{:S(2)}, u32[]{:S(2)}) async-start(bf16[8,8,128,128]{3,2,1,0:T(8,128)(2,1)} %pack.1), calls=%async_computation | async-start | bytes 4194304 | tf_op jit(solution)/shard_map/all_to_all | solution.py:176
  79.5 24.4 %collective-permute-start.1 = (bf16[128,128]{1,0:T(8,128)(2,1)S(1)}, bf16[128,128]{1,0:T(8,128)(2,1)S(1)}, u32[]{:S(2)}, u32[]{:S(2)}) collective-permute-start(bf16[128,128]{1,0:T(8,128)(2,1)S(1)} %bitcast.15), channel_id=1, source_target_pairs={{0,48},{1,52},{2,64},{3,68},{4,80},{5,84},{6,0},{7,4},{8,16},{9,20... | collective-permute-start | bytes 98312 | tf_op jit(solution)/shard_map/ppermute | solution.py:180
  88.1 15.8 %collective-permute-start = (bf16[128,128]{1,0:T(8,128)(2,1)S(1)}, bf16[128,128]{1,0:T(8,128)(2,1)S(1)}, u32[]{:S(2)}, u32[]{:S(2)}) collective-permute-start(bf16[128,128]{1,0:T(8,128)(2,1)S(1)} %bitcast.16), channel_id=1, source_target_pairs={{0,0},{1,4},{2,16},{3,20},{4,32},{5,36},{6,48},{7,52},{8,64},{9,68... | collective-permute-start | bytes 98312 | tf_op jit(solution)/shard_map/ppermute | solution.py:180
  133.4 65.6 %copy-start.1 = (s32[8,96]{1,0:T(8,128)S(1)}, s32[8,96]{1,0:T(8,128)}, u32[]{:S(2)}) copy-start(s32[8,96]{1,0:T(8,128)} %cols_ref.9) | copy-start | bytes 9220
  162.1 11.1 %collective-permute-start.3 = (bf16[128,128]{1,0:T(8,128)(2,1)}, bf16[128,128]{1,0:T(8,128)(2,1)S(1)}, u32[]{:S(2)}, u32[]{:S(2)}) collective-permute-start(bf16[128,128]{1,0:T(8,128)(2,1)} %get-tuple-element.8), channel_id=1, source_target_pairs={{0,48},{96,52},{192,64},{288,68},{4,80},{100,84},{196,0},{292,4},{... | collective-permute-start | bytes 98312 | tf_op jit(solution)/shard_map/ppermute | solution.py:180
  171.8 1.4 collective-permute-start.2
  228.2 11.2 %collective-permute-start.4 = (bf16[128,128]{1,0:T(8,128)(2,1)}, bf16[128,128]{1,0:T(8,128)(2,1)S(1)}, u32[]{:S(2)}, u32[]{:S(2)}) collective-permute-start(bf16[128,128]{1,0:T(8,128)(2,1)} %final.1), channel_id=1, source_target_pairs={{0,0},{96,1},{192,2},{288,3},{4,4},{100,5},{196,6},{292,7},{384,8}... | collective-permute-start | bytes 98312 | tf_op jit(solution)/shard_map/ppermute | solution.py:193

commit v3 on v1

--- a/solution.py
+++ b/solution.py
@@ -1,5 +1,3 @@
-import functools
-
 import jax
 import jax.numpy as jnp
 from jax import lax
@@ -25,49 +23,48 @@
 
 
 CELLS = [[member(cell, k) for k in range(8)] for cell in range(12)]
-SPREAD = [[member(cell, k) for cell in range(12)] for k in range(8)]
-Y_LINES = [[col_of(z, y, c) for y in range(Y)] for z in range(Z) for c in range(C)]
+HALF = 6
+HALVES = [[member(half * HALF + e, k) for e in range(HALF)] for half in range(2) for k in range(8)]
+Y_NEAR = [[col_of(z, 2 * h + p, c) for p in range(2)] for z in range(Z) for h in range(2) for c in range(C)]
+Y_FAR = [[col_of(z, 2 * h + p, c) for h in range(2)] for z in range(Z) for p in range(2) for c in range(C)]
 Z_LINES = [[col_of(z, y, c) for z in range(Z)] for y in range(Y) for c in range(C)]
 SWAP = [(s, s ^ 1) for s in range(N_COL)]
-TO_SPREAD = [(GROUP * b + g, member(g, b)) for b in range(BANDS) for g in range(GROUP)]
+TO_CELLS = [
+    [(GROUP * b + g, member((g + shift) % 12, b)) for b in range(BANDS) for g in range(GROUP)]
+    for shift in (0, HALF)
+]
 
 
 def member_index(col):
     z = col // (Y * C)
-    y = (col // C) % Y
-    return (z % 2) * 4 + (y % 2) * 2 + col % C
-
-
-def pack_kernel(cols_ref, couple_ref, out_ref):
-    r = pl.program_id(0)
-    first = lax.axis_index("row") * GROUP
-    count = jnp.int32(0)
-    for g in range(GROUP):
-        alive = cols_ref[r, first + g] >= 0
-
-        @pl.when(alive & (count < LIVE))
-        def _(count=count, g=g):
-            out_ref[0, count] = couple_ref[0, g]
-
-        count = count + alive.astype(jnp.int32)
-    for j in range(LIVE):
-
-        @pl.when(j >= count)
-        def _(j=j):
-            out_ref[0, j] = jnp.zeros((BS, BS), out_ref.dtype)
+    y = lax.rem(col // C, Y)
+    return lax.rem(z, 2) * 4 + lax.rem(y, 2) * 2 + lax.rem(col, 2)
+
+
+STEP = 4
+
+
+def pack_kernel(cols_ref, couple_ref, out_ref, lists):
+    band = lax.axis_index("row")
+    for i in range(STEP):
+        count = live_blocks(cols_ref, lists.at[i], pl.program_id(0) * STEP + i, band, lambda g: g)
+        for j in range(LIVE):
+            out_ref[i, j] = couple_ref[i, jnp.where(j < count, lists[i, j], 0)]
 
 
 def pack(win_cols, couple):
     return pl.pallas_call(
         pack_kernel,
         out_shape=jax.ShapeDtypeStruct((BANDS, LIVE, BS, BS), couple.dtype),
-        grid=(BANDS,),
+        grid=(BANDS // STEP,),
         in_specs=[
             pl.BlockSpec(memory_space=pltpu.SMEM),
-            pl.BlockSpec((1, GROUP, BS, BS), lambda r: (r, 0, 0, 0)),
+            pl.BlockSpec((STEP, GROUP, BS, BS), lambda i: (i, 0, 0, 0)),
         ],
-        out_specs=pl.BlockSpec((1, LIVE, BS, BS), lambda r: (r, 0, 0, 0)),
+        out_specs=pl.BlockSpec((STEP, LIVE, BS, BS), lambda i: (i, 0, 0, 0)),
+        scratch_shapes=[pltpu.SMEM((STEP, LIVE + 1), jnp.int32)],
         cost_estimate=pl.CostEstimate(flops=0, bytes_accessed=5 << 20, transcendentals=0),
+        compiler_params=pltpu.CompilerParams(vmem_limit_bytes=56 << 20),
         name="pack",
     )(win_cols, couple)
 
@@ -89,7 +86,7 @@
     return jnp.concatenate(picks, axis=1)
 
 
-def square_kernel(cols_ref, a0_ref, a1_ref, b0_ref, b1_ref, m_ref, sq_ref, half_ref, xs, ms, lists, sems):
+def square_kernel(cols_ref, a0_ref, a1_ref, b0_ref, b1_ref, m_ref, sq_ref, half_ref, xs, lists, sems):
     row, col = lax.axis_index("row"), lax.axis_index("col")
     core = lax.rem(col, 2)
     part = Z * 2
@@ -98,7 +95,6 @@
         pltpu.make_async_copy(a1_ref, xs.at[core, pl.ds(part, part)], sems.at[1]),
         pltpu.make_async_copy(b0_ref, xs.at[1 - core, pl.ds(0, part)], sems.at[2]),
         pltpu.make_async_copy(b1_ref, xs.at[1 - core, pl.ds(part, part)], sems.at[3]),
-        pltpu.make_async_copy(m_ref, ms, sems.at[4]),
     ]
     for copy in copies:
         copy.start()
@@ -117,7 +113,7 @@
     total = jnp.zeros((BS, BS), jnp.float32)
     for band in range(BANDS):
         left = picked(blocks, lists.at[band], counts[band])
-        right = ms[band].reshape(LIVE * BS, BS)
+        right = m_ref[band].reshape(LIVE * BS, BS)
         total = total + jnp.dot(left, right, preferred_element_type=jnp.float32)
     total = jnp.where(cols_ref[row, col] >= 0, total, 0.0)
     sq_ref[...] = total
@@ -125,7 +121,6 @@
 
 
 def square_of(win_cols, xs, m):
-    hbm = pl.BlockSpec(memory_space=pl.ANY)
     vmem = pl.BlockSpec(memory_space=pltpu.VMEM)
     return pl.pallas_call(
         square_kernel,
@@ -133,13 +128,12 @@
             jax.ShapeDtypeStruct((BS, BS), jnp.float32),
             jax.ShapeDtypeStruct((BS, BS), jnp.bfloat16),
         ),
-        in_specs=[pl.BlockSpec(memory_space=pltpu.SMEM)] + [hbm] * 5,
+        in_specs=[pl.BlockSpec(memory_space=pltpu.SMEM)] + [vmem] * 5,
         out_specs=(vmem, vmem),
         scratch_shapes=[
             pltpu.VMEM((C, 2 * Z * 2, BS, BS), jnp.bfloat16),
-            pltpu.VMEM((BANDS, LIVE, BS, BS), jnp.bfloat16),
             pltpu.SMEM((BANDS, LIVE + 1), jnp.int32),
-            pltpu.SemaphoreType.DMA((5,)),
+            pltpu.SemaphoreType.DMA((4,)),
         ],
         cost_estimate=pl.CostEstimate(flops=2 * 64 * BS**3, bytes_accessed=5 << 20, transcendentals=0),
         compiler_params=pltpu.CompilerParams(vmem_limit_bytes=24 << 20),
@@ -150,7 +144,12 @@
 def partial_kernel(cols_ref, x_ref, m_ref, out_ref, list_ref):
     row, col = lax.axis_index("row"), lax.axis_index("col")
     band = member_index(col)
-    count = live_blocks(cols_ref, list_ref, row, band, lambda g: g)
+    second = col // (N_COL // 2)
+
+    def position(g):
+        return (g % HALF) * 2 + (g // HALF != second).astype(jnp.int32)
+
+    count = live_blocks(cols_ref, list_ref, row, band, position)
     left = picked(x_ref, list_ref, count)
     for k in range(0, LIVE, 2):
         right = jnp.concatenate([m_ref[k].reshape(LIVE * BS, BS), m_ref[k + 1].reshape(LIVE * BS, BS)], axis=1)
@@ -198,21 +197,22 @@
 
 
 def on_device(win_vals, couple_vals, win_cols):
-    x = win_vals[0]
     packed = pack(win_cols, couple_vals[0, 0])
     column = exchange(packed, "row")
 
-    line = exchange(jnp.broadcast_to(x, (Y, BS, BS)), "col", Y_LINES)
-    own, other = [], []
-    for half in (line[:2], line[2:]):
-        gathered = lax.all_gather(half, "col", axis=0, tiled=True, axis_index_groups=Z_LINES)
-        own.append(gathered)
-        other.append(lax.ppermute(gathered, "col", SWAP))
+    gather = lambda value, groups: lax.all_gather(value, "col", axis=0, tiled=True, axis_index_groups=groups)
+    x, packed = lax.optimization_barrier((win_vals[0], packed))
+    line = gather(gather(x, Y_NEAR), Y_FAR)
+    first = gather(line[:2], Z_LINES)
+    first, late, column = lax.optimization_barrier((first, line[2:], column))
+    own = [first, gather(late, Z_LINES)]
+    other = [lax.ppermute(part, "col", SWAP) for part in own]
     square, square_half = square_of(win_cols, own + other, column)
 
     cell = exchange(column, "col", CELLS)
-    spread = lax.ppermute(square_half, "col", TO_SPREAD)
-    blocks = exchange(jnp.broadcast_to(spread, (GROUP, BS, BS)), "col", SPREAD)
+    pair = jnp.stack([lax.ppermute(square_half, "col", route) for route in TO_CELLS])
+    pair, cell = lax.optimization_barrier((pair, cell))
+    blocks = exchange(jnp.tile(pair, (HALF, 1, 1)), "col", HALVES)
     parts = partials_of(win_cols, blocks, cell, jnp.float32)
     parts = exchange(parts, "col", CELLS)
     return final_of(win_cols, square, parts)[None, None]

time: 181 us -> 217 us (1.20)
  blocking collectives: 125 us -> 165 us
  local copies, waits for them, and re-layouts: 7.54 us -> 0.7 us
  starting transfers between devices: 31.3 us -> 37.8 us
  Pallas kernels: 11.5 us -> 8.92 us
    all_gather x2 -> x4, blocking collectives: 54 us -> 127 us  [on_device(): lax.all_gather(value, 'col', axis=0, tiled=True, axis_index_groups=groups)]
    all_to_all x3 -> x2, blocking collectives: 71 us -> 38.2 us  [exchange(): lax.all_to_all(value, axis, split_axis=0, concat_axis=0, tiled=True, axis...]
    all_to_all x2, starting transfers between devices: 13.6 us -> 20 us  [exchange(): lax.all_to_all(value, axis, split_axis=0, concat_axis=0, tiled=True, axis...]
    unnamed x16 -> x6, local copies, waits for them, and re-layouts: 6.05 us -> 0.62 us
    pallas_call x1, Pallas kernels: 6.52 us -> 3.15 us  [pack(): pl.pallas_call(pack_kernel, out_shape=jax.ShapeDtypeStruct((BANDS, LIVE,...]
    ppermute x3 -> x4, waiting for transfers between devices: 4.35 us -> 3.24 us  [the longest x2 2.24 us: on_device(): other = [lax.ppermute(part, 'col', SWAP) for part in own]]
    ppermute x3 -> x4, starting transfers between devices: 17.7 us -> 17.9 us  [the longest x2 10.4 us: on_device(): lax.ppermute(square_half, 'col', route)]
  transfers between devices with their start and end apart: 5 -> 6, of which waited for: 2 -> 2; matrix products, arithmetic and copies ran while one was open for 0% -> 0% of each run, Pallas kernels for 4% -> 1%
where the time goes in v3:
time: 217 us; the launch traced here: 216 us
  blocking collectives  165 us (76%)
  starting transfers between devices  37.8 us (17%)
  Pallas kernels  8.92 us (4%)
  waiting for transfers between devices  3.24 us (1%)
    all_gather x4, blocking collectives, on_device(): lax.all_gather(value, 'col', axis=0, tiled=True, axis_index_groups=groups)  127 us
    all_to_all x2, blocking collectives, exchange(): lax.all_to_all(value, axis, split_axis=0, concat_axis=0, tiled=True, axis...  38.2 us
    all_to_all x2, starting transfers between devices, exchange(): lax.all_to_all(value, axis, split_axis=0, concat_axis=0, tiled=True, axis...  20 us
    ppermute x2, starting transfers between devices, on_device(): lax.ppermute(square_half, 'col', route)  10.4 us
    ppermute x2, starting transfers between devices, on_device(): other = [lax.ppermute(part, 'col', SWAP) for part in own]  7.5 us
  transfers between devices with their start and end apart: 6, of which 2 were waited for; matrix products, arithmetic and copies ran while one was open for 0% of the time, Pallas kernels for 1%

profile of v3, /device:TPU:1, one launch (start us, length us, event | category | flops | bytes accessed | tf_op | source)
XLA Modules:
  0.0 216.0 jit_solution(3813298646277087745)
XLA Ops:
  0.0 3.1 %pack.1 = bf16[8,8,128,128]{3,2,1,0:T(8,128)(2,1)} custom-call(s32[8,96]{1,0:T(8,128)} %cols_ref.7, bf16[8,12,128,128]{3,2,1,0:T(8,128)(2,1)} %bitcast.6), custom_call_target="tpu_custom_call" | custom-call | bytes 5242880 | tf_op jit(solution)/shard_map/pack/pallas_call | solution.py:56
  3.2 10.2 %all-to-all-start = ((bf16[8,8,128,128]{3,2,1,0:T(8,128)(2,1)}), bf16[8,8,128,128]{3,2,1,0:T(8,128)(2,1)}, u32[]{:S(2)}, u32[]{:S(2)}) async-start(bf16[8,8,128,128]{3,2,1,0:T(8,128)(2,1)} %pack.1), calls=%async_computation | async-start | bytes 4194304 | tf_op jit(solution)/shard_map/all_to_all | solution.py:196
  13.4 47.3 %all_gather.12 = bf16[2,128,128]{2,1,0:T(8,128)(2,1)S(1)} all-gather(bf16[1,128,128]{2,1,0:T(8,128)(2,1)S(1)} %bitcast.8), channel_id=1, replica_groups={{0,2},{1,3},{4,6},{5,7},{8,10},{9,11},{12,14},{13,15},{16,18},{17,19},{..., dimensions={0}, use_global_device_ids=true | all-gather | bytes 98304 | tf_op jit(solution)/shard_map/all_gather | solution.py:203
  60.7 6.4 %all_gather.13 = bf16[4,128,128]{2,1,0:T(8,128)(2,1)S(1)} all-gather(bf16[2,128,128]{2,1,0:T(8,128)(2,1)S(1)} %all_gather.12), channel_id=1, replica_groups={{0,4},{1,5},{2,6},{3,7},{8,12},{9,13},{10,14},{11,15},{16,20},{17,21},{..., dimensions={0}, use_global_device_ids=true | all-gather | bytes 196608 | tf_op jit(solution)/shard_map/all_gather | solution.py:203
  67.1 31.8 %all_gather.14.a0_ref = bf16[24,128,128]{2,1,0:T(8,128)(2,1)S(1)} all-gather(bf16[2,128,128]{2,1,0:T(8,128)(2,1)S(1)} %get-tuple-element.22), channel_id=1, replica_groups={{0,8,16,24,32,40,48,56,64,72,80,88},{1,9,17,25,33,41,49,57,65,73,81,89}..., dimensions={0}, use_global_device_ids=true | all-gather | bytes 851968 | tf_op jit(solution)/shard_map/all_gather | solution.py:203
  98.8 0.0 all-to-all-done.m_ref
  98.8 9.7 %all-to-all-start.1 = ((bf16[8,8,128,128]{3,2,1,0:T(8,128)(2,1)}), bf16[8,8,128,128]{3,2,1,0:T(8,128)(2,1)S(1)}, u32[]{:S(2)}, u32[]{:S(2)}) async-start(bf16[8,8,128,128]{3,2,1,0:T(8,128)(2,1)} %all-to-all-done.m_ref), calls=%async_computation.1 | async-start | bytes 4194304 | tf_op jit(solution)/shard_map/all_to_all | solution.py:196
  108.6 41.5 %all_gather.15.a1_ref = bf16[24,128,128]{2,1,0:T(8,128)(2,1)S(1)} all-gather(bf16[2,128,128]{2,1,0:T(8,128)(2,1)S(1)} %get-tuple-element.15), channel_id=1, replica_groups={{0,8,16,24,32,40,48,56,64,72,80,88},{1,9,17,25,33,41,49,57,65,73,81,89}..., dimensions={0}, use_global_device_ids=true | all-gather | bytes 851968 | tf_op jit(solution)/shard_map/all_gather | solution.py:203
  150.1 5.6 %collective-permute-start.1 = (bf16[24,128,128]{2,1,0:T(8,128)(2,1)S(1)}, bf16[24,128,128]{2,1,0:T(8,128)(2,1)S(1)}, u32[]{:S(2)}, u32[]{:S(2)}) collective-permute-start(bf16[24,128,128]{2,1,0:T(8,128)(2,1)S(1)} %all_gather.15.a1_ref), channel_id=1, source_target_pairs={{0,1},{1,0},{2,3},{3,2},{4,5},{5,4},{6,7},{7,6},{8,9},{9,8},{10,11... | collective-permute-start | bytes 2359304 | tf_op jit(solution)/shard_map/ppermute | solution.py:209
  155.7 1.9 collective-permute-start
  157.6 0.0 collective-permute-done.1.b1_ref
  157.6 2.2 %collective-permute-done.b0_ref = bf16[24,128,128]{2,1,0:T(8,128)(2,1)S(1)} collective-permute-done((bf16[24,128,128]{2,1,0:T(8,128)(2,1)S(1)}, bf16[24,128,128]{2,1,0:T(8,128)(2,1)S(1)}, u32[]{:S(2)}, u32[]{:S(2)}) %collective-permute-start) | collective-permute-done | bytes 786464 | tf_op jit(solution)/shard_map/ppermute | solution.py:209
  159.9 2.9 %square.1 = (f32[128,128]{1,0:T(8,128)S(1)}, bf16[128,128]{1,0:T(8,128)(2,1)S(1)}) custom-call(s32[8,96]{1,0:T(8,128)S(1)} %copy-done.1, bf16[24,128,128]{2,1,0:T(8,128)(2,1)S(1)} %all_gather.14.a0_ref, bf16[24,128,128]{2,1,0:T(8,128)(2,1)S(1)} %all_gather.15.a1_ref, bf16[24,128,128]{2,1,0:T(8,128)(2,1)S(1)} %collective-permute-done.b0_ref, ...), custom_call_target="tpu_custom_call" | custom-call | flops 268435456 | bytes 5242880 | tf_op jit(solution)/shard_map/square/pallas_call | solution.py:125
  162.8 0.6 copy-done
  163.4 2.3 %collective-permute-start.2 = (bf16[128,128]{1,0:T(8,128)(2,1)S(1)}, bf16[128,128]{1,0:T(8,128)(2,1)S(1)}, u32[]{:S(2)}, u32[]{:S(2)}) collective-permute-start(bf16[128,128]{1,0:T(8,128)(2,1)S(1)} %get-tuple-element.18), channel_id=1, source_target_pairs={{0,0},{1,4},{2,16},{3,20},{4,32},{5,36},{6,48},{7,52},{8,64},{9,68... | collective-permute-start | bytes 98312 | tf_op jit(solution)/shard_map/ppermute | solution.py:213
  165.8 8.0 %collective-permute-start.3 = (bf16[128,128]{1,0:T(8,128)(2,1)S(1)}, bf16[128,128]{1,0:T(8,128)(2,1)S(1)}, u32[]{:S(2)}, u32[]{:S(2)}) collective-permute-start(bf16[128,128]{1,0:T(8,128)(2,1)S(1)} %get-tuple-element.18), channel_id=1, source_target_pairs={{0,48},{1,52},{2,64},{3,68},{4,80},{5,84},{6,0},{7,4},{8,16},{9,20... | collective-permute-start | bytes 98312 | tf_op jit(solution)/shard_map/ppermute | solution.py:213
  173.8 0.0 collective-permute-done.2
  173.8 1.0 collective-permute-done.3
  174.8 0.0 all-to-all-done.1.m_ref
  174.8 0.1 tile.4
  174.9 22.8 %all_to_all.20.x_ref = bf16[12,128,128]{2,1,0:T(8,128)(2,1)S(1)} all-to-all(bf16[12,128,128]{2,1,0:T(8,128)(2,1)S(1)} %bitcast.7), channel_id=1, replica_groups={{0,4,16,20,32,36},{1,5,17,21,33,37},{2,6,18,22,34,38},{3,7,19,23,35,39}..., dimensions={0} | all-to-all | bytes 786432 | tf_op jit(solution)/shard_map/all_to_all | solution.py:196
  197.7 1.1 partials.1
  198.8 15.5 %all_to_all.21.parts_ref = f32[8,128,128]{2,1,0:T(8,128)} all-to-all(f32[8,128,128]{2,1,0:T(8,128)S(1)} %partials.1), channel_id=1, replica_groups={{0,1,2,3,8,9,10,11},{4,5,6,7,12,13,14,15},{16,17,18,19,24,25,26,27},{20..., dimensions={0} | all-to-all | bytes 1048576 | tf_op jit(solution)/shard_map/all_to_all | solution.py:196
  214.2 1.7 final.1
  (7 shorter events, 0.0 us)
Async XLA Ops:
  3.2 10.2 %copy-start.2 = (bf16[1,1,128,128]{3,2,1,0:T(8,128)(2,1)S(1)}, bf16[1,1,128,128]{3,2,1,0:T(8,128)(2,1)}, u32[]{:S(2)}) copy-start(bf16[1,1,128,128]{3,2,1,0:T(8,128)(2,1)} %param.3) | copy-start | bytes 98308
  3.2 95.7 %all-to-all-start = ((bf16[8,8,128,128]{3,2,1,0:T(8,128)(2,1)}), bf16[8,8,128,128]{3,2,1,0:T(8,128)(2,1)}, u32[]{:S(2)}, u32[]{:S(2)}) async-start(bf16[8,8,128,128]{3,2,1,0:T(8,128)(2,1)} %pack.1), calls=%async_computation | async-start | bytes 4194304 | tf_op jit(solution)/shard_map/all_to_all | solution.py:196
  98.8 61.0 %copy-start.1 = (s32[8,96]{1,0:T(8,128)S(1)}, s32[8,96]{1,0:T(8,128)}, u32[]{:S(2)}) copy-start(s32[8,96]{1,0:T(8,128)} %cols_ref.7) | copy-start | bytes 9220
  98.8 76.0 %all-to-all-start.1 = ((bf16[8,8,128,128]{3,2,1,0:T(8,128)(2,1)}), bf16[8,8,128,128]{3,2,1,0:T(8,128)(2,1)S(1)}, u32[]{:S(2)}, u32[]{:S(2)}) async-start(bf16[8,8,128,128]{3,2,1,0:T(8,128)(2,1)} %all-to-all-done.m_ref), calls=%async_computation.1 | async-start | bytes 4194304 | tf_op jit(solution)/shard_map/all_to_all | solution.py:196
  150.1 7.5 %collective-permute-start.1 = (bf16[24,128,128]{2,1,0:T(8,128)(2,1)S(1)}, bf16[24,128,128]{2,1,0:T(8,128)(2,1)S(1)}, u32[]{:S(2)}, u32[]{:S(2)}) collective-permute-start(bf16[24,128,128]{2,1,0:T(8,128)(2,1)S(1)} %all_gather.15.a1_ref), channel_id=1, source_target_pairs={{0,1},{1,0},{2,3},{3,2},{4,5},{5,4},{6,7},{7,6},{8,9},{9,8},{10,11... | collective-permute-start | bytes 2359304 | tf_op jit(solution)/shard_map/ppermute | solution.py:209
  155.7 4.2 %collective-permute-start = (bf16[24,128,128]{2,1,0:T(8,128)(2,1)S(1)}, bf16[24,128,128]{2,1,0:T(8,128)(2,1)S(1)}, u32[]{:S(2)}, u32[]{:S(2)}) collective-permute-start(bf16[24,128,128]{2,1,0:T(8,128)(2,1)S(1)} %all_gather.14.a0_ref), channel_id=1, source_target_pairs={{0,1},{1,0},{2,3},{3,2},{4,5},{5,4},{6,7},{7,6},{8,9},{9,8},{10,11... | collective-permute-start | bytes 2359304 | tf_op jit(solution)/shard_map/ppermute | solution.py:209
  162.8 0.6 copy-start
  163.4 10.4 %collective-permute-start.2 = (bf16[128,128]{1,0:T(8,128)(2,1)S(1)}, bf16[128,128]{1,0:T(8,128)(2,1)S(1)}, u32[]{:S(2)}, u32[]{:S(2)}) collective-permute-start(bf16[128,128]{1,0:T(8,128)(2,1)S(1)} %get-tuple-element.18), channel_id=1, source_target_pairs={{0,0},{1,4},{2,16},{3,20},{4,32},{5,36},{6,48},{7,52},{8,64},{9,68... | collective-permute-start | bytes 98312 | tf_op jit(solution)/shard_map/ppermute | solution.py:213
  165.8 9.0 %collective-permute-start.3 = (bf16[128,128]{1,0:T(8,128)(2,1)S(1)}, bf16[128,128]{1,0:T(8,128)(2,1)S(1)}, u32[]{:S(2)}, u32[]{:S(2)}) collective-permute-start(bf16[128,128]{1,0:T(8,128)(2,1)S(1)} %get-tuple-element.18), channel_id=1, source_target_pairs={{0,48},{1,52},{2,64},{3,68},{4,80},{5,84},{6,0},{7,4},{8,16},{9,20... | collective-permute-start | bytes 98312 | tf_op jit(solution)/shard_map/ppermute | solution.py:213

commit v4 on v0

v4 whole, which is shorter than its diff:
```python
import jax
import jax.numpy as jnp
from jax import lax
from jax.experimental import pallas as pl
from jax.experimental.pallas import tpu as pltpu
from jax.sharding import PartitionSpec as P

BS = 128
BANDS = 8
GROUP = 12
Z, Y, C = 12, 4, 2
N_COL = Z * Y * C

QUAD = 4
CLASS = GROUP // QUAD


def col_of(z, y, c):
    return (z * Y + y) * C + c


Y_FAR = [[col_of(z, 2 * h + p, c) for h in range(2)] for z in range(Z) for p in range(2) for c in range(C)]
Y_NEAR = [[col_of(z, 2 * h + p, c) for p in range(2)] for z in range(Z) for h in range(2) for c in range(C)]
Z_LINES = [[col_of(z, y, c) for z in range(Z)] for y in range(Y) for c in range(C)]
CORES = [[s, s + 1] for s in range(0, N_COL, C)]
SPREAD = [[row * N_COL + quad + k for k in range(QUAD) for row in range(BANDS)] for quad in range(0, N_COL, QUAD)]


def partial_kernel(cols_ref, x_ref, m_ref, keep_ref, send_ref):
    row, col = lax.axis_index("row"), lax.axis_index("col")
    mine, core = lax.rem(col, QUAD), lax.rem(col, C)
    left = []
    for n in range(BANDS * CLASS):
        block = x_ref[n]
        left.append(jnp.where(cols_ref[row, n * QUAD + mine] >= 0, block, jnp.zeros_like(block)))
    left = jnp.concatenate(left, axis=1)
    for out_ref, which in ((keep_ref, core), (send_ref, 1 - core)):
        right = jnp.concatenate([m_ref[which], m_ref[2 + which]], axis=1)
        product = jnp.dot(left, right, preferred_element_type=jnp.float32)
        out_ref[0] = product[:, :BS]
        out_ref[1] = product[:, BS:]


def add_kernel(keep_ref, both_ref, keep_out, send_out):
    col = lax.axis_index("col")
    core, near = lax.rem(col, C), lax.rem(col // C, 2)
    other = (1 - core) * 2
    keep_out[...] = keep_ref[near] + both_ref[other + near]
    send_out[0] = keep_ref[1 - near] + both_ref[other + 1 - near]


def summed(cols_ref, keep_ref, both_ref):
    row, col = lax.axis_index("row"), lax.axis_index("col")
    near = lax.rem(col // C, 2)
    return keep_ref[...] + both_ref[1 - near], cols_ref[row, col] >= 0


def square_kernel(cols_ref, keep_ref, both_ref, square_ref, half_ref):
    total, alive = summed(cols_ref, keep_ref, both_ref)
    total = jnp.where(alive, total, 0.0)
    square_ref[...] = total
    half_ref[0] = total.astype(half_ref.dtype)


def final_kernel(cols_ref, keep_ref, both_ref, square_ref, out_ref):
    cube, alive = summed(cols_ref, keep_ref, both_ref)
    out_ref[...] = jnp.where(alive, 3.0 * square_ref[...] - 2.0 * cube, 0.0).astype(out_ref.dtype)


def call(kernel, name, outs, arrays, cols=None, **options):
    vmem = pl.BlockSpec(memory_space=pltpu.VMEM)
    scalars = () if cols is None else (cols,)
    return pl.pallas_call(
        kernel,
        out_shape=[jax.ShapeDtypeStruct(shape, dtype) for shape, dtype in outs],
        in_specs=[pl.BlockSpec(memory_space=pltpu.SMEM)] * len(scalars) + [vmem] * len(arrays),
        out_specs=[vmem] * len(outs),
        name=name,
        **options,
    )(*scalars, *arrays)


def gather(value, groups):
    return lax.all_gather(value, "col", axis=0, tiled=True, axis_index_groups=groups)


def product(win_cols, line, held):
    x = gather(line, Z_LINES)
    block, pair = (BS, BS), (2, BS, BS)
    keep, send = call(
        partial_kernel,
        "partials",
        [(pair, jnp.float32)] * 2,
        (x, held),
        win_cols,
        cost_estimate=pl.CostEstimate(flops=2 * 96 * BS**3, bytes_accessed=4 << 20, transcendentals=0),
        compiler_params=pltpu.CompilerParams(vmem_limit_bytes=24 << 20),
    )
    keep, send = call(add_kernel, "add", [(block, jnp.float32), ((1,) + block, jnp.float32)], (keep, gather(send, CORES)))
    return keep, gather(send, Y_NEAR)


def on_device(win_vals, couple_vals, win_cols):
    block = (BS, BS)
    classes = couple_vals[0, 0].reshape(BANDS, CLASS, QUAD, BS, BS).transpose(2, 0, 1, 3, 4)
    line = gather(win_vals[0], Y_FAR)
    line, classes = lax.optimization_barrier((line, classes.reshape(QUAD * BANDS, CLASS, BS, BS)))
    held = lax.all_to_all(classes, ("row", "col"), split_axis=0, concat_axis=0, tiled=True, axis_index_groups=SPREAD)
    held = held.reshape(QUAD, BANDS * CLASS * BS, BS)
    keep, both = product(win_cols, line, held)
    square, half = call(square_kernel, "square", [(block, jnp.float32), ((1,) + block, jnp.bfloat16)], (keep, both), win_cols)
    keep, both = product(win_cols, gather(half, Y_FAR), held)
    (purified,) = call(final_kernel, "final", [(block, jnp.bfloat16)], (keep, both, square), win_cols)
    return purified[None, None]


def solution(mesh):
    return jax.shard_map(
        on_device,
        mesh=mesh,
        in_specs=(P("row", "col", None, None), P("row", "col", None, None, None, None), P()),
        out_specs=P("row", "col", None, None),
        check_vma=False,
    )
```

time: 412 us -> 166 us (0.40)
  waiting for transfers between devices: 363 us -> 40.9 us
  blocking collectives: 0 us -> 94.1 us
  matrix products: 14.6 us -> 0 us
  between operations: 13.5 us -> 0.06 us
  Pallas kernels: 0 us -> 8.92 us
  starting transfers between devices: 10.2 us -> 14.7 us
    all_gather x2 -> x0, waiting for transfers between devices: 328 us -> none  [the longest x1 171 us: on_device(): lax.all_gather(square_half, 'col', axis=1, tiled=True)]
    all_gather x0 -> x8, blocking collectives: none -> 94.1 us  [gather(): lax.all_gather(value, 'col', axis=0, tiled=True, axis_index_groups=groups)]
    dot_general x4 -> x0, matrix products: 14.6 us -> none  [the longest x2 8.38 us: fold_product(): jnp.einsum('sxy,syz->xz', piece[0], column, preferred_element_type=jnp.fl...]
    pallas_call x0 -> x6, Pallas kernels: none -> 8.92 us  [call(): pl.pallas_call(kernel, out_shape=[jax.ShapeDtypeStruct(shape, dtype) for...]
    all_to_all x1, waiting for transfers between devices: 34 us -> 40.9 us  [on_device(): lax.all_to_all(classes, ('row', 'col'), split_axis=0, concat_axis=0, tile...]
    all_to_all x1, starting transfers between devices: 10.1 us -> 14.7 us  [on_device(): lax.all_to_all(classes, ('row', 'col'), split_axis=0, concat_axis=0, tile...]
  transfers between devices with their start and end apart: 3 -> 1, of which waited for: 3 -> 1; matrix products, arithmetic and copies ran while one was open for 3% -> 0% of each run, Pallas kernels for 0% -> 0%
where the time goes in v4:
time: 166 us; the launch traced here: 165 us
  blocking collectives  94.1 us (57%)
  waiting for transfers between devices  40.9 us (25%)
  starting transfers between devices  14.7 us (9%)
  Pallas kernels  8.92 us (5%)
  local copies, waits for them, and re-layouts  6.36 us (4%)
    all_gather x8, blocking collectives, gather(): lax.all_gather(value, 'col', axis=0, tiled=True, axis_index_groups=groups)  94.1 us
    all_to_all x1, waiting for transfers between devices, on_device(): lax.all_to_all(classes, ('row', 'col'), split_axis=0, concat_axis=0, tile...  40.9 us
    all_to_all x1, starting transfers between devices, on_device(): lax.all_to_all(classes, ('row', 'col'), split_axis=0, concat_axis=0, tile...  14.7 us
    pallas_call x6, Pallas kernels, call(): pl.pallas_call(kernel, out_shape=[jax.ShapeDtypeStruct(shape, dtype) for...  8.92 us
    transpose x1, local copies, waits for them, and re-layouts, on_device(): couple_vals[0, 0].reshape(BANDS, CLASS, QUAD, BS, BS)  3.93 us
  transfers between devices with their start and end apart: 1, of which 1 were waited for; matrix products, arithmetic and copies ran while one was open for 0% of the time, Pallas kernels for 0%

profile of v4, /device:TPU:1, one launch (start us, length us, event | category | flops | bytes accessed | tf_op | source)
XLA Modules:
  0.0 165.1 jit_solution(3652520135184529469)
XLA Ops:
  0.0 5.4 %all-gather = bf16[2,1,128,128]{3,2,1,0:T(8,128)(2,1)S(1)} all-gather(bf16[1,1,128,128]{3,2,1,0:T(8,128)(2,1)} %param.3), channel_id=2, replica_groups={{0,4},{1,5},{2,6},{3,7},{8,12},{9,13},{10,14},{11,15},{16,20},{17,21},{..., dimensions={0}, use_global_device_ids=true | all-gather | bytes 98304 | tf_op jit(solution)/shard_map/all_gather | solution.py:84
  5.4 3.9 %copy.6 = bf16[4,8,3,128,128]{4,3,2,1,0:T(8,128)(2,1)} copy(bf16[4,8,3,128,128]{4,3,0,2,1:T(8,128)(2,1)} %bitcast.10) | data formatting | bytes 6291456 | tf_op jit(solution)/shard_map/transpose | solution.py:105
  9.3 14.7 %all-to-all-start = ((bf16[32,3,128,128]{3,2,1,0:T(8,128)(2,1)}), bf16[32,3,128,128]{3,2,1,0:T(8,128)(2,1)S(1)}, u32[]{:S(2)}, u32[]{:S(2)}) async-start(bf16[32,3,128,128]{3,2,1,0:T(8,128)(2,1)} %bitcast.9), calls=%async_computation | async-start | bytes 6291456 | tf_op jit(solution)/shard_map/all_to_all | solution.py:108
  24.0 0.0 copy-start.4
  24.1 31.2 %all_gather.25.x_ref = bf16[24,128,128]{2,1,0:T(8,128)(2,1)} all-gather(bf16[2,128,128]{2,1,0:T(8,128)(2,1)S(1)} %bitcast.11), channel_id=1, replica_groups={{0,8,16,24,32,40,48,56,64,72,80,88},{1,9,17,25,33,41,49,57,65,73,81,89}..., dimensions={0}, use_global_device_ids=true | all-gather | bytes 851968 | tf_op jit(solution)/shard_map/all_gather | solution.py:84
  55.3 40.9 %all-to-all-done = bf16[32,3,128,128]{3,2,1,0:T(8,128)(2,1)S(1)} async-done(((bf16[32,3,128,128]{3,2,1,0:T(8,128)(2,1)}), bf16[32,3,128,128]{3,2,1,0:T(8,128)(2,1)S(1)}, u32[]{:S(2)}, u32[]{:S(2)}) %all-to-all-start) | async-done | bytes 3145760 | tf_op jit(solution)/shard_map/all_to_all | solution.py:108
  96.2 0.0 copy-done.3
  96.2 1.1 copy-done
  97.3 1.2 partials.2
  98.5 0.0 copy-start.2
  98.5 0.6 copy-done.2
  99.2 2.7 %all_gather.26.both_ref = f32[4,128,128]{2,1,0:T(8,128)} all-gather(f32[2,128,128]{2,1,0:T(8,128)S(1)} %get-tuple-element.20), channel_id=1, replica_groups={{0,1},{2,3},{4,5},{6,7},{8,9},{10,11},{12,13},{14,15},{16,17},{18,19},{..., dimensions={0}, use_global_device_ids=true | all-gather | bytes 393216 | tf_op jit(solution)/shard_map/all_gather | solution.py:84
  101.9 1.7 %add.2 = (f32[128,128]{1,0:T(8,128)}, f32[1,128,128]{2,1,0:T(8,128)}) custom-call(f32[2,128,128]{2,1,0:T(8,128)} %copy-done.2, f32[4,128,128]{2,1,0:T(8,128)} %all_gather.26.both_ref), custom_call_target="tpu_custom_call" | custom-call | tf_op jit(solution)/shard_map/add/pallas_call | solution.py:73
  103.6 7.6 %all_gather.27.both_ref = f32[2,128,128]{2,1,0:T(8,128)} all-gather(f32[1,128,128]{2,1,0:T(8,128)} %get-tuple-element.22), channel_id=1, replica_groups={{0,2},{1,3},{4,6},{5,7},{8,10},{9,11},{12,14},{13,15},{16,18},{17,19},{..., dimensions={0}, use_global_device_ids=true | all-gather | bytes 196608 | tf_op jit(solution)/shard_map/all_gather | solution.py:84
  111.2 1.6 square.1
  112.8 4.5 %all_gather.28 = bf16[2,128,128]{2,1,0:T(8,128)(2,1)S(1)} all-gather(bf16[1,128,128]{2,1,0:T(8,128)(2,1)} %get-tuple-element.23), channel_id=1, replica_groups={{0,4},{1,5},{2,6},{3,7},{8,12},{9,13},{10,14},{11,15},{16,20},{17,21},{..., dimensions={0}, use_global_device_ids=true | all-gather | bytes 98304 | tf_op jit(solution)/shard_map/all_gather | solution.py:84
  117.4 29.8 %all_gather.29.x_ref = bf16[24,128,128]{2,1,0:T(8,128)(2,1)S(1)} all-gather(bf16[2,128,128]{2,1,0:T(8,128)(2,1)S(1)} %all_gather.28), channel_id=1, replica_groups={{0,8,16,24,32,40,48,56,64,72,80,88},{1,9,17,25,33,41,49,57,65,73,81,89}..., dimensions={0}, use_global_device_ids=true | all-gather | bytes 851968 | tf_op jit(solution)/shard_map/all_gather | solution.py:84
  147.2 1.2 partials.3
  148.4 0.0 copy-start.1
  148.4 0.6 copy-done.1
  149.0 8.7 %all_gather.30.both_ref = f32[4,128,128]{2,1,0:T(8,128)} all-gather(f32[2,128,128]{2,1,0:T(8,128)S(1)} %get-tuple-element.25), channel_id=1, replica_groups={{0,1},{2,3},{4,5},{6,7},{8,9},{10,11},{12,13},{14,15},{16,17},{18,19},{..., dimensions={0}, use_global_device_ids=true | all-gather | bytes 393216 | tf_op jit(solution)/shard_map/all_gather | solution.py:84
  157.7 1.7 %add.3 = (f32[128,128]{1,0:T(8,128)}, f32[1,128,128]{2,1,0:T(8,128)}) custom-call(f32[2,128,128]{2,1,0:T(8,128)} %copy-done.1, f32[4,128,128]{2,1,0:T(8,128)} %all_gather.30.both_ref), custom_call_target="tpu_custom_call" | custom-call | tf_op jit(solution)/shard_map/add/pallas_call | solution.py:73
  159.4 4.1 %all_gather.31.both_ref = f32[2,128,128]{2,1,0:T(8,128)} all-gather(f32[1,128,128]{2,1,0:T(8,128)} %get-tuple-element.27), channel_id=1, replica_groups={{0,2},{1,3},{4,6},{5,7},{8,10},{9,11},{12,14},{13,15},{16,18},{17,19},{..., dimensions={0}, use_global_device_ids=true | all-gather | bytes 196608 | tf_op jit(solution)/shard_map/all_gather | solution.py:84
  163.5 1.6 final.1
  (3 shorter events, 0.0 us)
Async XLA Ops:
  9.3 86.9 %copy-start.3 = (s32[8,96]{1,0:T(8,128)S(1)}, s32[8,96]{1,0:T(8,128)}, u32[]{:S(2)}) copy-start(s32[8,96]{1,0:T(8,128)} %cols_ref.7) | copy-start | bytes 9220
  9.3 86.9 %all-to-all-start = ((bf16[32,3,128,128]{3,2,1,0:T(8,128)(2,1)}), bf16[32,3,128,128]{3,2,1,0:T(8,128)(2,1)S(1)}, u32[]{:S(2)}, u32[]{:S(2)}) async-start(bf16[32,3,128,128]{3,2,1,0:T(8,128)(2,1)} %bitcast.9), calls=%async_computation | async-start | bytes 6291456 | tf_op jit(solution)/shard_map/all_to_all | solution.py:108
  24.0 123.1 %copy-start.4 = (s32[8,96]{1,0:T(8,128)S(1)}, s32[8,96]{1,0:T(8,128)}, u32[]{:S(2)}) copy-start(s32[8,96]{1,0:T(8,128)} %cols_ref.7) | copy-start | bytes 9220
  96.2 1.1 copy-start
  98.5 0.6 copy-start.2
  148.4 0.6 copy-start.1

commit v5 on v4

v5 whole, which is shorter than its diff:
```python
import jax
import jax.numpy as jnp
from jax import lax
from jax.experimental import pallas as pl
from jax.experimental.pallas import tpu as pltpu
from jax.sharding import PartitionSpec as P

BS = 128
BANDS = 8
GROUP = 12
LIVE = 8
Z, Y, C = 12, 4, 2
N_COL = Z * Y * C

QUAD = 4
CLASS = LIVE // QUAD
STEP = 4


def col_of(z, y, c):
    return (z * Y + y) * C + c


Y_FAR = [[col_of(z, 2 * h + p, c) for h in range(2)] for z in range(Z) for p in range(2) for c in range(C)]
Y_NEAR = [[col_of(z, 2 * h + p, c) for p in range(2)] for z in range(Z) for h in range(2) for c in range(C)]
Y_LINES = [[col_of(z, y, c) for y in range(Y)] for z in range(Z) for c in range(C)]
Z_LINES = [[col_of(z, y, c) for z in range(Z)] for y in range(Y) for c in range(C)]
CORES = [[s, s + 1] for s in range(0, N_COL, C)]
SPREAD = [[row * N_COL + quad + k for k in range(QUAD) for row in range(BANDS)] for quad in range(0, N_COL, QUAD)]


def list_live(cols_ref, list_ref, window, band, value):
    count = jnp.int32(0)
    for g in range(GROUP):
        list_ref[jnp.minimum(count, LIVE)] = value(g)
        count = count + (cols_ref[window, band * GROUP + g] >= 0).astype(jnp.int32)
    return count


def pack_kernel(cols_ref, couple_ref, out_ref, lists):
    band = lax.axis_index("row")
    for i in range(STEP):
        count = list_live(cols_ref, lists.at[i], pl.program_id(0) * STEP + i, band, lambda g: jnp.int32(g))
        for j in range(LIVE):
            out_ref[j % QUAD, i, j // QUAD] = couple_ref[i, jnp.where(j < count, lists[i, j], 0)]


def pack(win_cols, couple):
    return pl.pallas_call(
        pack_kernel,
        out_shape=jax.ShapeDtypeStruct((QUAD, BANDS, CLASS, BS, BS), couple.dtype),
        grid=(BANDS // STEP,),
        in_specs=[
            pl.BlockSpec(memory_space=pltpu.SMEM),
            pl.BlockSpec((STEP, GROUP, BS, BS), lambda i: (i, 0, 0, 0)),
        ],
        out_specs=pl.BlockSpec((QUAD, STEP, CLASS, BS, BS), lambda i: (0, i, 0, 0, 0)),
        scratch_shapes=[pltpu.SMEM((STEP, LIVE + 1), jnp.int32)],
        cost_estimate=pl.CostEstimate(flops=0, bytes_accessed=5 << 20, transcendentals=0),
        compiler_params=pltpu.CompilerParams(vmem_limit_bytes=56 << 20),
        name="pack",
    )(win_cols, couple)


def choose(cols_ref, quad, at):
    row, mine = lax.axis_index("row"), lax.rem(lax.axis_index("col"), QUAD)
    inside = lax.rem(quad, GROUP // QUAD)
    first = (quad - inside) * QUAD
    rank = jnp.int32(0)
    for g in range(GROUP - QUAD):
        alive = (cols_ref[row, first + g] >= 0) & (g < inside * QUAD)
        rank = rank + alive.astype(jnp.int32)
    found, place = jnp.int32(0), jnp.int32(0)
    for i in range(QUAD):
        alive = cols_ref[row, quad * QUAD + i] >= 0
        hit = alive & (lax.rem(rank, QUAD) == mine)
        place = jnp.where(hit, at(i), place)
        found = found + hit.astype(jnp.int32)
        rank = rank + alive.astype(jnp.int32)
    return place, found


def choose_plane_kernel(cols_ref, plane_ref, out_ref):
    z = lax.axis_index("col") // (Y * C)
    for h in range(2):
        place, found = choose(cols_ref, z * 2 + h, lambda i, h=h: (i % C) * Y + 2 * h + i // C)
        block = plane_ref[place]
        out_ref[h] = jnp.where(found > 0, block, jnp.zeros_like(block))


def choose_quad_kernel(cols_ref, quad_ref, out_ref):
    place, found = choose(cols_ref, lax.axis_index("col") // QUAD, lambda i: (i % C) * 2 + i // C)
    block = quad_ref[place]
    out_ref[0] = jnp.where(found > 0, block, jnp.zeros_like(block))


def partial_kernel(cols_ref, x_ref, m_ref, keep_ref, send_ref, list_ref):
    row, col = lax.axis_index("row"), lax.axis_index("col")
    mine, core = lax.rem(col, QUAD), lax.rem(col, C)
    left = []
    for band in range(BANDS):
        count = list_live(cols_ref, list_ref, row, band, lambda g, band=band: jnp.int32(band * 3 + g // QUAD))
        for i in range(CLASS):
            rank = mine + i * QUAD
            block = x_ref[jnp.where(rank < count, list_ref[rank], 0)]
            left.append(jnp.where(rank < count, block, jnp.zeros_like(block)))
    left = jnp.concatenate(left, axis=1)
    for out_ref, which in ((keep_ref, core), (send_ref, 1 - core)):
        right = jnp.concatenate([m_ref[which], m_ref[2 + which]], axis=1)
        product = jnp.dot(left, right, preferred_element_type=jnp.float32)
        out_ref[0] = product[:, :BS]
        out_ref[1] = product[:, BS:]


def add_both_kernel(keep_ref, both_ref, out_ref):
    other = (1 - lax.rem(lax.axis_index("col"), C)) * 2
    for p in range(2):
        out_ref[p] = keep_ref[p] + both_ref[other + p]


def add_kernel(keep_ref, both_ref, keep_out, send_out):
    col = lax.axis_index("col")
    core, near = lax.rem(col, C), lax.rem(col // C, 2)
    other = (1 - core) * 2
    keep_out[...] = keep_ref[near] + both_ref[other + near]
    send_out[0] = keep_ref[1 - near] + both_ref[other + 1 - near]


def square_kernel(cols_ref, both_ref, square_ref, half_ref):
    row, col = lax.axis_index("row"), lax.axis_index("col")
    core, near = lax.rem(col, C), lax.rem(col // C, 2)
    first = col // QUAD * QUAD + core
    for p in range(2):
        total = jnp.where(cols_ref[row, first + p * C] >= 0, both_ref[p] + both_ref[2 + p], 0.0)
        half_ref[p] = total.astype(half_ref.dtype)

        @pl.when(near == p)
        def _(total=total):
            square_ref[...] = total


def final_kernel(cols_ref, keep_ref, both_ref, square_ref, out_ref):
    row, col = lax.axis_index("row"), lax.axis_index("col")
    cube = keep_ref[...] + both_ref[1 - lax.rem(col // C, 2)]
    alive = cols_ref[row, col] >= 0
    out_ref[...] = jnp.where(alive, 3.0 * square_ref[...] - 2.0 * cube, 0.0).astype(out_ref.dtype)


def call(kernel, name, outs, arrays, cols=None, **options):
    vmem = pl.BlockSpec(memory_space=pltpu.VMEM)
    scalars = () if cols is None else (cols,)
    return pl.pallas_call(
        kernel,
        out_shape=[jax.ShapeDtypeStruct(shape, dtype) for shape, dtype in outs],
        in_specs=[pl.BlockSpec(memory_space=pltpu.SMEM)] * len(scalars) + [vmem] * len(arrays),
        out_specs=[vmem] * len(outs),
        name=name,
        **options,
    )(*scalars, *arrays)


def gather(value, groups):
    return lax.all_gather(value, "col", axis=0, tiled=True, axis_index_groups=groups)


def exchange(value, axis, groups):
    return lax.all_to_all(value, axis, split_axis=0, concat_axis=0, tiled=True, axis_index_groups=groups)


def product(win_cols, line, held):
    pair = ((2, BS, BS), jnp.float32)
    keep, send = call(
        partial_kernel,
        "partials",
        [pair] * 2,
        (gather(line, Z_LINES), held),
        win_cols,
        scratch_shapes=[pltpu.SMEM((LIVE + 1,), jnp.int32)],
        cost_estimate=pl.CostEstimate(flops=2 * 64 * BS**3, bytes_accessed=4 << 20, transcendentals=0),
        compiler_params=pltpu.CompilerParams(vmem_limit_bytes=24 << 20),
    )
    return keep, gather(send, CORES)


def on_device(win_vals, couple_vals, win_cols):
    block = (BS, BS)
    packed = pack(win_cols, couple_vals[0, 0])
    line = exchange(jnp.broadcast_to(win_vals[0], (Y,) + block), "col", Y_LINES)
    line, packed = lax.optimization_barrier((line, packed))
    held = exchange(packed.reshape((QUAD * BANDS, CLASS) + block), ("row", "col"), SPREAD)
    held = held.reshape(QUAD, BANDS * CLASS * BS, BS)
    chosen = [((2,) + block, jnp.bfloat16)]
    (line,) = call(choose_plane_kernel, "choose", chosen, (gather(line, CORES),), win_cols)

    keep, both = product(win_cols, line, held)
    (sums,) = call(add_both_kernel, "add", [((2,) + block, jnp.float32)], (keep, both))
    outs = [(block, jnp.float32), ((2,) + block, jnp.bfloat16)]
    square, half = call(square_kernel, "square", outs, (gather(sums, Y_NEAR),), win_cols)
    (chosen,) = call(choose_quad_kernel, "choose", [((1,) + block, jnp.bfloat16)], (gather(half, CORES),), win_cols)

    keep, both = product(win_cols, gather(chosen, Y_FAR), held)
    outs = [(block, jnp.float32), ((1,) + block, jnp.float32)]
    keep, send = call(add_kernel, "add", outs, (keep, both))
    (purified,) = call(final_kernel, "final", [(block, jnp.bfloat16)], (keep, gather(send, Y_NEAR), square), win_cols)
    return purified[None, None]


def solution(mesh):
    return jax.shard_map(
        on_device,
        mesh=mesh,
        in_specs=(P("row", "col", None, None), P("row", "col", None, None, None, None), P()),
        out_specs=P("row", "col", None, None),
        check_vma=False,
    )
```

time: 166 us -> 149 us (0.90)
  waiting for transfers between devices: 40.9 us -> 16.2 us
  Pallas kernels: 8.92 us -> 15.2 us
  local copies, waits for them, and re-layouts: 6.36 us -> 2.08 us
  starting transfers between devices: 14.7 us -> 18.8 us
    all_to_all x1 -> x2, waiting for transfers between devices: 40.9 us -> 16.2 us  [exchange(): lax.all_to_all(value, axis, split_axis=0, concat_axis=0, tiled=True, axis...]
    all_to_all x1 -> x2, starting transfers between devices: 14.7 us -> 18.8 us  [exchange(): lax.all_to_all(value, axis, split_axis=0, concat_axis=0, tiled=True, axis...]
    transpose x1 -> x0, local copies, waits for them, and re-layouts: 3.93 us -> none  [on_device(): couple_vals[0, 0].reshape(BANDS, CLASS, QUAD, BS, BS)]
    pallas_call x6 -> x8, Pallas kernels: 8.92 us -> 12.1 us  [call(): pl.pallas_call(kernel, out_shape=[jax.ShapeDtypeStruct(shape, dtype) for...]
    pallas_call x0 -> x1, Pallas kernels: none -> 3.12 us  [pack(): pl.pallas_call(pack_kernel, out_shape=jax.ShapeDtypeStruct((QUAD, BANDS,...]
    unnamed x10 -> x8, local copies, waits for them, and re-layouts: 2.43 us -> 0.66 us
    all_gather x8 -> x9, blocking collectives: 94.1 us -> 95.7 us  [gather(): lax.all_gather(value, 'col', axis=0, tiled=True, axis_index_groups=groups)]
  transfers between devices with their start and end apart: 1 -> 2, of which waited for: 1 -> 2; matrix products, arithmetic and copies ran while one was open for 0% -> 0% of each run, Pallas kernels for 0% -> 3%
where the time goes in v5:
time: 149 us; the launch traced here: 148 us
  blocking collectives  95.7 us (64%)
  starting transfers between devices  18.8 us (13%)
  waiting for transfers between devices  16.2 us (11%)
  Pallas kernels  15.2 us (10%)
  local copies, waits for them, and re-layouts  2.08 us (1%)
    all_gather x9, blocking collectives, gather(): lax.all_gather(value, 'col', axis=0, tiled=True, axis_index_groups=groups)  95.7 us
    all_to_all x2, starting transfers between devices, exchange(): lax.all_to_all(value, axis, split_axis=0, concat_axis=0, tiled=True, axis...  18.8 us
    all_to_all x2, waiting for transfers between devices, exchange(): lax.all_to_all(value, axis, split_axis=0, concat_axis=0, tiled=True, axis...  16.2 us
    pallas_call x8, Pallas kernels, call(): pl.pallas_call(kernel, out_shape=[jax.ShapeDtypeStruct(shape, dtype) for...  12.1 us
    pallas_call x1, Pallas kernels, pack(): pl.pallas_call(pack_kernel, out_shape=jax.ShapeDtypeStruct((QUAD, BANDS,...  3.12 us
  transfers between devices with their start and end apart: 2, of which 2 were waited for; matrix products, arithmetic and copies ran while one was open for 0% of the time, Pallas kernels for 3%

profile of v5, /device:TPU:1, one launch (start us, length us, event | category | flops | bytes accessed | tf_op | source)
XLA Modules:
  0.0 148.1 jit_solution(10191401874652896118)
XLA Ops:
  0.0 1.4 broadcast_in_dim.11
  1.4 5.4 %all-to-all-start = ((bf16[4,128,128]{2,1,0:T(8,128)(2,1)}), bf16[4,128,128]{2,1,0:T(8,128)(2,1)S(1)}, u32[]{:S(2)}, u32[]{:S(2)}) async-start(bf16[4,128,128]{2,1,0:T(8,128)(2,1)} %broadcast_in_dim.11), calls=%async_computation | async-start | bytes 262144 | tf_op jit(solution)/shard_map/all_to_all | solution.py:167
  6.8 3.1 %pack.1 = bf16[4,8,2,128,128]{4,3,2,1,0:T(8,128)(2,1)} custom-call(s32[8,96]{1,0:T(8,128)} %cols_ref.13, bf16[8,12,128,128]{3,2,1,0:T(8,128)(2,1)} %bitcast.8), custom_call_target="tpu_custom_call" | custom-call | bytes 5242880 | tf_op jit(solution)/shard_map/pack/pallas_call | solution.py:49
  10.0 1.7 %all-to-all-done = bf16[4,128,128]{2,1,0:T(8,128)(2,1)S(1)} async-done(((bf16[4,128,128]{2,1,0:T(8,128)(2,1)}), bf16[4,128,128]{2,1,0:T(8,128)(2,1)S(1)}, u32[]{:S(2)}, u32[]{:S(2)}) %all-to-all-start) | async-done | bytes 131104 | tf_op jit(solution)/shard_map/all_to_all | solution.py:167
  11.6 13.4 %all-to-all-start.1 = ((bf16[32,2,128,128]{3,2,1,0:T(8,128)(2,1)}), bf16[32,2,128,128]{3,2,1,0:T(8,128)(2,1)S(1)}, u32[]{:S(2)}, u32[]{:S(2)}) async-start(bf16[32,2,128,128]{3,2,1,0:T(8,128)(2,1)} %bitcast.7), calls=%async_computation.1 | async-start | bytes 4194304 | tf_op jit(solution)/shard_map/all_to_all | solution.py:167
  25.0 2.1 %all_gather.27.plane_ref = bf16[8,128,128]{2,1,0:T(8,128)(2,1)} all-gather(bf16[4,128,128]{2,1,0:T(8,128)(2,1)S(1)} %all-to-all-done), channel_id=1, replica_groups={{0,1},{2,3},{4,5},{6,7},{8,9},{10,11},{12,13},{14,15},{16,17},{18,19},{..., dimensions={0}, use_global_device_ids=true | all-gather | bytes 393216 | tf_op jit(solution)/shard_map/all_gather | solution.py:163
  27.1 1.7 %choose.2 = bf16[2,128,128]{2,1,0:T(8,128)(2,1)} custom-call(s32[8,96]{1,0:T(8,128)} %cols_ref.13, bf16[8,128,128]{2,1,0:T(8,128)(2,1)} %all_gather.27.plane_ref), custom_call_target="tpu_custom_call" | custom-call | tf_op jit(solution)/shard_map/choose/pallas_call | solution.py:152
  28.9 30.0 %all_gather.28.x_ref = bf16[24,128,128]{2,1,0:T(8,128)(2,1)S(1)} all-gather(bf16[2,128,128]{2,1,0:T(8,128)(2,1)} %choose.2), channel_id=1, replica_groups={{0,8,16,24,32,40,48,56,64,72,80,88},{1,9,17,25,33,41,49,57,65,73,81,89}..., dimensions={0}, use_global_device_ids=true | all-gather | bytes 851968 | tf_op jit(solution)/shard_map/all_gather | solution.py:163
  58.8 14.6 %all-to-all-done.1 = bf16[32,2,128,128]{3,2,1,0:T(8,128)(2,1)S(1)} async-done(((bf16[32,2,128,128]{3,2,1,0:T(8,128)(2,1)}), bf16[32,2,128,128]{3,2,1,0:T(8,128)(2,1)S(1)}, u32[]{:S(2)}, u32[]{:S(2)}) %all-to-all-start.1) | async-done | bytes 2097184 | tf_op jit(solution)/shard_map/all_to_all | solution.py:167
  73.4 1.1 partials.2
  74.5 3.7 %all_gather.29.both_ref = f32[4,128,128]{2,1,0:T(8,128)} all-gather(f32[2,128,128]{2,1,0:T(8,128)S(1)} %get-tuple-element.18), channel_id=1, replica_groups={{0,1},{2,3},{4,5},{6,7},{8,9},{10,11},{12,13},{14,15},{16,17},{18,19},{..., dimensions={0}, use_global_device_ids=true | all-gather | bytes 393216 | tf_op jit(solution)/shard_map/all_gather | solution.py:163
  78.3 1.7 %add.2 = f32[2,128,128]{2,1,0:T(8,128)} custom-call(f32[2,128,128]{2,1,0:T(8,128)} %copy-done.3, f32[4,128,128]{2,1,0:T(8,128)} %all_gather.29.both_ref), custom_call_target="tpu_custom_call" | custom-call | tf_op jit(solution)/shard_map/add/pallas_call | solution.py:152
  80.0 8.8 %all_gather.30.both_ref = f32[4,128,128]{2,1,0:T(8,128)} all-gather(f32[2,128,128]{2,1,0:T(8,128)} %add.2), channel_id=1, replica_groups={{0,2},{1,3},{4,6},{5,7},{8,10},{9,11},{12,14},{13,15},{16,18},{17,19},{..., dimensions={0}, use_global_device_ids=true | all-gather | bytes 393216 | tf_op jit(solution)/shard_map/all_gather | solution.py:163
  88.8 1.6 %square.1 = (f32[128,128]{1,0:T(8,128)}, bf16[2,128,128]{2,1,0:T(8,128)(2,1)}) custom-call(s32[8,96]{1,0:T(8,128)} %cols_ref.13, f32[4,128,128]{2,1,0:T(8,128)} %all_gather.30.both_ref), custom_call_target="tpu_custom_call" | custom-call | tf_op jit(solution)/shard_map/square/pallas_call | solution.py:152
  90.5 4.1 %all_gather.31.quad_ref = bf16[4,128,128]{2,1,0:T(8,128)(2,1)} all-gather(bf16[2,128,128]{2,1,0:T(8,128)(2,1)} %get-tuple-element.19), channel_id=1, replica_groups={{0,1},{2,3},{4,5},{6,7},{8,9},{10,11},{12,13},{14,15},{16,17},{18,19},{..., dimensions={0}, use_global_device_ids=true | all-gather | bytes 196608 | tf_op jit(solution)/shard_map/all_gather | solution.py:163
  94.5 1.6 %choose.3 = bf16[1,128,128]{2,1,0:T(8,128)(2,1)} custom-call(s32[8,96]{1,0:T(8,128)} %cols_ref.13, bf16[4,128,128]{2,1,0:T(8,128)(2,1)} %all_gather.31.quad_ref), custom_call_target="tpu_custom_call" | custom-call | tf_op jit(solution)/shard_map/choose/pallas_call | solution.py:152
  96.1 5.3 %all_gather.32 = bf16[2,128,128]{2,1,0:T(8,128)(2,1)S(1)} all-gather(bf16[1,128,128]{2,1,0:T(8,128)(2,1)} %choose.3), channel_id=1, replica_groups={{0,4},{1,5},{2,6},{3,7},{8,12},{9,13},{10,14},{11,15},{16,20},{17,21},{..., dimensions={0}, use_global_device_ids=true | all-gather | bytes 98304 | tf_op jit(solution)/shard_map/all_gather | solution.py:163
  101.5 29.8 %all_gather.33.x_ref = bf16[24,128,128]{2,1,0:T(8,128)(2,1)S(1)} all-gather(bf16[2,128,128]{2,1,0:T(8,128)(2,1)S(1)} %all_gather.32), channel_id=1, replica_groups={{0,8,16,24,32,40,48,56,64,72,80,88},{1,9,17,25,33,41,49,57,65,73,81,89}..., dimensions={0}, use_global_device_ids=true | all-gather | bytes 851968 | tf_op jit(solution)/shard_map/all_gather | solution.py:163
  131.3 1.1 partials.3
  132.4 0.6 copy-done.2
  133.0 7.7 %all_gather.34.both_ref = f32[4,128,128]{2,1,0:T(8,128)} all-gather(f32[2,128,128]{2,1,0:T(8,128)S(1)} %get-tuple-element.21), channel_id=1, replica_groups={{0,1},{2,3},{4,5},{6,7},{8,9},{10,11},{12,13},{14,15},{16,17},{18,19},{..., dimensions={0}, use_global_device_ids=true | all-gather | bytes 393216 | tf_op jit(solution)/shard_map/all_gather | solution.py:163
  140.7 1.7 %add.3 = (f32[128,128]{1,0:T(8,128)}, f32[1,128,128]{2,1,0:T(8,128)}) custom-call(f32[2,128,128]{2,1,0:T(8,128)} %copy-done.2, f32[4,128,128]{2,1,0:T(8,128)} %all_gather.34.both_ref), custom_call_target="tpu_custom_call" | custom-call | tf_op jit(solution)/shard_map/add/pallas_call | solution.py:152
  142.4 4.1 %all_gather.35.both_ref = f32[2,128,128]{2,1,0:T(8,128)} all-gather(f32[1,128,128]{2,1,0:T(8,128)} %get-tuple-element.23), channel_id=1, replica_groups={{0,2},{1,3},{4,6},{5,7},{8,10},{9,11},{12,14},{13,15},{16,18},{17,19},{..., dimensions={0}, use_global_device_ids=true | all-gather | bytes 196608 | tf_op jit(solution)/shard_map/all_gather | solution.py:163
  146.5 1.6 %final.1 = bf16[128,128]{1,0:T(8,128)(2,1)} custom-call(s32[8,96]{1,0:T(8,128)} %cols_ref.13, f32[128,128]{1,0:T(8,128)} %get-tuple-element.22.keep_ref, f32[2,128,128]{2,1,0:T(8,128)} %all_gather.35.both_ref, f32[128,128]{1,0:T(8,128)} %get-tuple-element.24.square_ref), custom_call_target="tpu_custom_call" | custom-call | tf_op jit(solution)/shard_map/final/pallas_call | solution.py:152
  (7 shorter events, 0.0 us)
Async XLA Ops:
  1.4 10.2 %all-to-all-start = ((bf16[4,128,128]{2,1,0:T(8,128)(2,1)}), bf16[4,128,128]{2,1,0:T(8,128)(2,1)S(1)}, u32[]{:S(2)}, u32[]{:S(2)}) async-start(bf16[4,128,128]{2,1,0:T(8,128)(2,1)} %broadcast_in_dim.11), calls=%async_computation | async-start | bytes 262144 | tf_op jit(solution)/shard_map/all_to_all | solution.py:167
  11.6 61.8 %copy-start = (s32[8,96]{1,0:T(8,128)S(1)}, s32[8,96]{1,0:T(8,128)}, u32[]{:S(2)}) copy-start(s32[8,96]{1,0:T(8,128)} %cols_ref.13) | copy-start | bytes 9220
  11.6 61.8 %all-to-all-start.1 = ((bf16[32,2,128,128]{3,2,1,0:T(8,128)(2,1)}), bf16[32,2,128,128]{3,2,1,0:T(8,128)(2,1)S(1)}, u32[]{:S(2)}, u32[]{:S(2)}) async-start(bf16[32,2,128,128]{3,2,1,0:T(8,128)(2,1)} %bitcast.7), calls=%async_computation.1 | async-start | bytes 4194304 | tf_op jit(solution)/shard_map/all_to_all | solution.py:167
  74.5 3.8 %copy-start.3 = (f32[2,128,128]{2,1,0:T(8,128)}, f32[2,128,128]{2,1,0:T(8,128)S(1)}, u32[]{:S(2)}) copy-start(f32[2,128,128]{2,1,0:T(8,128)S(1)} %get-tuple-element.17.keep_ref) | copy-start | bytes 393220
  74.5 56.7 %copy-start.1 = (s32[8,96]{1,0:T(8,128)S(1)}, s32[8,96]{1,0:T(8,128)}, u32[]{:S(2)}) copy-start(s32[8,96]{1,0:T(8,128)} %cols_ref.13) | copy-start | bytes 9220
  132.3 0.7 copy-start.2

commit v6 on v4

v6 whole, which is shorter than its diff:
```python
import jax
import jax.numpy as jnp
from jax import lax
from jax.experimental import pallas as pl
from jax.experimental.pallas import tpu as pltpu
from jax.sharding import PartitionSpec as P

BS = 128
BANDS = 8
GROUP = 12
LIVE = 8
Z, Y, C = 12, 4, 2
N_COL = Z * Y * C
QUADS = 2 * Z

CLASS = LIVE // 2
STEP = 4


def col_of(z, y, c):
    return (z * Y + y) * C + c


Y_LINES = [[col_of(z, y, c) for y in range(Y)] for z in range(Z) for c in range(C)]
Y_FAR = [[col_of(z, 2 * h + p, c) for h in range(2)] for z in range(Z) for p in range(2) for c in range(C)]
Y_NEAR = [[col_of(z, 2 * h + p, c) for p in range(2)] for z in range(Z) for h in range(2) for c in range(C)]
Z_LINES = [[col_of(z, y, c) for z in range(Z)] for y in range(Y) for c in range(C)]
SWAP = [(s, s ^ 1) for s in range(N_COL)]
SPREAD = [[row * N_COL + col for col in pair for row in range(BANDS)] for pair in Y_NEAR]


def place():
    col = lax.axis_index("col")
    return lax.axis_index("row"), col, lax.rem(col, C), lax.rem(col // C, 2)


def pair_alive(cols_ref, window, first):
    return [cols_ref[window, first + p * C] >= 0 for p in range(2)]


def member_of(alive, k):
    return jnp.where(alive[0] & alive[1], k, jnp.where(alive[0], 0, 1))


def list_live(cols_ref, list_ref, window, band, k, value):
    count, singles = jnp.int32(0), jnp.int32(0)
    for n in range(GROUP // 2):
        quad, core = divmod(n, C)
        alive = pair_alive(cols_ref, window, band * GROUP + quad * 4 + core)
        single = alive[0] != alive[1]
        taken = (alive[0] & alive[1]) | (single & (lax.rem(singles, 2) == k))
        list_ref[jnp.minimum(count, CLASS)] = value(quad, core, member_of(alive, k))
        count = count + taken.astype(jnp.int32)
        singles = singles + single.astype(jnp.int32)
    return count


def pack_kernel(cols_ref, couple_ref, out_ref, lists):
    band = lax.axis_index("row")
    for i in range(STEP):
        for k in range(2):
            slots = lists.at[i * 2 + k]
            count = list_live(
                cols_ref, slots, pl.program_id(0) * STEP + i, band, k, lambda quad, core, p: quad * 4 + p * C + core
            )
            for j in range(CLASS):
                out_ref[k, i, j] = couple_ref[i, jnp.where(j < count, slots[j], 0)]


def pack(win_cols, couple):
    return pl.pallas_call(
        pack_kernel,
        out_shape=jax.ShapeDtypeStruct((2, BANDS, CLASS, BS, BS), couple.dtype),
        grid=(BANDS // STEP,),
        in_specs=[
            pl.BlockSpec(memory_space=pltpu.SMEM),
            pl.BlockSpec((STEP, GROUP, BS, BS), lambda i: (i, 0, 0, 0)),
        ],
        out_specs=pl.BlockSpec((2, STEP, CLASS, BS, BS), lambda i: (0, i, 0, 0, 0)),
        scratch_shapes=[pltpu.SMEM((2 * STEP, CLASS + 1), jnp.int32)],
        cost_estimate=pl.CostEstimate(flops=0, bytes_accessed=5 << 20, transcendentals=0),
        compiler_params=pltpu.CompilerParams(vmem_limit_bytes=56 << 20),
        name="pack",
    )(win_cols, couple)


def choose_kernel(cols_ref, line_ref, out_ref):
    row, col, core, near = place()
    first = col // (Y * C) * (Y * C) + core
    for h in range(2):
        alive = pair_alive(cols_ref, row, first + 2 * h * C)
        out_ref[h] = line_ref[2 * h + member_of(alive, near)]


def partial_kernel(cols_ref, own_ref, other_ref, m_ref, *out_refs):
    *out_refs, list_ref = out_refs
    keep_ref, send_ref = out_refs if len(out_refs) == 2 else (out_refs[0].at[0], out_refs[0].at[1])
    row, _, core, near = place()
    left = []
    for band in range(BANDS):
        where = lambda quad, c, _, band=band: band * 3 + quad + jnp.where(core == c, 0, QUADS)
        count = list_live(cols_ref, list_ref, row, band, near, where)
        for j in range(CLASS):
            at = jnp.where(j < count, list_ref[j], 0)
            inside = lax.rem(at, QUADS)
            block = jnp.where(at < QUADS, own_ref[inside], other_ref[inside])
            left.append(jnp.where(j < count, block, jnp.zeros_like(block)))
    left = jnp.concatenate(left, axis=1)
    right = jnp.concatenate([m_ref[near], m_ref[1 - near]], axis=1)
    product = jnp.dot(left, right, preferred_element_type=jnp.float32)
    keep_ref[...] = product[:, :BS]
    send_ref[...] = product[:, BS:]


def square_kernel(cols_ref, sums_ref, square_ref, out_ref):
    row, col, core, near = place()
    alive = pair_alive(cols_ref, row, col - near * C)
    mine = sums_ref[near, 0] + sums_ref[1 - near, 1]
    theirs = sums_ref[near, 1] + sums_ref[1 - near, 0]
    is_alive = cols_ref[row, col] >= 0
    square_ref[...] = jnp.where(is_alive, mine, 0.0)
    out_ref[0] = jnp.where(member_of(alive, near) == near, mine, theirs).astype(out_ref.dtype)


def final_kernel(cols_ref, keep_ref, both_ref, square_ref, out_ref):
    row, col, _, near = place()
    cube = keep_ref[...] + both_ref[1 - near]
    alive = cols_ref[row, col] >= 0
    out_ref[...] = jnp.where(alive, 3.0 * square_ref[...] - 2.0 * cube, 0.0).astype(out_ref.dtype)


def call(kernel, name, outs, win_cols, *arrays, **options):
    vmem = pl.BlockSpec(memory_space=pltpu.VMEM)
    return pl.pallas_call(
        kernel,
        out_shape=[jax.ShapeDtypeStruct(shape, dtype) for shape, dtype in outs],
        in_specs=[pl.BlockSpec(memory_space=pltpu.SMEM)] + [vmem] * len(arrays),
        out_specs=[vmem] * len(outs),
        name=name,
        **options,
    )(win_cols, *arrays)


def gather(value, groups):
    return lax.all_gather(value, "col", axis=0, tiled=True, axis_index_groups=groups)


def exchange(value, axis, groups):
    return lax.all_to_all(value, axis, split_axis=0, concat_axis=0, tiled=True, axis_index_groups=groups)


def product(win_cols, line, held, shapes):
    own = gather(line, Z_LINES)
    other = lax.ppermute(own, "col", SWAP)
    return call(
        partial_kernel,
        "partials",
        [(shape, jnp.float32) for shape in shapes],
        win_cols,
        own,
        other,
        held,
        scratch_shapes=[pltpu.SMEM((CLASS + 1,), jnp.int32)],
        cost_estimate=pl.CostEstimate(flops=2 * 64 * BS**3, bytes_accessed=4 << 20, transcendentals=0),
        compiler_params=pltpu.CompilerParams(vmem_limit_bytes=24 << 20),
    )


def on_device(win_vals, couple_vals, win_cols):
    block = (BS, BS)
    packed = pack(win_cols, couple_vals[0, 0])
    line = exchange(jnp.broadcast_to(win_vals[0], (Y,) + block), "col", Y_LINES)
    line, packed = lax.optimization_barrier((line, packed))
    held = exchange(packed.reshape((2 * BANDS, CLASS) + block), ("row", "col"), SPREAD)
    held = held.reshape(2, BANDS * CLASS * BS, BS)
    (line,) = call(choose_kernel, "choose", [((2,) + block, jnp.bfloat16)], win_cols, line)

    (sums,) = product(win_cols, line, held, [(2,) + block])
    sums = gather(sums, Y_NEAR).reshape((2, 2) + block)
    outs = [(block, jnp.float32), ((1,) + block, jnp.bfloat16)]
    square, half = call(square_kernel, "square", outs, win_cols, sums)

    keep, send = product(win_cols, gather(half, Y_FAR), held, [block] * 2)
    both = gather(send[None], Y_NEAR)
    (purified,) = call(final_kernel, "final", [(block, jnp.bfloat16)], win_cols, keep, both, square)
    return purified[None, None]


def solution(mesh):
    return jax.shard_map(
        on_device,
        mesh=mesh,
        in_specs=(P("row", "col", None, None), P("row", "col", None, None, None, None), P()),
        out_specs=P("row", "col", None, None),
        check_vma=False,
    )
```

time: 166 us -> 138 us (0.83)
  waiting for transfers between devices: 40.9 us -> 5.03 us
  starting transfers between devices: 14.7 us -> 36.4 us
  blocking collectives: 94.1 us -> 81 us
  Pallas kernels: 8.92 us -> 11.2 us
  local copies, waits for them, and re-layouts: 6.36 us -> 4.1 us
    all_to_all x1 -> x2, waiting for transfers between devices: 40.9 us -> 1.25 us  [exchange(): lax.all_to_all(value, axis, split_axis=0, concat_axis=0, tiled=True, axis...]
    ppermute x0 -> x2, starting transfers between devices: none -> 22.8 us  [product(): other = lax.ppermute(own, 'col', SWAP)]
    all_gather x8 -> x5, blocking collectives: 94.1 us -> 81 us  [gather(): lax.all_gather(value, 'col', axis=0, tiled=True, axis_index_groups=groups)]
    transpose x1 -> x0, local copies, waits for them, and re-layouts: 3.93 us -> none  [on_device(): couple_vals[0, 0].reshape(BANDS, CLASS, QUAD, BS, BS)]
    ppermute x0 -> x2, waiting for transfers between devices: none -> 3.78 us  [product(): other = lax.ppermute(own, 'col', SWAP)]
    pallas_call x0 -> x1, Pallas kernels: none -> 3.53 us  [pack(): pl.pallas_call(pack_kernel, out_shape=jax.ShapeDtypeStruct((2, BANDS, CLA...]
    pallas_call x6 -> x5, Pallas kernels: 8.92 us -> 7.7 us  [call(): pl.pallas_call(kernel, out_shape=[jax.ShapeDtypeStruct(shape, dtype) for...]
    all_to_all x1 -> x2, starting transfers between devices: 14.7 us -> 13.5 us  [exchange(): lax.all_to_all(value, axis, split_axis=0, concat_axis=0, tiled=True, axis...]
  transfers between devices with their start and end apart: 1 -> 4, of which waited for: 1 -> 3; matrix products, arithmetic and copies ran while one was open for 0% -> 0% of each run, Pallas kernels for 0% -> 4%
where the time goes in v6:
time: 138 us
  blocking collectives  81 us (59%)
  starting transfers between devices  36.4 us (26%)
  Pallas kernels  11.2 us (8%)
  waiting for transfers between devices  5.03 us (4%)
  local copies, waits for them, and re-layouts  4.1 us (3%)
    all_gather x5, blocking collectives, gather(): lax.all_gather(value, 'col', axis=0, tiled=True, axis_index_groups=groups)  81 us
    ppermute x2, starting transfers between devices, product(): other = lax.ppermute(own, 'col', SWAP)  22.8 us
    all_to_all x2, starting transfers between devices, exchange(): lax.all_to_all(value, axis, split_axis=0, concat_axis=0, tiled=True, axis...  13.5 us
    pallas_call x5, Pallas kernels, call(): pl.pallas_call(kernel, out_shape=[jax.ShapeDtypeStruct(shape, dtype) for...  7.7 us
    ppermute x2, waiting for transfers between devices, product(): other = lax.ppermute(own, 'col', SWAP)  3.78 us
    pallas_call x1, Pallas kernels, pack(): pl.pallas_call(pack_kernel, out_shape=jax.ShapeDtypeStruct((2, BANDS, CLA...  3.53 us
  transfers between devices with their start and end apart: 4, of which 3 were waited for; matrix products, arithmetic and copies ran while one was open for 0% of the time, Pallas kernels for 4%

profile of v6, /device:TPU:1, one launch (start us, length us, event | category | flops | bytes accessed | tf_op | source)
XLA Modules:
  0.0 137.8 jit_solution(7217589599272293847)
XLA Ops:
  0.0 1.4 %broadcast_in_dim.14 = bf16[4,128,128]{2,1,0:T(8,128)(2,1)} broadcast(bf16[128,128]{1,0:T(8,128)(2,1)} %bitcast.13), dimensions={1,2} | broadcast | bytes 163840 | tf_op jit(solution)/shard_map/broadcast_in_dim | solution.py:172
  1.4 5.4 %all-to-all-start = ((bf16[4,128,128]{2,1,0:T(8,128)(2,1)}), bf16[4,128,128]{2,1,0:T(8,128)(2,1)S(1)}, u32[]{:S(2)}, u32[]{:S(2)}) async-start(bf16[4,128,128]{2,1,0:T(8,128)(2,1)} %broadcast_in_dim.14), calls=%async_computation | async-start | bytes 262144 | tf_op jit(solution)/shard_map/all_to_all | solution.py:149
  6.8 3.5 %pack.1 = bf16[2,8,4,128,128]{4,3,2,1,0:T(8,128)(2,1)} custom-call(s32[8,96]{1,0:T(8,128)} %cols_ref.11, bf16[8,12,128,128]{3,2,1,0:T(8,128)(2,1)} %bitcast.10), custom_call_target="tpu_custom_call" | custom-call | bytes 5242880 | tf_op jit(solution)/shard_map/pack/pallas_call | solution.py:71
  10.4 1.2 all-to-all-done.line_ref
  11.6 0.6 copy-done.5
  12.3 8.1 %all-to-all-start.1 = ((bf16[16,4,128,128]{3,2,1,0:T(8,128)(2,1)}), bf16[16,4,128,128]{3,2,1,0:T(8,128)(2,1)S(1)}, u32[]{:S(2)}, u32[]{:S(2)}) async-start(bf16[16,4,128,128]{3,2,1,0:T(8,128)(2,1)} %bitcast.9), calls=%async_computation.1 | async-start | bytes 4194304 | tf_op jit(solution)/shard_map/all_to_all | solution.py:149
  20.4 1.6 %choose.1 = bf16[2,128,128]{2,1,0:T(8,128)(2,1)} custom-call(s32[8,96]{1,0:T(8,128)} %cols_ref.11, bf16[4,128,128]{2,1,0:T(8,128)(2,1)} %copy-done.5), custom_call_target="tpu_custom_call" | custom-call | tf_op jit(solution)/shard_map/choose/pallas_call | solution.py:134
  22.0 33.4 %all_gather.15.own_ref = bf16[24,128,128]{2,1,0:T(8,128)(2,1)S(1)} all-gather(bf16[2,128,128]{2,1,0:T(8,128)(2,1)} %choose.1), channel_id=1, replica_groups={{0,8,16,24,32,40,48,56,64,72,80,88},{1,9,17,25,33,41,49,57,65,73,81,89}..., dimensions={0}, use_global_device_ids=true | all-gather | bytes 851968 | tf_op jit(solution)/shard_map/all_gather | solution.py:145
  55.4 7.6 %collective-permute-start = (bf16[24,128,128]{2,1,0:T(8,128)(2,1)S(1)}, bf16[24,128,128]{2,1,0:T(8,128)(2,1)S(1)}, u32[]{:S(2)}, u32[]{:S(2)}) collective-permute-start(bf16[24,128,128]{2,1,0:T(8,128)(2,1)S(1)} %all_gather.15.own_ref), channel_id=1, source_target_pairs={{0,1},{1,0},{2,3},{3,2},{4,5},{5,4},{6,7},{7,6},{8,9},{9,8},{10,11... | collective-permute-start | bytes 2359304 | tf_op jit(solution)/shard_map/ppermute | solution.py:154
  63.0 1.9 %collective-permute-done.other_ref = bf16[24,128,128]{2,1,0:T(8,128)(2,1)S(1)} collective-permute-done((bf16[24,128,128]{2,1,0:T(8,128)(2,1)S(1)}, bf16[24,128,128]{2,1,0:T(8,128)(2,1)S(1)}, u32[]{:S(2)}, u32[]{:S(2)}) %collective-permute-start) | collective-permute-done | bytes 786464 | tf_op jit(solution)/shard_map/ppermute | solution.py:154
  64.9 0.9 copy-done
  65.8 0.0 all-to-all-done.1
  65.8 0.0 copy-done.2
  65.8 1.1 copy-done.1
  66.9 1.5 %partials.2 = f32[2,128,128]{2,1,0:T(8,128)S(1)} custom-call(s32[8,96]{1,0:T(8,128)S(1)} %copy-done.2, bf16[24,128,128]{2,1,0:T(8,128)(2,1)S(1)} %all_gather.15.own_ref, bf16[24,128,128]{2,1,0:T(8,128)(2,1)S(1)} %copy-done.1, bf16[2,4096,128]{2,1,0:T(8,128)(2,1)S(1)} %bitcast.7), custom_call_target="tpu_custom_call" | custom-call | flops 268435456 | bytes 4194304 | tf_op jit(solution)/shard_map/partials/pallas_call | solution.py:134
  68.4 7.2 %all_gather.16 = f32[4,128,128]{2,1,0:T(8,128)} all-gather(f32[2,128,128]{2,1,0:T(8,128)S(1)} %partials.2), channel_id=1, replica_groups={{0,2},{1,3},{4,6},{5,7},{8,10},{9,11},{12,14},{13,15},{16,18},{17,19},{..., dimensions={0}, use_global_device_ids=true | all-gather | bytes 393216 | tf_op jit(solution)/shard_map/all_gather | solution.py:145
  75.6 1.6 %square.1 = (f32[128,128]{1,0:T(8,128)}, bf16[1,128,128]{2,1,0:T(8,128)(2,1)}) custom-call(s32[8,96]{1,0:T(8,128)} %cols_ref.11, f32[2,2,128,128]{3,2,1,0:T(8,128)} %bitcast.11), custom_call_target="tpu_custom_call" | custom-call | tf_op jit(solution)/shard_map/square/pallas_call | solution.py:134
  77.3 4.6 %all_gather.17 = bf16[2,128,128]{2,1,0:T(8,128)(2,1)S(1)} all-gather(bf16[1,128,128]{2,1,0:T(8,128)(2,1)} %get-tuple-element.13), channel_id=1, replica_groups={{0,4},{1,5},{2,6},{3,7},{8,12},{9,13},{10,14},{11,15},{16,20},{17,21},{..., dimensions={0}, use_global_device_ids=true | all-gather | bytes 98304 | tf_op jit(solution)/shard_map/all_gather | solution.py:145
  81.8 31.9 %all_gather.18.own_ref = bf16[24,128,128]{2,1,0:T(8,128)(2,1)S(1)} all-gather(bf16[2,128,128]{2,1,0:T(8,128)(2,1)S(1)} %all_gather.17), channel_id=1, replica_groups={{0,8,16,24,32,40,48,56,64,72,80,88},{1,9,17,25,33,41,49,57,65,73,81,89}..., dimensions={0}, use_global_device_ids=true | all-gather | bytes 851968 | tf_op jit(solution)/shard_map/all_gather | solution.py:145
  113.7 15.2 %collective-permute-start.1 = (bf16[24,128,128]{2,1,0:T(8,128)(2,1)S(1)}, bf16[24,128,128]{2,1,0:T(8,128)(2,1)S(1)}, u32[]{:S(2)}, u32[]{:S(2)}) collective-permute-start(bf16[24,128,128]{2,1,0:T(8,128)(2,1)S(1)} %all_gather.18.own_ref), channel_id=1, source_target_pairs={{0,1},{1,0},{2,3},{3,2},{4,5},{5,4},{6,7},{7,6},{8,9},{9,8},{10,11... | collective-permute-start | bytes 2359304 | tf_op jit(solution)/shard_map/ppermute | solution.py:154
  128.9 1.9 %collective-permute-done.1.other_ref = bf16[24,128,128]{2,1,0:T(8,128)(2,1)S(1)} collective-permute-done((bf16[24,128,128]{2,1,0:T(8,128)(2,1)S(1)}, bf16[24,128,128]{2,1,0:T(8,128)(2,1)S(1)}, u32[]{:S(2)}, u32[]{:S(2)}) %collective-permute-start.1) | collective-permute-done | bytes 786464 | tf_op jit(solution)/shard_map/ppermute | solution.py:154
  130.8 1.4 %partials.3 = (f32[128,128]{1,0:T(8,128)S(1)}, f32[128,128]{1,0:T(8,128)S(1)}) custom-call(s32[8,96]{1,0:T(8,128)S(1)} %copy-done.3, bf16[24,128,128]{2,1,0:T(8,128)(2,1)S(1)} %all_gather.18.own_ref, bf16[24,128,128]{2,1,0:T(8,128)(2,1)S(1)} %collective-permute-done.1.other_ref, bf16[2,4096,128]{2,1,0:T(8,128)(2,1)S(1)} %bitcast.8), custom_call_target="tpu_custom_call" | custom-call | flops 268435456 | bytes 4194304 | tf_op jit(solution)/shard_map/partials/pallas_call | solution.py:134
  132.3 3.9 %all-gather = f32[256,128]{1,0:T(8,128)} all-gather(f32[128,128]{1,0:T(8,128)S(1)} %get-tuple-element.15), channel_id=2, replica_groups={{0,2},{1,3},{4,6},{5,7},{8,10},{9,11},{12,14},{13,15},{16,18},{17,19},{..., dimensions={0}, use_global_device_ids=true | all-gather | bytes 196608 | tf_op jit(solution)/shard_map/all_gather | solution.py:145
  136.2 1.6 %final.1 = bf16[128,128]{1,0:T(8,128)(2,1)} custom-call(s32[8,96]{1,0:T(8,128)} %cols_ref.11, f32[128,128]{1,0:T(8,128)} %copy-done.4, f32[2,128,128]{2,1,0:T(8,128)} %bitcast.12, f32[128,128]{1,0:T(8,128)} %get-tuple-element.16.square_ref), custom_call_target="tpu_custom_call" | custom-call | tf_op jit(solution)/shard_map/final/pallas_call | solution.py:134
  (8 shorter events, 0.0 us)
Async XLA Ops:
  1.4 10.2 %all-to-all-start = ((bf16[4,128,128]{2,1,0:T(8,128)(2,1)}), bf16[4,128,128]{2,1,0:T(8,128)(2,1)S(1)}, u32[]{:S(2)}, u32[]{:S(2)}) async-start(bf16[4,128,128]{2,1,0:T(8,128)(2,1)} %broadcast_in_dim.14), calls=%async_computation | async-start | bytes 262144 | tf_op jit(solution)/shard_map/all_to_all | solution.py:149
  11.6 0.6 copy-start.5
  11.6 54.2 %copy-start.2 = (s32[8,96]{1,0:T(8,128)S(1)}, s32[8,96]{1,0:T(8,128)}, u32[]{:S(2)}) copy-start(s32[8,96]{1,0:T(8,128)} %cols_ref.11) | copy-start | bytes 9220
  12.3 53.5 %all-to-all-start.1 = ((bf16[16,4,128,128]{3,2,1,0:T(8,128)(2,1)}), bf16[16,4,128,128]{3,2,1,0:T(8,128)(2,1)S(1)}, u32[]{:S(2)}, u32[]{:S(2)}) async-start(bf16[16,4,128,128]{3,2,1,0:T(8,128)(2,1)} %bitcast.9), calls=%async_computation.1 | async-start | bytes 4194304 | tf_op jit(solution)/shard_map/all_to_all | solution.py:149
  55.4 9.5 %collective-permute-start = (bf16[24,128,128]{2,1,0:T(8,128)(2,1)S(1)}, bf16[24,128,128]{2,1,0:T(8,128)(2,1)S(1)}, u32[]{:S(2)}, u32[]{:S(2)}) collective-permute-start(bf16[24,128,128]{2,1,0:T(8,128)(2,1)S(1)} %all_gather.15.own_ref), channel_id=1, source_target_pairs={{0,1},{1,0},{2,3},{3,2},{4,5},{5,4},{6,7},{7,6},{8,9},{9,8},{10,11... | collective-permute-start | bytes 2359304 | tf_op jit(solution)/shard_map/ppermute | solution.py:154
  64.9 0.9 copy-start
  65.8 1.1 copy-start.1
  66.9 63.9 %copy-start.3 = (s32[8,96]{1,0:T(8,128)S(1)}, s32[8,96]{1,0:T(8,128)}, u32[]{:S(2)}) copy-start(s32[8,96]{1,0:T(8,128)} %cols_ref.11) | copy-start | bytes 9220
  113.7 17.1 %collective-permute-start.1 = (bf16[24,128,128]{2,1,0:T(8,128)(2,1)S(1)}, bf16[24,128,128]{2,1,0:T(8,128)(2,1)S(1)}, u32[]{:S(2)}, u32[]{:S(2)}) collective-permute-start(bf16[24,128,128]{2,1,0:T(8,128)(2,1)S(1)} %all_gather.18.own_ref), channel_id=1, source_target_pairs={{0,1},{1,0},{2,3},{3,2},{4,5},{5,4},{6,7},{7,6},{8,9},{9,8},{10,11... | collective-permute-start | bytes 2359304 | tf_op jit(solution)/shard_map/ppermute | solution.py:154
  132.3 3.9 %copy-start.4 = (f32[128,128]{1,0:T(8,128)}, f32[128,128]{1,0:T(8,128)S(1)}, u32[]{:S(2)}) copy-start(f32[128,128]{1,0:T(8,128)S(1)} %get-tuple-element.14.keep_ref) | copy-start | bytes 196612

commit v7 on v6

--- a/solution.py
+++ b/solution.py
@@ -92,11 +92,9 @@
         out_ref[h] = line_ref[2 * h + member_of(alive, near)]
 
 
-def partial_kernel(cols_ref, own_ref, other_ref, m_ref, *out_refs):
-    *out_refs, list_ref = out_refs
-    keep_ref, send_ref = out_refs if len(out_refs) == 2 else (out_refs[0].at[0], out_refs[0].at[1])
+def picked(cols_ref, own_ref, other_ref, list_ref):
     row, _, core, near = place()
-    left = []
+    picks = []
     for band in range(BANDS):
         where = lambda quad, c, _, band=band: band * 3 + quad + jnp.where(core == c, 0, QUADS)
         count = list_live(cols_ref, list_ref, row, band, near, where)
@@ -104,22 +102,35 @@
             at = jnp.where(j < count, list_ref[j], 0)
             inside = lax.rem(at, QUADS)
             block = jnp.where(at < QUADS, own_ref[inside], other_ref[inside])
-            left.append(jnp.where(j < count, block, jnp.zeros_like(block)))
-    left = jnp.concatenate(left, axis=1)
-    right = jnp.concatenate([m_ref[near], m_ref[1 - near]], axis=1)
-    product = jnp.dot(left, right, preferred_element_type=jnp.float32)
+            picks.append(jnp.where(j < count, block, jnp.zeros_like(block)))
+    return jnp.concatenate(picks, axis=1)
+
+
+def multiply(cols_ref, left, m_ref, keep_ref, send_ref):
+    row, col, _, near = place()
+    alive = pair_alive(cols_ref, row, col - near * C)
+    chosen = [m_ref[member_of(alive, k)] for k in (near, 1 - near)]
+    product = jnp.dot(left, jnp.concatenate(chosen, axis=1), preferred_element_type=jnp.float32)
     keep_ref[...] = product[:, :BS]
     send_ref[...] = product[:, BS:]
 
 
-def square_kernel(cols_ref, sums_ref, square_ref, out_ref):
-    row, col, core, near = place()
-    alive = pair_alive(cols_ref, row, col - near * C)
-    mine = sums_ref[near, 0] + sums_ref[1 - near, 1]
-    theirs = sums_ref[near, 1] + sums_ref[1 - near, 0]
-    is_alive = cols_ref[row, col] >= 0
-    square_ref[...] = jnp.where(is_alive, mine, 0.0)
-    out_ref[0] = jnp.where(member_of(alive, near) == near, mine, theirs).astype(out_ref.dtype)
+def pick_kernel(cols_ref, own_ref, other_ref, left_ref, list_ref):
+    left_ref[...] = picked(cols_ref, own_ref, other_ref, list_ref)
+
+
+def multiply_kernel(cols_ref, left_ref, m_ref, keep_ref, send_ref):
+    multiply(cols_ref, left_ref[...], m_ref, keep_ref, send_ref)
+
+
+def partial_kernel(cols_ref, own_ref, other_ref, m_ref, keep_ref, send_ref, list_ref):
+    multiply(cols_ref, picked(cols_ref, own_ref, other_ref, list_ref), m_ref, keep_ref, send_ref)
+
+
+def square_kernel(keep_ref, both_ref, square_ref, half_ref):
+    total = keep_ref[...] + both_ref[1 - place()[3]]
+    square_ref[...] = total
+    half_ref[0] = total.astype(half_ref.dtype)
 
 
 def final_kernel(cols_ref, keep_ref, both_ref, square_ref, out_ref):
@@ -129,16 +140,17 @@
     out_ref[...] = jnp.where(alive, 3.0 * square_ref[...] - 2.0 * cube, 0.0).astype(out_ref.dtype)
 
 
-def call(kernel, name, outs, win_cols, *arrays, **options):
+def call(kernel, name, outs, arrays, scalars=(), grant=4, **options):
     vmem = pl.BlockSpec(memory_space=pltpu.VMEM)
     return pl.pallas_call(
         kernel,
         out_shape=[jax.ShapeDtypeStruct(shape, dtype) for shape, dtype in outs],
-        in_specs=[pl.BlockSpec(memory_space=pltpu.SMEM)] + [vmem] * len(arrays),
+        in_specs=[pl.BlockSpec(memory_space=pltpu.SMEM)] * len(scalars) + [vmem] * len(arrays),
         out_specs=[vmem] * len(outs),
+        compiler_params=pltpu.CompilerParams(vmem_limit_bytes=grant << 20),
         name=name,
         **options,
-    )(win_cols, *arrays)
+    )(*scalars, *arrays)
 
 
 def gather(value, groups):
@@ -149,40 +161,34 @@
     return lax.all_to_all(value, axis, split_axis=0, concat_axis=0, tiled=True, axis_index_groups=groups)
 
 
-def product(win_cols, line, held, shapes):
+def lines(line):
     own = gather(line, Z_LINES)
-    other = lax.ppermute(own, "col", SWAP)
-    return call(
-        partial_kernel,
-        "partials",
-        [(shape, jnp.float32) for shape in shapes],
-        win_cols,
-        own,
-        other,
-        held,
-        scratch_shapes=[pltpu.SMEM((CLASS + 1,), jnp.int32)],
-        cost_estimate=pl.CostEstimate(flops=2 * 64 * BS**3, bytes_accessed=4 << 20, transcendentals=0),
-        compiler_params=pltpu.CompilerParams(vmem_limit_bytes=24 << 20),
-    )
+    return own, lax.ppermute(own, "col", SWAP)
 
 
 def on_device(win_vals, couple_vals, win_cols):
-    block = (BS, BS)
+    block, cols = (BS, BS), (win_cols,)
+    lists = dict(scratch_shapes=[pltpu.SMEM((CLASS + 1,), jnp.int32)])
+    flops = lambda count: pl.CostEstimate(flops=count * BS**3, bytes_accessed=4 << 20, transcendentals=0)
+    shares = [(block, jnp.float32)] * 2
+
     packed = pack(win_cols, couple_vals[0, 0])
     line = exchange(jnp.broadcast_to(win_vals[0], (Y,) + block), "col", Y_LINES)
     line, packed = lax.optimization_barrier((line, packed))
     held = exchange(packed.reshape((2 * BANDS, CLASS) + block), ("row", "col"), SPREAD)
     held = held.reshape(2, BANDS * CLASS * BS, BS)
-    (line,) = call(choose_kernel, "choose", [((2,) + block, jnp.bfloat16)], win_cols, line)
-
-    (sums,) = product(win_cols, line, held, [(2,) + block])
-    sums = gather(sums, Y_NEAR).reshape((2, 2) + block)
+    (line,) = call(choose_kernel, "choose", [((2,) + block, jnp.bfloat16)], (line,), cols)
+    left = [((BS, BANDS * CLASS * BS), jnp.bfloat16)]
+    (left,) = call(pick_kernel, "pick", left, lines(line), cols, 8, **lists)
+    keep, send = call(multiply_kernel, "multiply", shares, (left, held), cols, 16, cost_estimate=flops(128))
+
     outs = [(block, jnp.float32), ((1,) + block, jnp.bfloat16)]
-    square, half = call(square_kernel, "square", outs, win_cols, sums)
-
-    keep, send = product(win_cols, gather(half, Y_FAR), held, [block] * 2)
-    both = gather(send[None], Y_NEAR)
-    (purified,) = call(final_kernel, "final", [(block, jnp.bfloat16)], win_cols, keep, both, square)
+    square, half = call(square_kernel, "square", outs, (keep, gather(send[None], Y_NEAR)))
+
+    line = lines(gather(half, Y_FAR))
+    keep, send = call(partial_kernel, "partials", shares, (*line, held), cols, 16, cost_estimate=flops(128), **lists)
+    outs = [(block, jnp.bfloat16)]
+    (purified,) = call(final_kernel, "final", outs, (keep, gather(send[None], Y_NEAR), square), cols)
     return purified[None, None]
 
 

time: 138 us -> 133 us (0.964)
  local copies, waits for them, and re-layouts: 4.1 us -> 1.43 us
  Pallas kernels: 11.2 us -> 9.67 us
    unnamed x12 -> x2, local copies, waits for them, and re-layouts: 2.68 us -> 0.01 us
    pallas_call x5 -> x6, Pallas kernels: 7.7 us -> 6.14 us  [call(): pl.pallas_call(kernel, out_shape=[jax.ShapeDtypeStruct(shape, dtype) for...]
where the time goes in v7:
time: 133 us
  blocking collectives  80.2 us (60%)
  starting transfers between devices  36.4 us (27%)
  Pallas kernels  9.67 us (7%)
  waiting for transfers between devices  5.02 us (4%)
  local copies, waits for them, and re-layouts  1.43 us (1%)
    all_gather x5, blocking collectives, gather(): lax.all_gather(value, 'col', axis=0, tiled=True, axis_index_groups=groups)  80.2 us
    ppermute x2, starting transfers between devices, lines(): return (own, lax.ppermute(own, 'col', SWAP))  22.7 us
    all_to_all x2, starting transfers between devices, exchange(): lax.all_to_all(value, axis, split_axis=0, concat_axis=0, tiled=True, axis...  13.7 us
    pallas_call x6, Pallas kernels, call(): pl.pallas_call(kernel, out_shape=[jax.ShapeDtypeStruct(shape, dtype) for...  6.14 us
    ppermute x2, waiting for transfers between devices, lines(): return (own, lax.ppermute(own, 'col', SWAP))  3.78 us
    pallas_call x1, Pallas kernels, pack(): pl.pallas_call(pack_kernel, out_shape=jax.ShapeDtypeStruct((2, BANDS, CLA...  3.53 us
  transfers between devices with their start and end apart: 4, of which 3 were waited for; matrix products, arithmetic and copies ran while one was open for 0% of the time, Pallas kernels for 4%

profile of v7, /device:TPU:1, one launch (start us, length us, event | category | flops | bytes accessed | tf_op | source)
XLA Modules:
  0.0 132.8 jit_solution(925476710551856977)
XLA Ops:
  0.0 1.4 %broadcast_in_dim.17 = bf16[4,128,128]{2,1,0:T(8,128)(2,1)} broadcast(bf16[128,128]{1,0:T(8,128)(2,1)} %bitcast.13), dimensions={1,2} | broadcast | bytes 163840 | tf_op jit(solution)/shard_map/broadcast_in_dim | solution.py:176
  1.4 5.4 %all-to-all-start = ((bf16[4,128,128]{2,1,0:T(8,128)(2,1)}), bf16[4,128,128]{2,1,0:T(8,128)(2,1)S(1)}, u32[]{:S(2)}, u32[]{:S(2)}) async-start(bf16[4,128,128]{2,1,0:T(8,128)(2,1)} %broadcast_in_dim.17), calls=%async_computation | async-start | bytes 262144 | tf_op jit(solution)/shard_map/all_to_all | solution.py:161
  6.8 3.5 %pack.1 = bf16[2,8,4,128,128]{4,3,2,1,0:T(8,128)(2,1)} custom-call(s32[8,96]{1,0:T(8,128)} %cols_ref.11, bf16[8,12,128,128]{3,2,1,0:T(8,128)(2,1)} %bitcast.12), custom_call_target="tpu_custom_call" | custom-call | bytes 5242880 | tf_op jit(solution)/shard_map/pack/pallas_call | solution.py:71
  10.4 1.2 all-to-all-done.line_ref
  11.6 0.0 copy-start
  11.6 8.3 %all-to-all-start.1 = ((bf16[16,4,128,128]{3,2,1,0:T(8,128)(2,1)}), bf16[16,4,128,128]{3,2,1,0:T(8,128)(2,1)S(1)}, u32[]{:S(2)}, u32[]{:S(2)}) async-start(bf16[16,4,128,128]{3,2,1,0:T(8,128)(2,1)} %bitcast.11), calls=%async_computation.1 | async-start | bytes 4194304 | tf_op jit(solution)/shard_map/all_to_all | solution.py:161
  19.9 0.0 copy-done
  19.9 0.6 choose.1
  20.5 33.4 %all_gather.15.own_ref = bf16[24,128,128]{2,1,0:T(8,128)(2,1)S(1)} all-gather(bf16[2,128,128]{2,1,0:T(8,128)(2,1)S(1)} %choose.1), channel_id=1, replica_groups={{0,8,16,24,32,40,48,56,64,72,80,88},{1,9,17,25,33,41,49,57,65,73,81,89}..., dimensions={0}, use_global_device_ids=true | all-gather | bytes 851968 | tf_op jit(solution)/shard_map/all_gather | solution.py:157
  53.9 7.5 %collective-permute-start = (bf16[24,128,128]{2,1,0:T(8,128)(2,1)S(1)}, bf16[24,128,128]{2,1,0:T(8,128)(2,1)S(1)}, u32[]{:S(2)}, u32[]{:S(2)}) collective-permute-start(bf16[24,128,128]{2,1,0:T(8,128)(2,1)S(1)} %all_gather.15.own_ref), channel_id=1, source_target_pairs={{0,1},{1,0},{2,3},{3,2},{4,5},{5,4},{6,7},{7,6},{8,9},{9,8},{10,11... | collective-permute-start | bytes 2359304 | tf_op jit(solution)/shard_map/ppermute | solution.py:166
  61.4 1.9 %collective-permute-done.other_ref = bf16[24,128,128]{2,1,0:T(8,128)(2,1)S(1)} collective-permute-done((bf16[24,128,128]{2,1,0:T(8,128)(2,1)S(1)}, bf16[24,128,128]{2,1,0:T(8,128)(2,1)S(1)}, u32[]{:S(2)}, u32[]{:S(2)}) %collective-permute-start) | collective-permute-done | bytes 786464 | tf_op jit(solution)/shard_map/ppermute | solution.py:166
  63.3 1.6 %pick.1.left_ref = bf16[128,4096]{1,0:T(8,128)(2,1)S(1)} custom-call(s32[8,96]{1,0:T(8,128)S(1)} %copy-done, bf16[24,128,128]{2,1,0:T(8,128)(2,1)S(1)} %all_gather.15.own_ref, bf16[24,128,128]{2,1,0:T(8,128)(2,1)S(1)} %collective-permute-done.other_ref), custom_call_target="tpu_custom_call" | custom-call | tf_op jit(solution)/shard_map/pick/pallas_call | solution.py:145
  64.9 0.0 all-to-all-done.1
  64.9 1.1 multiply.1
  66.0 6.8 %all-gather = f32[256,128]{1,0:T(8,128)S(1)} all-gather(f32[128,128]{1,0:T(8,128)S(1)} %get-tuple-element.16), channel_id=2, replica_groups={{0,2},{1,3},{4,6},{5,7},{8,10},{9,11},{12,14},{13,15},{16,18},{17,19},{..., dimensions={0}, use_global_device_ids=true | all-gather | bytes 196608 | tf_op jit(solution)/shard_map/all_gather | solution.py:157
  72.8 4.3 %all_gather.17 = bf16[2,128,128]{2,1,0:T(8,128)(2,1)S(1)} all-gather(bf16[1,128,128]{2,1,0:T(8,128)(2,1)S(1)} %get-tuple-element.17), channel_id=1, replica_groups={{0,4},{1,5},{2,6},{3,7},{8,12},{9,13},{10,14},{11,15},{16,20},{17,21},{..., dimensions={0}, use_global_device_ids=true | all-gather | bytes 98304 | tf_op jit(solution)/shard_map/all_gather | solution.py:157
  77.1 31.9 %all_gather.18.own_ref = bf16[24,128,128]{2,1,0:T(8,128)(2,1)S(1)} all-gather(bf16[2,128,128]{2,1,0:T(8,128)(2,1)S(1)} %all_gather.17), channel_id=1, replica_groups={{0,8,16,24,32,40,48,56,64,72,80,88},{1,9,17,25,33,41,49,57,65,73,81,89}..., dimensions={0}, use_global_device_ids=true | all-gather | bytes 851968 | tf_op jit(solution)/shard_map/all_gather | solution.py:157
  109.1 15.3 %collective-permute-start.1 = (bf16[24,128,128]{2,1,0:T(8,128)(2,1)S(1)}, bf16[24,128,128]{2,1,0:T(8,128)(2,1)S(1)}, u32[]{:S(2)}, u32[]{:S(2)}) collective-permute-start(bf16[24,128,128]{2,1,0:T(8,128)(2,1)S(1)} %all_gather.18.own_ref), channel_id=1, source_target_pairs={{0,1},{1,0},{2,3},{3,2},{4,5},{5,4},{6,7},{7,6},{8,9},{9,8},{10,11... | collective-permute-start | bytes 2359304 | tf_op jit(solution)/shard_map/ppermute | solution.py:166
  124.4 1.9 %collective-permute-done.1.other_ref = bf16[24,128,128]{2,1,0:T(8,128)(2,1)S(1)} collective-permute-done((bf16[24,128,128]{2,1,0:T(8,128)(2,1)S(1)}, bf16[24,128,128]{2,1,0:T(8,128)(2,1)S(1)}, u32[]{:S(2)}, u32[]{:S(2)}) %collective-permute-start.1) | collective-permute-done | bytes 786464 | tf_op jit(solution)/shard_map/ppermute | solution.py:166
  126.3 1.5 %partials.1 = (f32[128,128]{1,0:T(8,128)S(1)}, f32[128,128]{1,0:T(8,128)S(1)}) custom-call(s32[8,96]{1,0:T(8,128)S(1)} %copy-done, bf16[24,128,128]{2,1,0:T(8,128)(2,1)S(1)} %all_gather.18.own_ref, bf16[24,128,128]{2,1,0:T(8,128)(2,1)S(1)} %collective-permute-done.1.other_ref, bf16[2,4096,128]{2,1,0:T(8,128)(2,1)S(1)} %bitcast.8), custom_call_target="tpu_custom_call" | custom-call | flops 268435456 | bytes 4194304 | tf_op jit(solution)/shard_map/partials/pallas_call | solution.py:145
  127.8 3.8 %all-gather.1 = f32[256,128]{1,0:T(8,128)S(1)} all-gather(f32[128,128]{1,0:T(8,128)S(1)} %get-tuple-element.19), channel_id=3, replica_groups={{0,2},{1,3},{4,6},{5,7},{8,10},{9,11},{12,14},{13,15},{16,18},{17,19},{..., dimensions={0}, use_global_device_ids=true | all-gather | bytes 196608 | tf_op jit(solution)/shard_map/all_gather | solution.py:157
  131.6 1.2 final.1
  (1 shorter events, 0.0 us)
Async XLA Ops:
  1.4 10.2 %all-to-all-start = ((bf16[4,128,128]{2,1,0:T(8,128)(2,1)}), bf16[4,128,128]{2,1,0:T(8,128)(2,1)S(1)}, u32[]{:S(2)}, u32[]{:S(2)}) async-start(bf16[4,128,128]{2,1,0:T(8,128)(2,1)} %broadcast_in_dim.17), calls=%async_computation | async-start | bytes 262144 | tf_op jit(solution)/shard_map/all_to_all | solution.py:161
  11.6 8.3 %copy-start = (s32[8,96]{1,0:T(8,128)S(1)}, s32[8,96]{1,0:T(8,128)}, u32[]{:S(2)}) copy-start(s32[8,96]{1,0:T(8,128)} %cols_ref.11) | copy-start | bytes 9220
  11.6 53.3 %all-to-all-start.1 = ((bf16[16,4,128,128]{3,2,1,0:T(8,128)(2,1)}), bf16[16,4,128,128]{3,2,1,0:T(8,128)(2,1)S(1)}, u32[]{:S(2)}, u32[]{:S(2)}) async-start(bf16[16,4,128,128]{3,2,1,0:T(8,128)(2,1)} %bitcast.11), calls=%async_computation.1 | async-start | bytes 4194304 | tf_op jit(solution)/shard_map/all_to_all | solution.py:161
  53.9 9.4 %collective-permute-start = (bf16[24,128,128]{2,1,0:T(8,128)(2,1)S(1)}, bf16[24,128,128]{2,1,0:T(8,128)(2,1)S(1)}, u32[]{:S(2)}, u32[]{:S(2)}) collective-permute-start(bf16[24,128,128]{2,1,0:T(8,128)(2,1)S(1)} %all_gather.15.own_ref), channel_id=1, source_target_pairs={{0,1},{1,0},{2,3},{3,2},{4,5},{5,4},{6,7},{7,6},{8,9},{9,8},{10,11... | collective-permute-start | bytes 2359304 | tf_op jit(solution)/shard_map/ppermute | solution.py:166
  109.1 17.2 %collective-permute-start.1 = (bf16[24,128,128]{2,1,0:T(8,128)(2,1)S(1)}, bf16[24,128,128]{2,1,0:T(8,128)(2,1)S(1)}, u32[]{:S(2)}, u32[]{:S(2)}) collective-permute-start(bf16[24,128,128]{2,1,0:T(8,128)(2,1)S(1)} %all_gather.18.own_ref), channel_id=1, source_target_pairs={{0,1},{1,0},{2,3},{3,2},{4,5},{5,4},{6,7},{7,6},{8,9},{9,8},{10,11... | collective-permute-start | bytes 2359304 | tf_op jit(solution)/shard_map/ppermute | solution.py:166

commit v8 on v7

--- a/solution.py
+++ b/solution.py
@@ -22,7 +22,6 @@
 
 
 Y_LINES = [[col_of(z, y, c) for y in range(Y)] for z in range(Z) for c in range(C)]
-Y_FAR = [[col_of(z, 2 * h + p, c) for h in range(2)] for z in range(Z) for p in range(2) for c in range(C)]
 Y_NEAR = [[col_of(z, 2 * h + p, c) for p in range(2)] for z in range(Z) for h in range(2) for c in range(C)]
 Z_LINES = [[col_of(z, y, c) for z in range(Z)] for y in range(Y) for c in range(C)]
 SWAP = [(s, s ^ 1) for s in range(N_COL)]
@@ -84,6 +83,11 @@
     )(win_cols, couple)
 
 
+def copies_kernel(x_ref, out_ref):
+    for y in range(Y):
+        out_ref[y] = x_ref[0]
+
+
 def choose_kernel(cols_ref, line_ref, out_ref):
     row, col, core, near = place()
     first = col // (Y * C) * (Y * C) + core
@@ -106,31 +110,36 @@
     return jnp.concatenate(picks, axis=1)
 
 
-def multiply(cols_ref, left, m_ref, keep_ref, send_ref):
+def multiply(cols_ref, left, m_ref):
     row, col, _, near = place()
     alive = pair_alive(cols_ref, row, col - near * C)
-    chosen = [m_ref[member_of(alive, k)] for k in (near, 1 - near)]
+    chosen = [m_ref[member_of(alive, k)] for k in range(2)]
     product = jnp.dot(left, jnp.concatenate(chosen, axis=1), preferred_element_type=jnp.float32)
-    keep_ref[...] = product[:, :BS]
-    send_ref[...] = product[:, BS:]
+    return product[:, :BS], product[:, BS:]
 
 
 def pick_kernel(cols_ref, own_ref, other_ref, left_ref, list_ref):
     left_ref[...] = picked(cols_ref, own_ref, other_ref, list_ref)
 
 
-def multiply_kernel(cols_ref, left_ref, m_ref, keep_ref, send_ref):
-    multiply(cols_ref, left_ref[...], m_ref, keep_ref, send_ref)
+def multiply_kernel(cols_ref, left_ref, m_ref, out_ref):
+    shares = multiply(cols_ref, left_ref[...], m_ref)
+    for y in range(Y):
+        out_ref[y] = shares[y % 2]
 
 
 def partial_kernel(cols_ref, own_ref, other_ref, m_ref, keep_ref, send_ref, list_ref):
-    multiply(cols_ref, picked(cols_ref, own_ref, other_ref, list_ref), m_ref, keep_ref, send_ref)
-
-
-def square_kernel(keep_ref, both_ref, square_ref, half_ref):
-    total = keep_ref[...] + both_ref[1 - place()[3]]
-    square_ref[...] = total
-    half_ref[0] = total.astype(half_ref.dtype)
+    shares = multiply(cols_ref, picked(cols_ref, own_ref, other_ref, list_ref), m_ref)
+    near = place()[3]
+    keep_ref[...] = jnp.where(near == 0, *shares)
+    send_ref[...] = jnp.where(near == 0, *shares[::-1])
+
+
+def square_kernel(shares_ref, square_ref, half_ref):
+    h = lax.rem(lax.axis_index("col") // (2 * C), 2)
+    square_ref[...] = shares_ref[2 * h] + shares_ref[2 * h + 1]
+    for pair in range(2):
+        half_ref[pair] = (shares_ref[2 * pair] + shares_ref[2 * pair + 1]).astype(half_ref.dtype)
 
 
 def final_kernel(cols_ref, keep_ref, both_ref, square_ref, out_ref):
@@ -173,19 +182,21 @@
     shares = [(block, jnp.float32)] * 2
 
     packed = pack(win_cols, couple_vals[0, 0])
-    line = exchange(jnp.broadcast_to(win_vals[0], (Y,) + block), "col", Y_LINES)
+    (line,) = call(copies_kernel, "copies", [((Y,) + block, jnp.bfloat16)], (win_vals[0],))
+    line = exchange(line, "col", Y_LINES)
     line, packed = lax.optimization_barrier((line, packed))
     held = exchange(packed.reshape((2 * BANDS, CLASS) + block), ("row", "col"), SPREAD)
     held = held.reshape(2, BANDS * CLASS * BS, BS)
     (line,) = call(choose_kernel, "choose", [((2,) + block, jnp.bfloat16)], (line,), cols)
     left = [((BS, BANDS * CLASS * BS), jnp.bfloat16)]
     (left,) = call(pick_kernel, "pick", left, lines(line), cols, 8, **lists)
-    keep, send = call(multiply_kernel, "multiply", shares, (left, held), cols, 16, cost_estimate=flops(128))
-
-    outs = [(block, jnp.float32), ((1,) + block, jnp.bfloat16)]
-    square, half = call(square_kernel, "square", outs, (keep, gather(send[None], Y_NEAR)))
-
-    line = lines(gather(half, Y_FAR))
+    outs = [((Y,) + block, jnp.float32)]
+    (sums,) = call(multiply_kernel, "multiply", outs, (left, held), cols, 16, cost_estimate=flops(128))
+
+    outs = [(block, jnp.float32), ((2,) + block, jnp.bfloat16)]
+    square, half = call(square_kernel, "square", outs, (exchange(sums, "col", Y_LINES),))
+
+    line = lines(half)
     keep, send = call(partial_kernel, "partials", shares, (*line, held), cols, 16, cost_estimate=flops(128), **lists)
     outs = [(block, jnp.bfloat16)]
     (purified,) = call(final_kernel, "final", outs, (keep, gather(send[None], Y_NEAR), square), cols)

time: 133 us -> 132 us (level)
  starting transfers between devices: 36.4 us -> 33.4 us
  blocking collectives: 80.2 us -> 82.2 us
    all_to_all x0 -> x1, blocking collectives: none -> 12.4 us  [exchange(): lax.all_to_all(value, axis, split_axis=0, concat_axis=0, tiled=True, axis...]
    all_gather x5 -> x3, blocking collectives: 80.2 us -> 69.8 us  [gather(): lax.all_gather(value, 'col', axis=0, tiled=True, axis_index_groups=groups)]
    ppermute x2, starting transfers between devices: 22.7 us -> 19.7 us  [lines(): return (own, lax.ppermute(own, 'col', SWAP))]
    broadcast_in_dim x1 -> x0, local copies, waits for them, and re-layouts: 1.43 us -> none  [on_device(): line = exchange(jnp.broadcast_to(win_vals[0], (Y,) + block), 'col', Y_LINES)]
    pallas_call x6 -> x7, Pallas kernels: 6.14 us -> 6.83 us  [call(): pl.pallas_call(kernel, out_shape=[jax.ShapeDtypeStruct(shape, dtype) for...]
where the time goes in v8:
time: 132 us
  blocking collectives  82.2 us (62%)
  starting transfers between devices  33.4 us (25%)
  Pallas kernels  10.4 us (8%)
  waiting for transfers between devices  5.02 us (4%)
    all_gather x3, blocking collectives, gather(): lax.all_gather(value, 'col', axis=0, tiled=True, axis_index_groups=groups)  69.8 us
    ppermute x2, starting transfers between devices, lines(): return (own, lax.ppermute(own, 'col', SWAP))  19.7 us
    all_to_all x2, starting transfers between devices, exchange(): lax.all_to_all(value, axis, split_axis=0, concat_axis=0, tiled=True, axis...  13.7 us
    all_to_all x1, blocking collectives, exchange(): lax.all_to_all(value, axis, split_axis=0, concat_axis=0, tiled=True, axis...  12.4 us
    pallas_call x7, Pallas kernels, call(): pl.pallas_call(kernel, out_shape=[jax.ShapeDtypeStruct(shape, dtype) for...  6.83 us
    ppermute x2, waiting for transfers between devices, lines(): return (own, lax.ppermute(own, 'col', SWAP))  3.78 us
    pallas_call x1, Pallas kernels, pack(): pl.pallas_call(pack_kernel, out_shape=jax.ShapeDtypeStruct((2, BANDS, CLA...  3.53 us
  transfers between devices with their start and end apart: 4, of which 3 were waited for; matrix products, arithmetic and copies ran while one was open for 0% of the time, Pallas kernels for 4%

profile of v8, /device:TPU:1, one launch (start us, length us, event | category | flops | bytes accessed | tf_op | source)
XLA Modules:
  0.0 131.8 jit_solution(10514158424358516521)
XLA Ops:
  0.0 0.0 copy-start.1
  0.0 0.8 copy-done.1
  0.8 0.7 copies.1
  1.4 5.4 %all-to-all-start = ((bf16[4,128,128]{2,1,0:T(8,128)(2,1)}), bf16[4,128,128]{2,1,0:T(8,128)(2,1)S(1)}, u32[]{:S(2)}, u32[]{:S(2)}) async-start(bf16[4,128,128]{2,1,0:T(8,128)(2,1)} %copies.1), calls=%async_computation | async-start | bytes 262144 | tf_op jit(solution)/shard_map/all_to_all | solution.py:170
  6.9 3.5 %pack.1 = bf16[2,8,4,128,128]{4,3,2,1,0:T(8,128)(2,1)} custom-call(s32[8,96]{1,0:T(8,128)} %cols_ref.11, bf16[8,12,128,128]{3,2,1,0:T(8,128)(2,1)} %bitcast.11), custom_call_target="tpu_custom_call" | custom-call | bytes 5242880 | tf_op jit(solution)/shard_map/pack/pallas_call | solution.py:70
  10.4 1.2 all-to-all-done.line_ref
  11.6 0.0 copy-start
  11.6 8.3 %all-to-all-start.1 = ((bf16[16,4,128,128]{3,2,1,0:T(8,128)(2,1)}), bf16[16,4,128,128]{3,2,1,0:T(8,128)(2,1)S(1)}, u32[]{:S(2)}, u32[]{:S(2)}) async-start(bf16[16,4,128,128]{3,2,1,0:T(8,128)(2,1)} %bitcast.10), calls=%async_computation.1 | async-start | bytes 4194304 | tf_op jit(solution)/shard_map/all_to_all | solution.py:170
  19.9 0.0 copy-done
  19.9 0.6 choose.1
  20.5 33.4 %all_gather.9.own_ref = bf16[24,128,128]{2,1,0:T(8,128)(2,1)S(1)} all-gather(bf16[2,128,128]{2,1,0:T(8,128)(2,1)S(1)} %choose.1), channel_id=1, replica_groups={{0,8,16,24,32,40,48,56,64,72,80,88},{1,9,17,25,33,41,49,57,65,73,81,89}..., dimensions={0}, use_global_device_ids=true | all-gather | bytes 851968 | tf_op jit(solution)/shard_map/all_gather | solution.py:166
  53.9 7.5 %collective-permute-start = (bf16[24,128,128]{2,1,0:T(8,128)(2,1)S(1)}, bf16[24,128,128]{2,1,0:T(8,128)(2,1)S(1)}, u32[]{:S(2)}, u32[]{:S(2)}) collective-permute-start(bf16[24,128,128]{2,1,0:T(8,128)(2,1)S(1)} %all_gather.9.own_ref), channel_id=1, source_target_pairs={{0,1},{1,0},{2,3},{3,2},{4,5},{5,4},{6,7},{7,6},{8,9},{9,8},{10,11... | collective-permute-start | bytes 2359304 | tf_op jit(solution)/shard_map/ppermute | solution.py:175
  61.4 1.9 %collective-permute-done.other_ref = bf16[24,128,128]{2,1,0:T(8,128)(2,1)S(1)} collective-permute-done((bf16[24,128,128]{2,1,0:T(8,128)(2,1)S(1)}, bf16[24,128,128]{2,1,0:T(8,128)(2,1)S(1)}, u32[]{:S(2)}, u32[]{:S(2)}) %collective-permute-start) | collective-permute-done | bytes 786464 | tf_op jit(solution)/shard_map/ppermute | solution.py:175
  63.3 1.6 %pick.1.left_ref = bf16[128,4096]{1,0:T(8,128)(2,1)S(1)} custom-call(s32[8,96]{1,0:T(8,128)S(1)} %copy-done, bf16[24,128,128]{2,1,0:T(8,128)(2,1)S(1)} %all_gather.9.own_ref, bf16[24,128,128]{2,1,0:T(8,128)(2,1)S(1)} %collective-permute-done.other_ref), custom_call_target="tpu_custom_call" | custom-call | tf_op jit(solution)/shard_map/pick/pallas_call | solution.py:154
  64.9 0.0 all-to-all-done.1
  64.9 1.1 multiply.1
  66.0 12.4 %all_to_all.15.shares_ref = f32[4,128,128]{2,1,0:T(8,128)S(1)} all-to-all(f32[4,128,128]{2,1,0:T(8,128)S(1)} %multiply.1), channel_id=1, replica_groups={{0,2,4,6},{1,3,5,7},{8,10,12,14},{9,11,13,15},{16,18,20,22},{17,19,21,2..., dimensions={0} | all-to-all | bytes 524288 | tf_op jit(solution)/shard_map/all_to_all | solution.py:170
  78.4 32.6 %all_gather.10.own_ref = bf16[24,128,128]{2,1,0:T(8,128)(2,1)S(1)} all-gather(bf16[2,128,128]{2,1,0:T(8,128)(2,1)S(1)} %get-tuple-element.13), channel_id=1, replica_groups={{0,8,16,24,32,40,48,56,64,72,80,88},{1,9,17,25,33,41,49,57,65,73,81,89}..., dimensions={0}, use_global_device_ids=true | all-gather | bytes 851968 | tf_op jit(solution)/shard_map/all_gather | solution.py:166
  111.1 12.3 %collective-permute-start.1 = (bf16[24,128,128]{2,1,0:T(8,128)(2,1)S(1)}, bf16[24,128,128]{2,1,0:T(8,128)(2,1)S(1)}, u32[]{:S(2)}, u32[]{:S(2)}) collective-permute-start(bf16[24,128,128]{2,1,0:T(8,128)(2,1)S(1)} %all_gather.10.own_ref), channel_id=1, source_target_pairs={{0,1},{1,0},{2,3},{3,2},{4,5},{5,4},{6,7},{7,6},{8,9},{9,8},{10,11... | collective-permute-start | bytes 2359304 | tf_op jit(solution)/shard_map/ppermute | solution.py:175
  123.3 1.9 %collective-permute-done.1.other_ref = bf16[24,128,128]{2,1,0:T(8,128)(2,1)S(1)} collective-permute-done((bf16[24,128,128]{2,1,0:T(8,128)(2,1)S(1)}, bf16[24,128,128]{2,1,0:T(8,128)(2,1)S(1)}, u32[]{:S(2)}, u32[]{:S(2)}) %collective-permute-start.1) | collective-permute-done | bytes 786464 | tf_op jit(solution)/shard_map/ppermute | solution.py:175
  125.2 1.5 %partials.1 = (f32[128,128]{1,0:T(8,128)S(1)}, f32[128,128]{1,0:T(8,128)S(1)}) custom-call(s32[8,96]{1,0:T(8,128)S(1)} %copy-done, bf16[24,128,128]{2,1,0:T(8,128)(2,1)S(1)} %all_gather.10.own_ref, bf16[24,128,128]{2,1,0:T(8,128)(2,1)S(1)} %collective-permute-done.1.other_ref, bf16[2,4096,128]{2,1,0:T(8,128)(2,1)S(1)} %bitcast.7), custom_call_target="tpu_custom_call" | custom-call | flops 268435456 | bytes 4194304 | tf_op jit(solution)/shard_map/partials/pallas_call | solution.py:154
  126.8 3.8 %all-gather = f32[256,128]{1,0:T(8,128)S(1)} all-gather(f32[128,128]{1,0:T(8,128)S(1)} %get-tuple-element.15), channel_id=2, replica_groups={{0,2},{1,3},{4,6},{5,7},{8,10},{9,11},{12,14},{13,15},{16,18},{17,19},{..., dimensions={0}, use_global_device_ids=true | all-gather | bytes 196608 | tf_op jit(solution)/shard_map/all_gather | solution.py:166
  130.5 1.2 final.1
  (1 shorter events, 0.0 us)
Async XLA Ops:
  0.0 0.8 copy-start.1
  1.4 10.2 %all-to-all-start = ((bf16[4,128,128]{2,1,0:T(8,128)(2,1)}), bf16[4,128,128]{2,1,0:T(8,128)(2,1)S(1)}, u32[]{:S(2)}, u32[]{:S(2)}) async-start(bf16[4,128,128]{2,1,0:T(8,128)(2,1)} %copies.1), calls=%async_computation | async-start | bytes 262144 | tf_op jit(solution)/shard_map/all_to_all | solution.py:170
  11.6 8.3 %copy-start = (s32[8,96]{1,0:T(8,128)S(1)}, s32[8,96]{1,0:T(8,128)}, u32[]{:S(2)}) copy-start(s32[8,96]{1,0:T(8,128)} %cols_ref.11) | copy-start | bytes 9220
  11.6 53.3 %all-to-all-start.1 = ((bf16[16,4,128,128]{3,2,1,0:T(8,128)(2,1)}), bf16[16,4,128,128]{3,2,1,0:T(8,128)(2,1)S(1)}, u32[]{:S(2)}, u32[]{:S(2)}) async-start(bf16[16,4,128,128]{3,2,1,0:T(8,128)(2,1)} %bitcast.10), calls=%async_computation.1 | async-start | bytes 4194304 | tf_op jit(solution)/shard_map/all_to_all | solution.py:170
  53.9 9.4 %collective-permute-start = (bf16[24,128,128]{2,1,0:T(8,128)(2,1)S(1)}, bf16[24,128,128]{2,1,0:T(8,128)(2,1)S(1)}, u32[]{:S(2)}, u32[]{:S(2)}) collective-permute-start(bf16[24,128,128]{2,1,0:T(8,128)(2,1)S(1)} %all_gather.9.own_ref), channel_id=1, source_target_pairs={{0,1},{1,0},{2,3},{3,2},{4,5},{5,4},{6,7},{7,6},{8,9},{9,8},{10,11... | collective-permute-start | bytes 2359304 | tf_op jit(solution)/shard_map/ppermute | solution.py:175
  111.1 14.2 %collective-permute-start.1 = (bf16[24,128,128]{2,1,0:T(8,128)(2,1)S(1)}, bf16[24,128,128]{2,1,0:T(8,128)(2,1)S(1)}, u32[]{:S(2)}, u32[]{:S(2)}) collective-permute-start(bf16[24,128,128]{2,1,0:T(8,128)(2,1)S(1)} %all_gather.10.own_ref), channel_id=1, source_target_pairs={{0,1},{1,0},{2,3},{3,2},{4,5},{5,4},{6,7},{7,6},{8,9},{9,8},{10,11... | collective-permute-start | bytes 2359304 | tf_op jit(solution)/shard_map/ppermute | solution.py:175

commit v9 on v8

--- a/solution.py
+++ b/solution.py
@@ -23,7 +23,7 @@
 
 Y_LINES = [[col_of(z, y, c) for y in range(Y)] for z in range(Z) for c in range(C)]
 Y_NEAR = [[col_of(z, 2 * h + p, c) for p in range(2)] for z in range(Z) for h in range(2) for c in range(C)]
-Z_LINES = [[col_of(z, y, c) for z in range(Z)] for y in range(Y) for c in range(C)]
+Z_LINES = [[col_of(z, y, (z + c) % C) for z in range(Z)] for y in range(Y) for c in range(C)]
 SWAP = [(s, s ^ 1) for s in range(N_COL)]
 SPREAD = [[row * N_COL + col for col in pair for row in range(BANDS)] for pair in Y_NEAR]
 
@@ -97,10 +97,13 @@
 
 
 def picked(cols_ref, own_ref, other_ref, list_ref):
-    row, _, core, near = place()
+    row, col, core, near = place()
+    line = lax.rem(col // (Y * C) + core, 2)
     picks = []
     for band in range(BANDS):
-        where = lambda quad, c, _, band=band: band * 3 + quad + jnp.where(core == c, 0, QUADS)
+        where = lambda quad, c, _, band=band: (
+            band * 3 + quad + QUADS * lax.rem(line + c + (band * 3 + quad) // 2, 2)
+        )
         count = list_live(cols_ref, list_ref, row, band, near, where)
         for j in range(CLASS):
             at = jnp.where(j < count, list_ref[j], 0)

time: 132 us -> 130 us (0.985)
  starting transfers between devices: 33.4 us -> 17.5 us
  blocking collectives: 82.2 us -> 93.4 us
  waiting for transfers between devices: 5.02 us -> 7.05 us
    ppermute x2, starting transfers between devices: 19.7 us -> 3.82 us  [lines(): return (own, lax.ppermute(own, 'col', SWAP))]
    all_gather x3, blocking collectives: 69.8 us -> 80.5 us  [gather(): lax.all_gather(value, 'col', axis=0, tiled=True, axis_index_groups=groups)]
  transfers between devices with their start and end apart: 4 -> 4, of which waited for: 3 -> 4; matrix products, arithmetic and copies ran while one was open for 0% -> 0% of each run, Pallas kernels for 4% -> 5%
where the time goes in v9:
time: 130 us; the launch traced here: 129 us
  blocking collectives  93.4 us (72%)
  starting transfers between devices  17.5 us (13%)
  Pallas kernels  10.4 us (8%)
  waiting for transfers between devices  7.05 us (5%)
    all_gather x3, blocking collectives, gather(): lax.all_gather(value, 'col', axis=0, tiled=True, axis_index_groups=groups)  80.5 us
    all_to_all x2, starting transfers between devices, exchange(): lax.all_to_all(value, axis, split_axis=0, concat_axis=0, tiled=True, axis...  13.7 us
    all_to_all x1, blocking collectives, exchange(): lax.all_to_all(value, axis, split_axis=0, concat_axis=0, tiled=True, axis...  12.9 us
    pallas_call x7, Pallas kernels, call(): pl.pallas_call(kernel, out_shape=[jax.ShapeDtypeStruct(shape, dtype) for...  6.85 us
    ppermute x2, waiting for transfers between devices, lines(): return (own, lax.ppermute(own, 'col', SWAP))  4.5 us
    ppermute x2, starting transfers between devices, lines(): return (own, lax.ppermute(own, 'col', SWAP))  3.82 us
    pallas_call x1, Pallas kernels, pack(): pl.pallas_call(pack_kernel, out_shape=jax.ShapeDtypeStruct((2, BANDS, CLA...  3.53 us
  transfers between devices with their start and end apart: 4, of which 4 were waited for; matrix products, arithmetic and copies ran while one was open for 0% of the time, Pallas kernels for 5%

profile of v9, /device:TPU:1, one launch (start us, length us, event | category | flops | bytes accessed | tf_op | source)
XLA Modules:
  0.0 129.2 jit_solution(14664039934993719421)
XLA Ops:
  0.0 0.0 copy-start.1
  0.0 0.8 copy-done.1
  0.8 0.7 copies.1
  1.4 5.4 %all-to-all-start = ((bf16[4,128,128]{2,1,0:T(8,128)(2,1)}), bf16[4,128,128]{2,1,0:T(8,128)(2,1)S(1)}, u32[]{:S(2)}, u32[]{:S(2)}) async-start(bf16[4,128,128]{2,1,0:T(8,128)(2,1)} %copies.1), calls=%async_computation | async-start | bytes 262144 | tf_op jit(solution)/shard_map/all_to_all | solution.py:173
  6.9 3.5 %pack.1 = bf16[2,8,4,128,128]{4,3,2,1,0:T(8,128)(2,1)} custom-call(s32[8,96]{1,0:T(8,128)} %cols_ref.11, bf16[8,12,128,128]{3,2,1,0:T(8,128)(2,1)} %bitcast.11), custom_call_target="tpu_custom_call" | custom-call | bytes 5242880 | tf_op jit(solution)/shard_map/pack/pallas_call | solution.py:70
  10.4 1.2 all-to-all-done.line_ref
  11.6 0.0 copy-start
  11.6 8.3 %all-to-all-start.1 = ((bf16[16,4,128,128]{3,2,1,0:T(8,128)(2,1)}), bf16[16,4,128,128]{3,2,1,0:T(8,128)(2,1)S(1)}, u32[]{:S(2)}, u32[]{:S(2)}) async-start(bf16[16,4,128,128]{3,2,1,0:T(8,128)(2,1)} %bitcast.10), calls=%async_computation.1 | async-start | bytes 4194304 | tf_op jit(solution)/shard_map/all_to_all | solution.py:173
  19.9 0.0 copy-done
  19.9 0.6 choose.1
  20.5 36.7 %all_gather.9.own_ref = bf16[24,128,128]{2,1,0:T(8,128)(2,1)S(1)} all-gather(bf16[2,128,128]{2,1,0:T(8,128)(2,1)S(1)} %choose.1), channel_id=1, replica_groups={{0,9,16,25,32,41,48,57,64,73,80,89},{1,8,17,24,33,40,49,56,65,72,81,88}..., dimensions={0}, use_global_device_ids=true | all-gather | bytes 851968 | tf_op jit(solution)/shard_map/all_gather | solution.py:169
  57.2 1.9 %collective-permute-start = (bf16[24,128,128]{2,1,0:T(8,128)(2,1)S(1)}, bf16[24,128,128]{2,1,0:T(8,128)(2,1)S(1)}, u32[]{:S(2)}, u32[]{:S(2)}) collective-permute-start(bf16[24,128,128]{2,1,0:T(8,128)(2,1)S(1)} %all_gather.9.own_ref), channel_id=1, source_target_pairs={{0,1},{1,0},{2,3},{3,2},{4,5},{5,4},{6,7},{7,6},{8,9},{9,8},{10,11... | collective-permute-start | bytes 2359304 | tf_op jit(solution)/shard_map/ppermute | solution.py:178
  59.2 2.3 %collective-permute-done.other_ref = bf16[24,128,128]{2,1,0:T(8,128)(2,1)S(1)} collective-permute-done((bf16[24,128,128]{2,1,0:T(8,128)(2,1)S(1)}, bf16[24,128,128]{2,1,0:T(8,128)(2,1)S(1)}, u32[]{:S(2)}, u32[]{:S(2)}) %collective-permute-start) | collective-permute-done | bytes 786464 | tf_op jit(solution)/shard_map/ppermute | solution.py:178
  61.4 1.7 %pick.1.left_ref = bf16[128,4096]{1,0:T(8,128)(2,1)S(1)} custom-call(s32[8,96]{1,0:T(8,128)S(1)} %copy-done, bf16[24,128,128]{2,1,0:T(8,128)(2,1)S(1)} %all_gather.9.own_ref, bf16[24,128,128]{2,1,0:T(8,128)(2,1)S(1)} %collective-permute-done.other_ref), custom_call_target="tpu_custom_call" | custom-call | tf_op jit(solution)/shard_map/pick/pallas_call | solution.py:157
  63.1 1.3 %all-to-all-done.1 = bf16[16,4,128,128]{3,2,1,0:T(8,128)(2,1)S(1)} async-done(((bf16[16,4,128,128]{3,2,1,0:T(8,128)(2,1)}), bf16[16,4,128,128]{3,2,1,0:T(8,128)(2,1)S(1)}, u32[]{:S(2)}, u32[]{:S(2)}) %all-to-all-start.1) | async-done | bytes 2097184 | tf_op jit(solution)/shard_map/all_to_all | solution.py:173
  64.4 1.1 multiply.1
  65.5 12.9 %all_to_all.15.shares_ref = f32[4,128,128]{2,1,0:T(8,128)S(1)} all-to-all(f32[4,128,128]{2,1,0:T(8,128)S(1)} %multiply.1), channel_id=1, replica_groups={{0,2,4,6},{1,3,5,7},{8,10,12,14},{9,11,13,15},{16,18,20,22},{17,19,21,2..., dimensions={0} | all-to-all | bytes 524288 | tf_op jit(solution)/shard_map/all_to_all | solution.py:173
  78.4 39.6 %all_gather.10.own_ref = bf16[24,128,128]{2,1,0:T(8,128)(2,1)S(1)} all-gather(bf16[2,128,128]{2,1,0:T(8,128)(2,1)S(1)} %get-tuple-element.13), channel_id=1, replica_groups={{0,9,16,25,32,41,48,57,64,73,80,89},{1,8,17,24,33,40,49,56,65,72,81,88}..., dimensions={0}, use_global_device_ids=true | all-gather | bytes 851968 | tf_op jit(solution)/shard_map/all_gather | solution.py:169
  118.0 1.9 %collective-permute-start.1 = (bf16[24,128,128]{2,1,0:T(8,128)(2,1)S(1)}, bf16[24,128,128]{2,1,0:T(8,128)(2,1)S(1)}, u32[]{:S(2)}, u32[]{:S(2)}) collective-permute-start(bf16[24,128,128]{2,1,0:T(8,128)(2,1)S(1)} %all_gather.10.own_ref), channel_id=1, source_target_pairs={{0,1},{1,0},{2,3},{3,2},{4,5},{5,4},{6,7},{7,6},{8,9},{9,8},{10,11... | collective-permute-start | bytes 2359304 | tf_op jit(solution)/shard_map/ppermute | solution.py:178
  119.9 2.2 %collective-permute-done.1.other_ref = bf16[24,128,128]{2,1,0:T(8,128)(2,1)S(1)} collective-permute-done((bf16[24,128,128]{2,1,0:T(8,128)(2,1)S(1)}, bf16[24,128,128]{2,1,0:T(8,128)(2,1)S(1)}, u32[]{:S(2)}, u32[]{:S(2)}) %collective-permute-start.1) | collective-permute-done | bytes 786464 | tf_op jit(solution)/shard_map/ppermute | solution.py:178
  122.1 1.5 %partials.1 = (f32[128,128]{1,0:T(8,128)S(1)}, f32[128,128]{1,0:T(8,128)S(1)}) custom-call(s32[8,96]{1,0:T(8,128)S(1)} %copy-done, bf16[24,128,128]{2,1,0:T(8,128)(2,1)S(1)} %all_gather.10.own_ref, bf16[24,128,128]{2,1,0:T(8,128)(2,1)S(1)} %collective-permute-done.1.other_ref, bf16[2,4096,128]{2,1,0:T(8,128)(2,1)S(1)} %bitcast.7), custom_call_target="tpu_custom_call" | custom-call | flops 268435456 | bytes 4194304 | tf_op jit(solution)/shard_map/partials/pallas_call | solution.py:157
  123.7 4.2 %all-gather = f32[256,128]{1,0:T(8,128)S(1)} all-gather(f32[128,128]{1,0:T(8,128)S(1)} %get-tuple-element.15), channel_id=2, replica_groups={{0,2},{1,3},{4,6},{5,7},{8,10},{9,11},{12,14},{13,15},{16,18},{17,19},{..., dimensions={0}, use_global_device_ids=true | all-gather | bytes 196608 | tf_op jit(solution)/shard_map/all_gather | solution.py:169
  127.9 1.2 final.1
  (1 shorter events, 0.0 us)
Async XLA Ops:
  0.0 0.8 copy-start.1
  1.4 10.2 %all-to-all-start = ((bf16[4,128,128]{2,1,0:T(8,128)(2,1)}), bf16[4,128,128]{2,1,0:T(8,128)(2,1)S(1)}, u32[]{:S(2)}, u32[]{:S(2)}) async-start(bf16[4,128,128]{2,1,0:T(8,128)(2,1)} %copies.1), calls=%async_computation | async-start | bytes 262144 | tf_op jit(solution)/shard_map/all_to_all | solution.py:173
  11.6 8.3 %copy-start = (s32[8,96]{1,0:T(8,128)S(1)}, s32[8,96]{1,0:T(8,128)}, u32[]{:S(2)}) copy-start(s32[8,96]{1,0:T(8,128)} %cols_ref.11) | copy-start | bytes 9220
  11.6 52.8 %all-to-all-start.1 = ((bf16[16,4,128,128]{3,2,1,0:T(8,128)(2,1)}), bf16[16,4,128,128]{3,2,1,0:T(8,128)(2,1)S(1)}, u32[]{:S(2)}, u32[]{:S(2)}) async-start(bf16[16,4,128,128]{3,2,1,0:T(8,128)(2,1)} %bitcast.10), calls=%async_computation.1 | async-start | bytes 4194304 | tf_op jit(solution)/shard_map/all_to_all | solution.py:173
  57.2 4.2 %collective-permute-start = (bf16[24,128,128]{2,1,0:T(8,128)(2,1)S(1)}, bf16[24,128,128]{2,1,0:T(8,128)(2,1)S(1)}, u32[]{:S(2)}, u32[]{:S(2)}) collective-permute-start(bf16[24,128,128]{2,1,0:T(8,128)(2,1)S(1)} %all_gather.9.own_ref), channel_id=1, source_target_pairs={{0,1},{1,0},{2,3},{3,2},{4,5},{5,4},{6,7},{7,6},{8,9},{9,8},{10,11... | collective-permute-start | bytes 2359304 | tf_op jit(solution)/shard_map/ppermute | solution.py:178
  118.0 4.2 %collective-permute-start.1 = (bf16[24,128,128]{2,1,0:T(8,128)(2,1)S(1)}, bf16[24,128,128]{2,1,0:T(8,128)(2,1)S(1)}, u32[]{:S(2)}, u32[]{:S(2)}) collective-permute-start(bf16[24,128,128]{2,1,0:T(8,128)(2,1)S(1)} %all_gather.10.own_ref), channel_id=1, source_target_pairs={{0,1},{1,0},{2,3},{3,2},{4,5},{5,4},{6,7},{7,6},{8,9},{9,8},{10,11... | collective-permute-start | bytes 2359304 | tf_op jit(solution)/shard_map/ppermute | solution.py:178

commit v10 on v9

--- a/solution.py
+++ b/solution.py
@@ -25,6 +25,7 @@
 Y_NEAR = [[col_of(z, 2 * h + p, c) for p in range(2)] for z in range(Z) for h in range(2) for c in range(C)]
 Z_LINES = [[col_of(z, y, (z + c) % C) for z in range(Z)] for y in range(Y) for c in range(C)]
 SWAP = [(s, s ^ 1) for s in range(N_COL)]
+Y_OTHERS = [[(s, s ^ step * C) for s in range(N_COL)] for step in (1, 2, 3)]
 SPREAD = [[row * N_COL + col for col in pair for row in range(BANDS)] for pair in Y_NEAR]
 
 
@@ -83,27 +84,24 @@
     )(win_cols, couple)
 
 
-def copies_kernel(x_ref, out_ref):
-    for y in range(Y):
-        out_ref[y] = x_ref[0]
-
-
-def choose_kernel(cols_ref, line_ref, out_ref):
+def choose_kernel(cols_ref, mine_ref, theirs_ref, far_mine_ref, far_theirs_ref, out_ref):
     row, col, core, near = place()
-    first = col // (Y * C) * (Y * C) + core
-    for h in range(2):
-        alive = pair_alive(cols_ref, row, first + 2 * h * C)
-        out_ref[h] = line_ref[2 * h + member_of(alive, near)]
+    here = col - near * C
+    pairs = ((here, mine_ref, theirs_ref), (here ^ 2 * C, far_mine_ref, far_theirs_ref))
+    for n, (first, same_ref, other_ref) in enumerate(pairs):
+        alive = pair_alive(cols_ref, row, first)
+        out_ref[n] = jnp.where(member_of(alive, near) == near, same_ref[...], other_ref[...])
 
 
 def picked(cols_ref, own_ref, other_ref, list_ref):
     row, col, core, near = place()
-    line = lax.rem(col // (Y * C) + core, 2)
+    line, half = lax.rem(col // (Y * C) + core, 2), lax.rem(col // (2 * C), 2)
     picks = []
     for band in range(BANDS):
-        where = lambda quad, c, _, band=band: (
-            band * 3 + quad + QUADS * lax.rem(line + c + (band * 3 + quad) // 2, 2)
-        )
+        def where(quad, c, _, band=band):
+            z, h = divmod(band * 3 + quad, 2)
+            return z * 2 + lax.rem(half + h, 2) + QUADS * lax.rem(line + c + z, 2)
+
         count = list_live(cols_ref, list_ref, row, band, near, where)
         for j in range(CLASS):
             at = jnp.where(j < count, list_ref[j], 0)
@@ -140,9 +138,10 @@
 
 def square_kernel(shares_ref, square_ref, half_ref):
     h = lax.rem(lax.axis_index("col") // (2 * C), 2)
-    square_ref[...] = shares_ref[2 * h] + shares_ref[2 * h + 1]
+    totals = [shares_ref[2 * pair] + shares_ref[2 * pair + 1] for pair in (h, 1 - h)]
+    square_ref[...] = totals[0]
     for pair in range(2):
-        half_ref[pair] = (shares_ref[2 * pair] + shares_ref[2 * pair + 1]).astype(half_ref.dtype)
+        half_ref[pair] = totals[pair].astype(half_ref.dtype)
 
 
 def final_kernel(cols_ref, keep_ref, both_ref, square_ref, out_ref):
@@ -184,13 +183,13 @@
     flops = lambda count: pl.CostEstimate(flops=count * BS**3, bytes_accessed=4 << 20, transcendentals=0)
     shares = [(block, jnp.float32)] * 2
 
+    x = win_vals[0, 0]
+    others = [lax.ppermute(x, "col", route) for route in Y_OTHERS]
     packed = pack(win_cols, couple_vals[0, 0])
-    (line,) = call(copies_kernel, "copies", [((Y,) + block, jnp.bfloat16)], (win_vals[0],))
-    line = exchange(line, "col", Y_LINES)
-    line, packed = lax.optimization_barrier((line, packed))
+    *others, packed = lax.optimization_barrier((*others, packed))
     held = exchange(packed.reshape((2 * BANDS, CLASS) + block), ("row", "col"), SPREAD)
     held = held.reshape(2, BANDS * CLASS * BS, BS)
-    (line,) = call(choose_kernel, "choose", [((2,) + block, jnp.bfloat16)], (line,), cols)
+    (line,) = call(choose_kernel, "choose", [((2,) + block, jnp.bfloat16)], (x, *others), cols)
     left = [((BS, BANDS * CLASS * BS), jnp.bfloat16)]
     (left,) = call(pick_kernel, "pick", left, lines(line), cols, 8, **lists)
     outs = [((Y,) + block, jnp.float32)]

time: 130 us -> 133 us (1.023)
  starting transfers between devices: 17.5 us -> 23.3 us
  blocking collectives: 93.4 us -> 89.7 us
  waiting for transfers between devices: 7.05 us -> 9.24 us
    ppermute x0 -> x3, starting transfers between devices: none -> 10.2 us  [on_device(): others = [lax.ppermute(x, 'col', route) for route in Y_OTHERS]]
    all_to_all x2 -> x1, starting transfers between devices: 13.7 us -> 9.33 us  [exchange(): lax.all_to_all(value, axis, split_axis=0, concat_axis=0, tiled=True, axis...]
    all_gather x3, blocking collectives: 80.5 us -> 77.5 us  [gather(): lax.all_gather(value, 'col', axis=0, tiled=True, axis_index_groups=groups)]
    all_to_all x2 -> x1, waiting for transfers between devices: 2.55 us -> 4.74 us  [exchange(): lax.all_to_all(value, axis, split_axis=0, concat_axis=0, tiled=True, axis...]
    pallas_call x7 -> x6, Pallas kernels: 6.85 us -> 6.22 us  [call(): pl.pallas_call(kernel, out_shape=[jax.ShapeDtypeStruct(shape, dtype) for...]
  transfers between devices with their start and end apart: 4 -> 6, of which waited for: 4 -> 3; matrix products, arithmetic and copies ran while one was open for 0% -> 0% of each run, Pallas kernels for 5% -> 4%
where the time goes in v10:
time: 133 us; the launch traced here: 132 us
  blocking collectives  89.7 us (67%)
  starting transfers between devices  23.3 us (18%)
  Pallas kernels  9.77 us (7%)
  waiting for transfers between devices  9.24 us (7%)
    all_gather x3, blocking collectives, gather(): lax.all_gather(value, 'col', axis=0, tiled=True, axis_index_groups=groups)  77.5 us
    all_to_all x1, blocking collectives, exchange(): lax.all_to_all(value, axis, split_axis=0, concat_axis=0, tiled=True, axis...  12.2 us
    ppermute x3, starting transfers between devices, on_device(): others = [lax.ppermute(x, 'col', route) for route in Y_OTHERS]  10.2 us
    all_to_all x1, starting transfers between devices, exchange(): lax.all_to_all(value, axis, split_axis=0, concat_axis=0, tiled=True, axis...  9.33 us
    pallas_call x6, Pallas kernels, call(): pl.pallas_call(kernel, out_shape=[jax.ShapeDtypeStruct(shape, dtype) for...  6.22 us
    all_to_all x1, waiting for transfers between devices, exchange(): lax.all_to_all(value, axis, split_axis=0, concat_axis=0, tiled=True, axis...  4.74 us
    ppermute x2, waiting for transfers between devices, lines(): return (own, lax.ppermute(own, 'col', SWAP))  4.5 us
    ppermute x2, starting transfers between devices, lines(): return (own, lax.ppermute(own, 'col', SWAP))  3.82 us
  transfers between devices with their start and end apart: 6, of which 3 were waited for; matrix products, arithmetic and copies ran while one was open for 0% of the time, Pallas kernels for 4%

profile of v10, /device:TPU:1, one launch (start us, length us, event | category | flops | bytes accessed | tf_op | source)
XLA Modules:
  0.0 132.2 jit_solution(2469485584352353843)
XLA Ops:
  0.0 6.0 %collective-permute-start.2 = (bf16[128,128]{1,0:T(8,128)(2,1)}, bf16[128,128]{1,0:T(8,128)(2,1)S(1)}, u32[]{:S(2)}, u32[]{:S(2)}) collective-permute-start(bf16[128,128]{1,0:T(8,128)(2,1)} %bitcast.9), channel_id=1, source_target_pairs={{0,6},{1,7},{2,4},{3,5},{4,2},{5,3},{6,0},{7,1},{8,14},{9,15},{10,... | collective-permute-start | bytes 98312 | tf_op jit(solution)/shard_map/ppermute | solution.py:187
  6.1 1.9 %collective-permute-start.1 = (bf16[128,128]{1,0:T(8,128)(2,1)}, bf16[128,128]{1,0:T(8,128)(2,1)S(1)}, u32[]{:S(2)}, u32[]{:S(2)}) collective-permute-start(bf16[128,128]{1,0:T(8,128)(2,1)} %bitcast.10), channel_id=1, source_target_pairs={{0,4},{1,5},{2,6},{3,7},{4,0},{5,1},{6,2},{7,3},{8,12},{9,13},{10,... | collective-permute-start | bytes 98312 | tf_op jit(solution)/shard_map/ppermute | solution.py:187
  8.0 2.2 %collective-permute-start = (bf16[128,128]{1,0:T(8,128)(2,1)}, bf16[128,128]{1,0:T(8,128)(2,1)S(1)}, u32[]{:S(2)}, u32[]{:S(2)}) collective-permute-start(bf16[128,128]{1,0:T(8,128)(2,1)} %bitcast.11), channel_id=1, source_target_pairs={{0,2},{1,3},{2,0},{3,1},{4,6},{5,7},{6,4},{7,5},{8,10},{9,11},{10,... | collective-permute-start | bytes 98312 | tf_op jit(solution)/shard_map/ppermute | solution.py:187
  10.2 3.6 %pack.1 = bf16[2,8,4,128,128]{4,3,2,1,0:T(8,128)(2,1)} custom-call(s32[8,96]{1,0:T(8,128)} %cols_ref.11, bf16[8,12,128,128]{3,2,1,0:T(8,128)(2,1)} %bitcast.14), custom_call_target="tpu_custom_call" | custom-call | bytes 5242880 | tf_op jit(solution)/shard_map/pack/pallas_call | solution.py:71
  13.7 0.0 collective-permute-done.2.far_theirs_ref
  13.7 0.0 collective-permute-done.1.far_mine_ref
  13.8 0.0 collective-permute-done.theirs_ref
  13.8 0.0 copy-start
  13.8 0.0 copy-start.1
  13.8 9.3 %all-to-all-start = ((bf16[16,4,128,128]{3,2,1,0:T(8,128)(2,1)}), bf16[16,4,128,128]{3,2,1,0:T(8,128)(2,1)S(1)}, u32[]{:S(2)}, u32[]{:S(2)}) async-start(bf16[16,4,128,128]{3,2,1,0:T(8,128)(2,1)} %bitcast.13), calls=%async_computation | async-start | bytes 4194304 | tf_op jit(solution)/shard_map/all_to_all | solution.py:172
  23.1 0.6 choose.1
  23.8 35.9 %all_gather.9.own_ref = bf16[24,128,128]{2,1,0:T(8,128)(2,1)S(1)} all-gather(bf16[2,128,128]{2,1,0:T(8,128)(2,1)S(1)} %choose.1), channel_id=1, replica_groups={{0,9,16,25,32,41,48,57,64,73,80,89},{1,8,17,24,33,40,49,56,65,72,81,88}..., dimensions={0}, use_global_device_ids=true | all-gather | bytes 851968 | tf_op jit(solution)/shard_map/all_gather | solution.py:168
  59.6 1.9 %collective-permute-start.3 = (bf16[24,128,128]{2,1,0:T(8,128)(2,1)S(1)}, bf16[24,128,128]{2,1,0:T(8,128)(2,1)S(1)}, u32[]{:S(2)}, u32[]{:S(2)}) collective-permute-start(bf16[24,128,128]{2,1,0:T(8,128)(2,1)S(1)} %all_gather.9.own_ref), channel_id=1, source_target_pairs={{0,1},{1,0},{2,3},{3,2},{4,5},{5,4},{6,7},{7,6},{8,9},{9,8},{10,11... | collective-permute-start | bytes 2359304 | tf_op jit(solution)/shard_map/ppermute | solution.py:177
  61.6 2.3 %collective-permute-done.3.other_ref = bf16[24,128,128]{2,1,0:T(8,128)(2,1)S(1)} collective-permute-done((bf16[24,128,128]{2,1,0:T(8,128)(2,1)S(1)}, bf16[24,128,128]{2,1,0:T(8,128)(2,1)S(1)}, u32[]{:S(2)}, u32[]{:S(2)}) %collective-permute-start.3) | collective-permute-done | bytes 786464 | tf_op jit(solution)/shard_map/ppermute | solution.py:177
  63.8 1.7 %pick.1.left_ref = bf16[128,4096]{1,0:T(8,128)(2,1)S(1)} custom-call(s32[8,96]{1,0:T(8,128)S(1)} %copy-done, bf16[24,128,128]{2,1,0:T(8,128)(2,1)S(1)} %all_gather.9.own_ref, bf16[24,128,128]{2,1,0:T(8,128)(2,1)S(1)} %collective-permute-done.3.other_ref), custom_call_target="tpu_custom_call" | custom-call | tf_op jit(solution)/shard_map/pick/pallas_call | solution.py:156
  65.5 4.7 %all-to-all-done = bf16[16,4,128,128]{3,2,1,0:T(8,128)(2,1)S(1)} async-done(((bf16[16,4,128,128]{3,2,1,0:T(8,128)(2,1)}), bf16[16,4,128,128]{3,2,1,0:T(8,128)(2,1)S(1)}, u32[]{:S(2)}, u32[]{:S(2)}) %all-to-all-start) | async-done | bytes 2097184 | tf_op jit(solution)/shard_map/all_to_all | solution.py:172
  70.2 1.1 multiply.1
  71.3 12.2 %all_to_all.10.shares_ref = f32[4,128,128]{2,1,0:T(8,128)S(1)} all-to-all(f32[4,128,128]{2,1,0:T(8,128)S(1)} %multiply.1), channel_id=1, replica_groups={{0,2,4,6},{1,3,5,7},{8,10,12,14},{9,11,13,15},{16,18,20,22},{17,19,21,2..., dimensions={0} | all-to-all | bytes 524288 | tf_op jit(solution)/shard_map/all_to_all | solution.py:172
  83.5 37.4 %all_gather.10.own_ref = bf16[24,128,128]{2,1,0:T(8,128)(2,1)S(1)} all-gather(bf16[2,128,128]{2,1,0:T(8,128)(2,1)S(1)} %get-tuple-element.17), channel_id=1, replica_groups={{0,9,16,25,32,41,48,57,64,73,80,89},{1,8,17,24,33,40,49,56,65,72,81,88}..., dimensions={0}, use_global_device_ids=true | all-gather | bytes 851968 | tf_op jit(solution)/shard_map/all_gather | solution.py:168
  120.9 1.9 %collective-permute-start.4 = (bf16[24,128,128]{2,1,0:T(8,128)(2,1)S(1)}, bf16[24,128,128]{2,1,0:T(8,128)(2,1)S(1)}, u32[]{:S(2)}, u32[]{:S(2)}) collective-permute-start(bf16[24,128,128]{2,1,0:T(8,128)(2,1)S(1)} %all_gather.10.own_ref), channel_id=1, source_target_pairs={{0,1},{1,0},{2,3},{3,2},{4,5},{5,4},{6,7},{7,6},{8,9},{9,8},{10,11... | collective-permute-start | bytes 2359304 | tf_op jit(solution)/shard_map/ppermute | solution.py:177
  122.9 2.2 %collective-permute-done.4.other_ref = bf16[24,128,128]{2,1,0:T(8,128)(2,1)S(1)} collective-permute-done((bf16[24,128,128]{2,1,0:T(8,128)(2,1)S(1)}, bf16[24,128,128]{2,1,0:T(8,128)(2,1)S(1)}, u32[]{:S(2)}, u32[]{:S(2)}) %collective-permute-start.4) | collective-permute-done | bytes 786464 | tf_op jit(solution)/shard_map/ppermute | solution.py:177
  125.1 1.6 %partials.1 = (f32[128,128]{1,0:T(8,128)S(1)}, f32[128,128]{1,0:T(8,128)S(1)}) custom-call(s32[8,96]{1,0:T(8,128)S(1)} %copy-done, bf16[24,128,128]{2,1,0:T(8,128)(2,1)S(1)} %all_gather.10.own_ref, bf16[24,128,128]{2,1,0:T(8,128)(2,1)S(1)} %collective-permute-done.4.other_ref, bf16[2,4096,128]{2,1,0:T(8,128)(2,1)S(1)} %bitcast.7), custom_call_target="tpu_custom_call" | custom-call | flops 268435456 | bytes 4194304 | tf_op jit(solution)/shard_map/partials/pallas_call | solution.py:156
  126.7 4.2 %all-gather = f32[256,128]{1,0:T(8,128)S(1)} all-gather(f32[128,128]{1,0:T(8,128)S(1)} %get-tuple-element.19), channel_id=2, replica_groups={{0,2},{1,3},{4,6},{5,7},{8,10},{9,11},{12,14},{13,15},{16,18},{17,19},{..., dimensions={0}, use_global_device_ids=true | all-gather | bytes 196608 | tf_op jit(solution)/shard_map/all_gather | solution.py:168
  130.9 1.2 final.1
  (3 shorter events, 0.0 us)
Async XLA Ops:
  0.0 13.7 %collective-permute-start.2 = (bf16[128,128]{1,0:T(8,128)(2,1)}, bf16[128,128]{1,0:T(8,128)(2,1)S(1)}, u32[]{:S(2)}, u32[]{:S(2)}) collective-permute-start(bf16[128,128]{1,0:T(8,128)(2,1)} %bitcast.9), channel_id=1, source_target_pairs={{0,6},{1,7},{2,4},{3,5},{4,2},{5,3},{6,0},{7,1},{8,14},{9,15},{10,... | collective-permute-start | bytes 98312 | tf_op jit(solution)/shard_map/ppermute | solution.py:187
  6.1 7.7 %collective-permute-start.1 = (bf16[128,128]{1,0:T(8,128)(2,1)}, bf16[128,128]{1,0:T(8,128)(2,1)S(1)}, u32[]{:S(2)}, u32[]{:S(2)}) collective-permute-start(bf16[128,128]{1,0:T(8,128)(2,1)} %bitcast.10), channel_id=1, source_target_pairs={{0,4},{1,5},{2,6},{3,7},{4,0},{5,1},{6,2},{7,3},{8,12},{9,13},{10,... | collective-permute-start | bytes 98312 | tf_op jit(solution)/shard_map/ppermute | solution.py:187
  8.0 5.8 %collective-permute-start = (bf16[128,128]{1,0:T(8,128)(2,1)}, bf16[128,128]{1,0:T(8,128)(2,1)S(1)}, u32[]{:S(2)}, u32[]{:S(2)}) collective-permute-start(bf16[128,128]{1,0:T(8,128)(2,1)} %bitcast.11), channel_id=1, source_target_pairs={{0,2},{1,3},{2,0},{3,1},{4,6},{5,7},{6,4},{7,5},{8,10},{9,11},{10,... | collective-permute-start | bytes 98312 | tf_op jit(solution)/shard_map/ppermute | solution.py:187
  13.8 9.4 %copy-start = (s32[8,96]{1,0:T(8,128)S(1)}, s32[8,96]{1,0:T(8,128)}, u32[]{:S(2)}) copy-start(s32[8,96]{1,0:T(8,128)} %cols_ref.11) | copy-start | bytes 9220
  13.8 9.4 %copy-start.1 = (bf16[1,1,128,128]{3,2,1,0:T(8,128)(2,1)S(1)}, bf16[1,1,128,128]{3,2,1,0:T(8,128)(2,1)}, u32[]{:S(2)}) copy-start(bf16[1,1,128,128]{3,2,1,0:T(8,128)(2,1)} %param.3) | copy-start | bytes 98308
  13.8 56.5 %all-to-all-start = ((bf16[16,4,128,128]{3,2,1,0:T(8,128)(2,1)}), bf16[16,4,128,128]{3,2,1,0:T(8,128)(2,1)S(1)}, u32[]{:S(2)}, u32[]{:S(2)}) async-start(bf16[16,4,128,128]{3,2,1,0:T(8,128)(2,1)} %bitcast.13), calls=%async_computation | async-start | bytes 4194304 | tf_op jit(solution)/shard_map/all_to_all | solution.py:172
  59.6 4.2 %collective-permute-start.3 = (bf16[24,128,128]{2,1,0:T(8,128)(2,1)S(1)}, bf16[24,128,128]{2,1,0:T(8,128)(2,1)S(1)}, u32[]{:S(2)}, u32[]{:S(2)}) collective-permute-start(bf16[24,128,128]{2,1,0:T(8,128)(2,1)S(1)} %all_gather.9.own_ref), channel_id=1, source_target_pairs={{0,1},{1,0},{2,3},{3,2},{4,5},{5,4},{6,7},{7,6},{8,9},{9,8},{10,11... | collective-permute-start | bytes 2359304 | tf_op jit(solution)/shard_map/ppermute | solution.py:177
  120.9 4.2 %collective-permute-start.4 = (bf16[24,128,128]{2,1,0:T(8,128)(2,1)S(1)}, bf16[24,128,128]{2,1,0:T(8,128)(2,1)S(1)}, u32[]{:S(2)}, u32[]{:S(2)}) collective-permute-start(bf16[24,128,128]{2,1,0:T(8,128)(2,1)S(1)} %all_gather.10.own_ref), channel_id=1, source_target_pairs={{0,1},{1,0},{2,3},{3,2},{4,5},{5,4},{6,7},{7,6},{8,9},{9,8},{10,11... | collective-permute-start | bytes 2359304 | tf_op jit(solution)/shard_map/ppermute | solution.py:177

commit v11 on v7

--- a/solution.py
+++ b/solution.py
@@ -24,7 +24,7 @@
 Y_LINES = [[col_of(z, y, c) for y in range(Y)] for z in range(Z) for c in range(C)]
 Y_FAR = [[col_of(z, 2 * h + p, c) for h in range(2)] for z in range(Z) for p in range(2) for c in range(C)]
 Y_NEAR = [[col_of(z, 2 * h + p, c) for p in range(2)] for z in range(Z) for h in range(2) for c in range(C)]
-Z_LINES = [[col_of(z, y, c) for z in range(Z)] for y in range(Y) for c in range(C)]
+Z_LINES = [[col_of(z, y, (z + c) % C) for z in range(Z)] for y in range(Y) for c in range(C)]
 SWAP = [(s, s ^ 1) for s in range(N_COL)]
 SPREAD = [[row * N_COL + col for col in pair for row in range(BANDS)] for pair in Y_NEAR]
 
@@ -84,6 +84,11 @@
     )(win_cols, couple)
 
 
+def copies_kernel(x_ref, out_ref):
+    for y in range(Y):
+        out_ref[y] = x_ref[0]
+
+
 def choose_kernel(cols_ref, line_ref, out_ref):
     row, col, core, near = place()
     first = col // (Y * C) * (Y * C) + core
@@ -92,39 +97,53 @@
         out_ref[h] = line_ref[2 * h + member_of(alive, near)]
 
 
-def picked(cols_ref, own_ref, other_ref, list_ref):
-    row, _, core, near = place()
-    picks = []
+def list_picks(cols_ref, list_ref, picks_ref):
+    row, col, core, near = place()
+    line = lax.rem(col // (Y * C) + core, 2)
     for band in range(BANDS):
-        where = lambda quad, c, _, band=band: band * 3 + quad + jnp.where(core == c, 0, QUADS)
+        where = lambda quad, c, _, band=band: (
+            band * 3 + quad + QUADS * lax.rem(line + c + (band * 3 + quad) // 2, 2)
+        )
         count = list_live(cols_ref, list_ref, row, band, near, where)
         for j in range(CLASS):
-            at = jnp.where(j < count, list_ref[j], 0)
-            inside = lax.rem(at, QUADS)
-            block = jnp.where(at < QUADS, own_ref[inside], other_ref[inside])
-            picks.append(jnp.where(j < count, block, jnp.zeros_like(block)))
-    return jnp.concatenate(picks, axis=1)
-
-
-def multiply(cols_ref, left, m_ref, keep_ref, send_ref):
+            picks_ref[band * CLASS + j] = jnp.where(j < count, list_ref[j], -1)
+
+
+def picked(picks_ref, own_ref, other_ref):
+    blocks = []
+    for n in range(BANDS * CLASS):
+        pick = picks_ref[n]
+        inside = lax.rem(jnp.maximum(pick, 0), QUADS)
+        block = jnp.where(pick < QUADS, own_ref[inside], other_ref[inside])
+        blocks.append(jnp.where(pick >= 0, block, jnp.zeros_like(block)))
+    return jnp.concatenate(blocks, axis=1)
+
+
+def multiply(cols_ref, left, m_ref):
     row, col, _, near = place()
     alive = pair_alive(cols_ref, row, col - near * C)
-    chosen = [m_ref[member_of(alive, k)] for k in (near, 1 - near)]
+    chosen = [m_ref[member_of(alive, k)] for k in range(2)]
     product = jnp.dot(left, jnp.concatenate(chosen, axis=1), preferred_element_type=jnp.float32)
-    keep_ref[...] = product[:, :BS]
-    send_ref[...] = product[:, BS:]
-
-
-def pick_kernel(cols_ref, own_ref, other_ref, left_ref, list_ref):
-    left_ref[...] = picked(cols_ref, own_ref, other_ref, list_ref)
+    return product[:, :BS], product[:, BS:]
+
+
+def pick_kernel(cols_ref, own_ref, other_ref, left_ref, picks_ref, list_ref):
+    list_picks(cols_ref, list_ref, picks_ref)
+    left_ref[...] = picked(picks_ref, own_ref, other_ref)
+
+
+def share(keep_ref, send_ref, shares):
+    near = place()[3]
+    keep_ref[...] = jnp.where(near == 0, *shares)
+    send_ref[0] = jnp.where(near == 0, *shares[::-1])
 
 
 def multiply_kernel(cols_ref, left_ref, m_ref, keep_ref, send_ref):
-    multiply(cols_ref, left_ref[...], m_ref, keep_ref, send_ref)
-
-
-def partial_kernel(cols_ref, own_ref, other_ref, m_ref, keep_ref, send_ref, list_ref):
-    multiply(cols_ref, picked(cols_ref, own_ref, other_ref, list_ref), m_ref, keep_ref, send_ref)
+    share(keep_ref, send_ref, multiply(cols_ref, left_ref[...], m_ref))
+
+
+def partial_kernel(cols_ref, picks_ref, own_ref, other_ref, m_ref, keep_ref, send_ref):
+    share(keep_ref, send_ref, multiply(cols_ref, picked(picks_ref, own_ref, other_ref), m_ref))
 
 
 def square_kernel(keep_ref, both_ref, square_ref, half_ref):
@@ -141,12 +160,12 @@
 
 
 def call(kernel, name, outs, arrays, scalars=(), grant=4, **options):
-    vmem = pl.BlockSpec(memory_space=pltpu.VMEM)
+    smem, vmem = (pl.BlockSpec(memory_space=space) for space in (pltpu.SMEM, pltpu.VMEM))
     return pl.pallas_call(
         kernel,
         out_shape=[jax.ShapeDtypeStruct(shape, dtype) for shape, dtype in outs],
-        in_specs=[pl.BlockSpec(memory_space=pltpu.SMEM)] * len(scalars) + [vmem] * len(arrays),
-        out_specs=[vmem] * len(outs),
+        in_specs=[smem] * len(scalars) + [vmem] * len(arrays),
+        out_specs=[smem if dtype == jnp.int32 else vmem for _, dtype in outs],
         compiler_params=pltpu.CompilerParams(vmem_limit_bytes=grant << 20),
         name=name,
         **options,
@@ -170,25 +189,27 @@
     block, cols = (BS, BS), (win_cols,)
     lists = dict(scratch_shapes=[pltpu.SMEM((CLASS + 1,), jnp.int32)])
     flops = lambda count: pl.CostEstimate(flops=count * BS**3, bytes_accessed=4 << 20, transcendentals=0)
-    shares = [(block, jnp.float32)] * 2
+    shares = [(block, jnp.float32), ((1,) + block, jnp.float32)]
 
     packed = pack(win_cols, couple_vals[0, 0])
-    line = exchange(jnp.broadcast_to(win_vals[0], (Y,) + block), "col", Y_LINES)
+    (line,) = call(copies_kernel, "copies", [((Y,) + block, jnp.bfloat16)], (win_vals[0],))
+    line = exchange(line, "col", Y_LINES)
     line, packed = lax.optimization_barrier((line, packed))
     held = exchange(packed.reshape((2 * BANDS, CLASS) + block), ("row", "col"), SPREAD)
     held = held.reshape(2, BANDS * CLASS * BS, BS)
     (line,) = call(choose_kernel, "choose", [((2,) + block, jnp.bfloat16)], (line,), cols)
-    left = [((BS, BANDS * CLASS * BS), jnp.bfloat16)]
-    (left,) = call(pick_kernel, "pick", left, lines(line), cols, 8, **lists)
+    outs = [((BS, BANDS * CLASS * BS), jnp.bfloat16), ((BANDS * CLASS,), jnp.int32)]
+    left, picks = call(pick_kernel, "pick", outs, lines(line), cols, 8, **lists)
     keep, send = call(multiply_kernel, "multiply", shares, (left, held), cols, 16, cost_estimate=flops(128))
 
     outs = [(block, jnp.float32), ((1,) + block, jnp.bfloat16)]
-    square, half = call(square_kernel, "square", outs, (keep, gather(send[None], Y_NEAR)))
+    square, half = call(square_kernel, "square", outs, (keep, gather(send, Y_NEAR)))
 
     line = lines(gather(half, Y_FAR))
-    keep, send = call(partial_kernel, "partials", shares, (*line, held), cols, 16, cost_estimate=flops(128), **lists)
+    scalars = (win_cols, picks)
+    keep, send = call(partial_kernel, "partials", shares, (*line, held), scalars, 16, cost_estimate=flops(128))
     outs = [(block, jnp.bfloat16)]
-    (purified,) = call(final_kernel, "final", outs, (keep, gather(send[None], Y_NEAR), square), cols)
+    (purified,) = call(final_kernel, "final", outs, (keep, gather(send, Y_NEAR), square), cols)
     return purified[None, None]
 
 

time: 133 us -> 130 us (0.977)
  starting transfers between devices: 36.4 us -> 17.5 us
  blocking collectives: 80.2 us -> 94.3 us
  waiting for transfers between devices: 5.02 us -> 6.47 us
    ppermute x2, starting transfers between devices: 22.7 us -> 3.82 us  [lines(): return (own, lax.ppermute(own, 'col', SWAP))]
    all_gather x5, blocking collectives: 80.2 us -> 94.3 us  [gather(): lax.all_gather(value, 'col', axis=0, tiled=True, axis_index_groups=groups)]
    broadcast_in_dim x1 -> x0, local copies, waits for them, and re-layouts: 1.43 us -> none  [on_device(): line = exchange(jnp.broadcast_to(win_vals[0], (Y,) + block), 'col', Y_LINES)]
    pallas_call x6 -> x7, Pallas kernels: 6.14 us -> 7.1 us  [call(): pl.pallas_call(kernel, out_shape=[jax.ShapeDtypeStruct(shape, dtype) for...]
  transfers between devices with their start and end apart: 4 -> 4, of which waited for: 3 -> 4; matrix products, arithmetic and copies ran while one was open for 0% -> 0% of each run, Pallas kernels for 4% -> 5%
where the time goes in v11:
time: 130 us
  blocking collectives  94.3 us (73%)
  starting transfers between devices  17.5 us (13%)
  Pallas kernels  10.6 us (8%)
  waiting for transfers between devices  6.47 us (5%)
    all_gather x5, blocking collectives, gather(): lax.all_gather(value, 'col', axis=0, tiled=True, axis_index_groups=groups)  94.3 us
    all_to_all x2, starting transfers between devices, exchange(): lax.all_to_all(value, axis, split_axis=0, concat_axis=0, tiled=True, axis...  13.7 us
    pallas_call x7, Pallas kernels, call(): pl.pallas_call(kernel, out_shape=[jax.ShapeDtypeStruct(shape, dtype) for...  7.1 us
    ppermute x2, waiting for transfers between devices, lines(): return (own, lax.ppermute(own, 'col', SWAP))  4.5 us
    ppermute x2, starting transfers between devices, lines(): return (own, lax.ppermute(own, 'col', SWAP))  3.82 us
    pallas_call x1, Pallas kernels, pack(): pl.pallas_call(pack_kernel, out_shape=jax.ShapeDtypeStruct((2, BANDS, CLA...  3.53 us
  transfers between devices with their start and end apart: 4, of which 4 were waited for; matrix products, arithmetic and copies ran while one was open for 0% of the time, Pallas kernels for 5%

profile of v11, /device:TPU:1, one launch (start us, length us, event | category | flops | bytes accessed | tf_op | source)
XLA Modules:
  0.0 129.7 jit_solution(6622223928164282491)
XLA Ops:
  0.0 0.0 copy-start.1
  0.0 0.8 copy-done.1
  0.8 0.7 copies.1
  1.4 5.4 %all-to-all-start = ((bf16[4,128,128]{2,1,0:T(8,128)(2,1)}), bf16[4,128,128]{2,1,0:T(8,128)(2,1)S(1)}, u32[]{:S(2)}, u32[]{:S(2)}) async-start(bf16[4,128,128]{2,1,0:T(8,128)(2,1)} %copies.1), calls=%async_computation | async-start | bytes 262144 | tf_op jit(solution)/shard_map/all_to_all | solution.py:180
  6.8 3.5 %pack.1 = bf16[2,8,4,128,128]{4,3,2,1,0:T(8,128)(2,1)} custom-call(s32[8,96]{1,0:T(8,128)} %cols_ref.11, bf16[8,12,128,128]{3,2,1,0:T(8,128)(2,1)} %bitcast.9), custom_call_target="tpu_custom_call" | custom-call | bytes 5242880 | tf_op jit(solution)/shard_map/pack/pallas_call | solution.py:71
  10.4 1.2 all-to-all-done.line_ref
  11.6 0.0 copy-start
  11.6 8.3 %all-to-all-start.1 = ((bf16[16,4,128,128]{3,2,1,0:T(8,128)(2,1)}), bf16[16,4,128,128]{3,2,1,0:T(8,128)(2,1)S(1)}, u32[]{:S(2)}, u32[]{:S(2)}) async-start(bf16[16,4,128,128]{3,2,1,0:T(8,128)(2,1)} %bitcast.8), calls=%async_computation.1 | async-start | bytes 4194304 | tf_op jit(solution)/shard_map/all_to_all | solution.py:180
  19.9 0.0 copy-done
  19.9 0.6 choose.1
  20.5 36.7 %all_gather.15.own_ref = bf16[24,128,128]{2,1,0:T(8,128)(2,1)S(1)} all-gather(bf16[2,128,128]{2,1,0:T(8,128)(2,1)S(1)} %choose.1), channel_id=1, replica_groups={{0,9,16,25,32,41,48,57,64,73,80,89},{1,8,17,24,33,40,49,56,65,72,81,88}..., dimensions={0}, use_global_device_ids=true | all-gather | bytes 851968 | tf_op jit(solution)/shard_map/all_gather | solution.py:176
  57.2 1.9 %collective-permute-start = (bf16[24,128,128]{2,1,0:T(8,128)(2,1)S(1)}, bf16[24,128,128]{2,1,0:T(8,128)(2,1)S(1)}, u32[]{:S(2)}, u32[]{:S(2)}) collective-permute-start(bf16[24,128,128]{2,1,0:T(8,128)(2,1)S(1)} %all_gather.15.own_ref), channel_id=1, source_target_pairs={{0,1},{1,0},{2,3},{3,2},{4,5},{5,4},{6,7},{7,6},{8,9},{9,8},{10,11... | collective-permute-start | bytes 2359304 | tf_op jit(solution)/shard_map/ppermute | solution.py:185
  59.2 2.3 %collective-permute-done.other_ref = bf16[24,128,128]{2,1,0:T(8,128)(2,1)S(1)} collective-permute-done((bf16[24,128,128]{2,1,0:T(8,128)(2,1)S(1)}, bf16[24,128,128]{2,1,0:T(8,128)(2,1)S(1)}, u32[]{:S(2)}, u32[]{:S(2)}) %collective-permute-start) | collective-permute-done | bytes 786464 | tf_op jit(solution)/shard_map/ppermute | solution.py:185
  61.4 2.2 %pick.1 = (bf16[128,4096]{1,0:T(8,128)(2,1)S(1)}, s32[32]{0:T(128)S(1)}) custom-call(s32[8,96]{1,0:T(8,128)S(1)} %copy-done, bf16[24,128,128]{2,1,0:T(8,128)(2,1)S(1)} %all_gather.15.own_ref, bf16[24,128,128]{2,1,0:T(8,128)(2,1)S(1)} %collective-permute-done.other_ref), custom_call_target="tpu_custom_call" | custom-call | tf_op jit(solution)/shard_map/pick/pallas_call | solution.py:164
  63.6 0.7 all-to-all-done.1
  64.4 1.1 multiply.1
  65.5 7.3 %all_gather.16.both_ref = f32[2,128,128]{2,1,0:T(8,128)S(1)} all-gather(f32[1,128,128]{2,1,0:T(8,128)S(1)} %get-tuple-element.20), channel_id=1, replica_groups={{0,2},{1,3},{4,6},{5,7},{8,10},{9,11},{12,14},{13,15},{16,18},{17,19},{..., dimensions={0}, use_global_device_ids=true | all-gather | bytes 196608 | tf_op jit(solution)/shard_map/all_gather | solution.py:176
  72.8 4.3 %all_gather.17 = bf16[2,128,128]{2,1,0:T(8,128)(2,1)S(1)} all-gather(bf16[1,128,128]{2,1,0:T(8,128)(2,1)S(1)} %get-tuple-element.21), channel_id=1, replica_groups={{0,4},{1,5},{2,6},{3,7},{8,12},{9,13},{10,14},{11,15},{16,20},{17,21},{..., dimensions={0}, use_global_device_ids=true | all-gather | bytes 98304 | tf_op jit(solution)/shard_map/all_gather | solution.py:176
  77.2 41.7 %all_gather.18.own_ref = bf16[24,128,128]{2,1,0:T(8,128)(2,1)S(1)} all-gather(bf16[2,128,128]{2,1,0:T(8,128)(2,1)S(1)} %all_gather.17), channel_id=1, replica_groups={{0,9,16,25,32,41,48,57,64,73,80,89},{1,8,17,24,33,40,49,56,65,72,81,88}..., dimensions={0}, use_global_device_ids=true | all-gather | bytes 851968 | tf_op jit(solution)/shard_map/all_gather | solution.py:176
  118.9 1.9 %collective-permute-start.1 = (bf16[24,128,128]{2,1,0:T(8,128)(2,1)S(1)}, bf16[24,128,128]{2,1,0:T(8,128)(2,1)S(1)}, u32[]{:S(2)}, u32[]{:S(2)}) collective-permute-start(bf16[24,128,128]{2,1,0:T(8,128)(2,1)S(1)} %all_gather.18.own_ref), channel_id=1, source_target_pairs={{0,1},{1,0},{2,3},{3,2},{4,5},{5,4},{6,7},{7,6},{8,9},{9,8},{10,11... | collective-permute-start | bytes 2359304 | tf_op jit(solution)/shard_map/ppermute | solution.py:185
  120.8 2.2 %collective-permute-done.1.other_ref = bf16[24,128,128]{2,1,0:T(8,128)(2,1)S(1)} collective-permute-done((bf16[24,128,128]{2,1,0:T(8,128)(2,1)S(1)}, bf16[24,128,128]{2,1,0:T(8,128)(2,1)S(1)}, u32[]{:S(2)}, u32[]{:S(2)}) %collective-permute-start.1) | collective-permute-done | bytes 786464 | tf_op jit(solution)/shard_map/ppermute | solution.py:185
  123.0 1.2 partials.1
  124.3 4.2 %all_gather.19.both_ref = f32[2,128,128]{2,1,0:T(8,128)S(1)} all-gather(f32[1,128,128]{2,1,0:T(8,128)S(1)} %get-tuple-element.23), channel_id=1, replica_groups={{0,2},{1,3},{4,6},{5,7},{8,10},{9,11},{12,14},{13,15},{16,18},{17,19},{..., dimensions={0}, use_global_device_ids=true | all-gather | bytes 196608 | tf_op jit(solution)/shard_map/all_gather | solution.py:176
  128.5 1.2 final.1
  (1 shorter events, 0.0 us)
Async XLA Ops:
  0.0 0.8 copy-start.1
  1.4 10.2 %all-to-all-start = ((bf16[4,128,128]{2,1,0:T(8,128)(2,1)}), bf16[4,128,128]{2,1,0:T(8,128)(2,1)S(1)}, u32[]{:S(2)}, u32[]{:S(2)}) async-start(bf16[4,128,128]{2,1,0:T(8,128)(2,1)} %copies.1), calls=%async_computation | async-start | bytes 262144 | tf_op jit(solution)/shard_map/all_to_all | solution.py:180
  11.6 8.3 %copy-start = (s32[8,96]{1,0:T(8,128)S(1)}, s32[8,96]{1,0:T(8,128)}, u32[]{:S(2)}) copy-start(s32[8,96]{1,0:T(8,128)} %cols_ref.11) | copy-start | bytes 9220
  11.6 52.8 %all-to-all-start.1 = ((bf16[16,4,128,128]{3,2,1,0:T(8,128)(2,1)}), bf16[16,4,128,128]{3,2,1,0:T(8,128)(2,1)S(1)}, u32[]{:S(2)}, u32[]{:S(2)}) async-start(bf16[16,4,128,128]{3,2,1,0:T(8,128)(2,1)} %bitcast.8), calls=%async_computation.1 | async-start | bytes 4194304 | tf_op jit(solution)/shard_map/all_to_all | solution.py:180
  57.2 4.2 %collective-permute-start = (bf16[24,128,128]{2,1,0:T(8,128)(2,1)S(1)}, bf16[24,128,128]{2,1,0:T(8,128)(2,1)S(1)}, u32[]{:S(2)}, u32[]{:S(2)}) collective-permute-start(bf16[24,128,128]{2,1,0:T(8,128)(2,1)S(1)} %all_gather.15.own_ref), channel_id=1, source_target_pairs={{0,1},{1,0},{2,3},{3,2},{4,5},{5,4},{6,7},{7,6},{8,9},{9,8},{10,11... | collective-permute-start | bytes 2359304 | tf_op jit(solution)/shard_map/ppermute | solution.py:185
  118.9 4.2 %collective-permute-start.1 = (bf16[24,128,128]{2,1,0:T(8,128)(2,1)S(1)}, bf16[24,128,128]{2,1,0:T(8,128)(2,1)S(1)}, u32[]{:S(2)}, u32[]{:S(2)}) collective-permute-start(bf16[24,128,128]{2,1,0:T(8,128)(2,1)S(1)} %all_gather.18.own_ref), channel_id=1, source_target_pairs={{0,1},{1,0},{2,3},{3,2},{4,5},{5,4},{6,7},{7,6},{8,9},{9,8},{10,11... | collective-permute-start | bytes 2359304 | tf_op jit(solution)/shard_map/ppermute | solution.py:185

commit v12 on v11

--- a/solution.py
+++ b/solution.py
@@ -22,7 +22,6 @@
 
 
 Y_LINES = [[col_of(z, y, c) for y in range(Y)] for z in range(Z) for c in range(C)]
-Y_FAR = [[col_of(z, 2 * h + p, c) for h in range(2)] for z in range(Z) for p in range(2) for c in range(C)]
 Y_NEAR = [[col_of(z, 2 * h + p, c) for p in range(2)] for z in range(Z) for h in range(2) for c in range(C)]
 Z_LINES = [[col_of(z, y, (z + c) % C) for z in range(Z)] for y in range(Y) for c in range(C)]
 SWAP = [(s, s ^ 1) for s in range(N_COL)]
@@ -132,24 +131,24 @@
     left_ref[...] = picked(picks_ref, own_ref, other_ref)
 
 
-def share(keep_ref, send_ref, shares):
+def multiply_kernel(cols_ref, left_ref, m_ref, out_ref):
+    shares = multiply(cols_ref, left_ref[...], m_ref)
+    for y in range(Y):
+        out_ref[y] = shares[y % 2]
+
+
+def partial_kernel(cols_ref, picks_ref, own_ref, other_ref, m_ref, keep_ref, send_ref):
+    shares = multiply(cols_ref, picked(picks_ref, own_ref, other_ref), m_ref)
     near = place()[3]
     keep_ref[...] = jnp.where(near == 0, *shares)
-    send_ref[0] = jnp.where(near == 0, *shares[::-1])
-
-
-def multiply_kernel(cols_ref, left_ref, m_ref, keep_ref, send_ref):
-    share(keep_ref, send_ref, multiply(cols_ref, left_ref[...], m_ref))
-
-
-def partial_kernel(cols_ref, picks_ref, own_ref, other_ref, m_ref, keep_ref, send_ref):
-    share(keep_ref, send_ref, multiply(cols_ref, picked(picks_ref, own_ref, other_ref), m_ref))
-
-
-def square_kernel(keep_ref, both_ref, square_ref, half_ref):
-    total = keep_ref[...] + both_ref[1 - place()[3]]
-    square_ref[...] = total
-    half_ref[0] = total.astype(half_ref.dtype)
+    send_ref[...] = jnp.where(near == 0, *shares[::-1])
+
+
+def square_kernel(shares_ref, square_ref, half_ref):
+    h = lax.rem(lax.axis_index("col") // (2 * C), 2)
+    square_ref[...] = shares_ref[2 * h] + shares_ref[2 * h + 1]
+    for pair in range(2):
+        half_ref[pair] = (shares_ref[2 * pair] + shares_ref[2 * pair + 1]).astype(half_ref.dtype)
 
 
 def final_kernel(cols_ref, keep_ref, both_ref, square_ref, out_ref):
@@ -189,7 +188,7 @@
     block, cols = (BS, BS), (win_cols,)
     lists = dict(scratch_shapes=[pltpu.SMEM((CLASS + 1,), jnp.int32)])
     flops = lambda count: pl.CostEstimate(flops=count * BS**3, bytes_accessed=4 << 20, transcendentals=0)
-    shares = [(block, jnp.float32), ((1,) + block, jnp.float32)]
+    shares = [(block, jnp.float32)] * 2
 
     packed = pack(win_cols, couple_vals[0, 0])
     (line,) = call(copies_kernel, "copies", [((Y,) + block, jnp.bfloat16)], (win_vals[0],))
@@ -200,16 +199,17 @@
     (line,) = call(choose_kernel, "choose", [((2,) + block, jnp.bfloat16)], (line,), cols)
     outs = [((BS, BANDS * CLASS * BS), jnp.bfloat16), ((BANDS * CLASS,), jnp.int32)]
     left, picks = call(pick_kernel, "pick", outs, lines(line), cols, 8, **lists)
-    keep, send = call(multiply_kernel, "multiply", shares, (left, held), cols, 16, cost_estimate=flops(128))
-
-    outs = [(block, jnp.float32), ((1,) + block, jnp.bfloat16)]
-    square, half = call(square_kernel, "square", outs, (keep, gather(send, Y_NEAR)))
-
-    line = lines(gather(half, Y_FAR))
+    outs = [((Y,) + block, jnp.float32)]
+    (sums,) = call(multiply_kernel, "multiply", outs, (left, held), cols, 16, cost_estimate=flops(128))
+
+    outs = [(block, jnp.float32), ((2,) + block, jnp.bfloat16)]
+    square, half = call(square_kernel, "square", outs, (exchange(sums, "col", Y_LINES),))
+
+    line = lines(half)
     scalars = (win_cols, picks)
     keep, send = call(partial_kernel, "partials", shares, (*line, held), scalars, 16, cost_estimate=flops(128))
     outs = [(block, jnp.bfloat16)]
-    (purified,) = call(final_kernel, "final", outs, (keep, gather(send, Y_NEAR), square), cols)
+    (purified,) = call(final_kernel, "final", outs, (keep, gather(send[None], Y_NEAR), square), cols)
     return purified[None, None]
 
 

time: 130 us -> 129 us (level)
    all_gather x5 -> x3, blocking collectives: 94.3 us -> 80.5 us  [gather(): lax.all_gather(value, 'col', axis=0, tiled=True, axis_index_groups=groups)]
    all_to_all x0 -> x1, blocking collectives: none -> 12.9 us  [exchange(): lax.all_to_all(value, axis, split_axis=0, concat_axis=0, tiled=True, axis...]
where the time goes in v12:
time: 129 us
  blocking collectives  93.4 us (72%)
  starting transfers between devices  17.5 us (14%)
  Pallas kernels  10.6 us (8%)
  waiting for transfers between devices  6.47 us (5%)
    all_gather x3, blocking collectives, gather(): lax.all_gather(value, 'col', axis=0, tiled=True, axis_index_groups=groups)  80.5 us
    all_to_all x2, starting transfers between devices, exchange(): lax.all_to_all(value, axis, split_axis=0, concat_axis=0, tiled=True, axis...  13.7 us
    all_to_all x1, blocking collectives, exchange(): lax.all_to_all(value, axis, split_axis=0, concat_axis=0, tiled=True, axis...  12.9 us
    pallas_call x7, Pallas kernels, call(): pl.pallas_call(kernel, out_shape=[jax.ShapeDtypeStruct(shape, dtype) for...  7.11 us
    ppermute x2, waiting for transfers between devices, lines(): return (own, lax.ppermute(own, 'col', SWAP))  4.5 us
    ppermute x2, starting transfers between devices, lines(): return (own, lax.ppermute(own, 'col', SWAP))  3.82 us
    pallas_call x1, Pallas kernels, pack(): pl.pallas_call(pack_kernel, out_shape=jax.ShapeDtypeStruct((2, BANDS, CLA...  3.53 us
  transfers between devices with their start and end apart: 4, of which 4 were waited for; matrix products, arithmetic and copies ran while one was open for 0% of the time, Pallas kernels for 5%

profile of v12, /device:TPU:1, one launch (start us, length us, event | category | flops | bytes accessed | tf_op | source)
XLA Modules:
  0.0 128.8 jit_solution(11560504342164488137)
XLA Ops:
  0.0 0.0 copy-start.1
  0.0 0.8 copy-done.1
  0.8 0.7 copies.1
  1.4 5.4 %all-to-all-start = ((bf16[4,128,128]{2,1,0:T(8,128)(2,1)}), bf16[4,128,128]{2,1,0:T(8,128)(2,1)S(1)}, u32[]{:S(2)}, u32[]{:S(2)}) async-start(bf16[4,128,128]{2,1,0:T(8,128)(2,1)} %copies.1), calls=%async_computation | async-start | bytes 262144 | tf_op jit(solution)/shard_map/all_to_all | solution.py:179
  6.8 3.5 %pack.1 = bf16[2,8,4,128,128]{4,3,2,1,0:T(8,128)(2,1)} custom-call(s32[8,96]{1,0:T(8,128)} %cols_ref.11, bf16[8,12,128,128]{3,2,1,0:T(8,128)(2,1)} %bitcast.11), custom_call_target="tpu_custom_call" | custom-call | bytes 5242880 | tf_op jit(solution)/shard_map/pack/pallas_call | solution.py:70
  10.4 1.2 all-to-all-done.line_ref
  11.6 0.0 copy-start
  11.6 8.3 %all-to-all-start.1 = ((bf16[16,4,128,128]{3,2,1,0:T(8,128)(2,1)}), bf16[16,4,128,128]{3,2,1,0:T(8,128)(2,1)S(1)}, u32[]{:S(2)}, u32[]{:S(2)}) async-start(bf16[16,4,128,128]{3,2,1,0:T(8,128)(2,1)} %bitcast.10), calls=%async_computation.1 | async-start | bytes 4194304 | tf_op jit(solution)/shard_map/all_to_all | solution.py:179
  19.9 0.0 copy-done
  19.9 0.6 choose.1
  20.5 36.7 %all_gather.9.own_ref = bf16[24,128,128]{2,1,0:T(8,128)(2,1)S(1)} all-gather(bf16[2,128,128]{2,1,0:T(8,128)(2,1)S(1)} %choose.1), channel_id=1, replica_groups={{0,9,16,25,32,41,48,57,64,73,80,89},{1,8,17,24,33,40,49,56,65,72,81,88}..., dimensions={0}, use_global_device_ids=true | all-gather | bytes 851968 | tf_op jit(solution)/shard_map/all_gather | solution.py:175
  57.2 1.9 %collective-permute-start = (bf16[24,128,128]{2,1,0:T(8,128)(2,1)S(1)}, bf16[24,128,128]{2,1,0:T(8,128)(2,1)S(1)}, u32[]{:S(2)}, u32[]{:S(2)}) collective-permute-start(bf16[24,128,128]{2,1,0:T(8,128)(2,1)S(1)} %all_gather.9.own_ref), channel_id=1, source_target_pairs={{0,1},{1,0},{2,3},{3,2},{4,5},{5,4},{6,7},{7,6},{8,9},{9,8},{10,11... | collective-permute-start | bytes 2359304 | tf_op jit(solution)/shard_map/ppermute | solution.py:184
  59.2 2.3 %collective-permute-done.other_ref = bf16[24,128,128]{2,1,0:T(8,128)(2,1)S(1)} collective-permute-done((bf16[24,128,128]{2,1,0:T(8,128)(2,1)S(1)}, bf16[24,128,128]{2,1,0:T(8,128)(2,1)S(1)}, u32[]{:S(2)}, u32[]{:S(2)}) %collective-permute-start) | collective-permute-done | bytes 786464 | tf_op jit(solution)/shard_map/ppermute | solution.py:184
  61.4 2.2 %pick.1 = (bf16[128,4096]{1,0:T(8,128)(2,1)S(1)}, s32[32]{0:T(128)S(1)}) custom-call(s32[8,96]{1,0:T(8,128)S(1)} %copy-done, bf16[24,128,128]{2,1,0:T(8,128)(2,1)S(1)} %all_gather.9.own_ref, bf16[24,128,128]{2,1,0:T(8,128)(2,1)S(1)} %collective-permute-done.other_ref), custom_call_target="tpu_custom_call" | custom-call | tf_op jit(solution)/shard_map/pick/pallas_call | solution.py:163
  63.6 0.7 all-to-all-done.1
  64.4 1.1 multiply.1
  65.5 12.9 %all_to_all.15.shares_ref = f32[4,128,128]{2,1,0:T(8,128)S(1)} all-to-all(f32[4,128,128]{2,1,0:T(8,128)S(1)} %multiply.1), channel_id=1, replica_groups={{0,2,4,6},{1,3,5,7},{8,10,12,14},{9,11,13,15},{16,18,20,22},{17,19,21,2..., dimensions={0} | all-to-all | bytes 524288 | tf_op jit(solution)/shard_map/all_to_all | solution.py:179
  78.4 39.6 %all_gather.10.own_ref = bf16[24,128,128]{2,1,0:T(8,128)(2,1)S(1)} all-gather(bf16[2,128,128]{2,1,0:T(8,128)(2,1)S(1)} %get-tuple-element.17), channel_id=1, replica_groups={{0,9,16,25,32,41,48,57,64,73,80,89},{1,8,17,24,33,40,49,56,65,72,81,88}..., dimensions={0}, use_global_device_ids=true | all-gather | bytes 851968 | tf_op jit(solution)/shard_map/all_gather | solution.py:175
  118.0 1.9 %collective-permute-start.1 = (bf16[24,128,128]{2,1,0:T(8,128)(2,1)S(1)}, bf16[24,128,128]{2,1,0:T(8,128)(2,1)S(1)}, u32[]{:S(2)}, u32[]{:S(2)}) collective-permute-start(bf16[24,128,128]{2,1,0:T(8,128)(2,1)S(1)} %all_gather.10.own_ref), channel_id=1, source_target_pairs={{0,1},{1,0},{2,3},{3,2},{4,5},{5,4},{6,7},{7,6},{8,9},{9,8},{10,11... | collective-permute-start | bytes 2359304 | tf_op jit(solution)/shard_map/ppermute | solution.py:184
  119.9 2.2 %collective-permute-done.1.other_ref = bf16[24,128,128]{2,1,0:T(8,128)(2,1)S(1)} collective-permute-done((bf16[24,128,128]{2,1,0:T(8,128)(2,1)S(1)}, bf16[24,128,128]{2,1,0:T(8,128)(2,1)S(1)}, u32[]{:S(2)}, u32[]{:S(2)}) %collective-permute-start.1) | collective-permute-done | bytes 786464 | tf_op jit(solution)/shard_map/ppermute | solution.py:184
  122.2 1.2 partials.1
  123.4 4.2 %all-gather = f32[256,128]{1,0:T(8,128)S(1)} all-gather(f32[128,128]{1,0:T(8,128)S(1)} %get-tuple-element.19), channel_id=2, replica_groups={{0,2},{1,3},{4,6},{5,7},{8,10},{9,11},{12,14},{13,15},{16,18},{17,19},{..., dimensions={0}, use_global_device_ids=true | all-gather | bytes 196608 | tf_op jit(solution)/shard_map/all_gather | solution.py:175
  127.6 1.2 final.1
  (1 shorter events, 0.0 us)
Async XLA Ops:
  0.0 0.8 copy-start.1
  1.4 10.2 %all-to-all-start = ((bf16[4,128,128]{2,1,0:T(8,128)(2,1)}), bf16[4,128,128]{2,1,0:T(8,128)(2,1)S(1)}, u32[]{:S(2)}, u32[]{:S(2)}) async-start(bf16[4,128,128]{2,1,0:T(8,128)(2,1)} %copies.1), calls=%async_computation | async-start | bytes 262144 | tf_op jit(solution)/shard_map/all_to_all | solution.py:179
  11.6 8.3 %copy-start = (s32[8,96]{1,0:T(8,128)S(1)}, s32[8,96]{1,0:T(8,128)}, u32[]{:S(2)}) copy-start(s32[8,96]{1,0:T(8,128)} %cols_ref.11) | copy-start | bytes 9220
  11.6 52.8 %all-to-all-start.1 = ((bf16[16,4,128,128]{3,2,1,0:T(8,128)(2,1)}), bf16[16,4,128,128]{3,2,1,0:T(8,128)(2,1)S(1)}, u32[]{:S(2)}, u32[]{:S(2)}) async-start(bf16[16,4,128,128]{3,2,1,0:T(8,128)(2,1)} %bitcast.10), calls=%async_computation.1 | async-start | bytes 4194304 | tf_op jit(solution)/shard_map/all_to_all | solution.py:179
  57.2 4.2 %collective-permute-start = (bf16[24,128,128]{2,1,0:T(8,128)(2,1)S(1)}, bf16[24,128,128]{2,1,0:T(8,128)(2,1)S(1)}, u32[]{:S(2)}, u32[]{:S(2)}) collective-permute-start(bf16[24,128,128]{2,1,0:T(8,128)(2,1)S(1)} %all_gather.9.own_ref), channel_id=1, source_target_pairs={{0,1},{1,0},{2,3},{3,2},{4,5},{5,4},{6,7},{7,6},{8,9},{9,8},{10,11... | collective-permute-start | bytes 2359304 | tf_op jit(solution)/shard_map/ppermute | solution.py:184
  118.0 4.2 %collective-permute-start.1 = (bf16[24,128,128]{2,1,0:T(8,128)(2,1)S(1)}, bf16[24,128,128]{2,1,0:T(8,128)(2,1)S(1)}, u32[]{:S(2)}, u32[]{:S(2)}) collective-permute-start(bf16[24,128,128]{2,1,0:T(8,128)(2,1)S(1)} %all_gather.10.own_ref), channel_id=1, source_target_pairs={{0,1},{1,0},{2,3},{3,2},{4,5},{5,4},{6,7},{7,6},{8,9},{9,8},{10,11... | collective-permute-start | bytes 2359304 | tf_op jit(solution)/shard_map/ppermute | solution.py:184

commit v13 on v12

--- a/solution.py
+++ b/solution.py
@@ -54,16 +54,30 @@
     return count
 
 
+def list_both(cols_ref, lists, window, band):
+    counts, singles = [jnp.int32(0)] * 2, jnp.int32(0)
+    for n in range(GROUP // 2):
+        quad, core = divmod(n, C)
+        slot = quad * 4 + core
+        alive = [a.astype(jnp.int32) for a in pair_alive(cols_ref, window, band * GROUP + slot)]
+        both, single = alive[0] & alive[1], alive[0] ^ alive[1]
+        lists[0, jnp.minimum(counts[0], CLASS)] = slot + C * (1 - alive[0])
+        lists[1, jnp.minimum(counts[1], CLASS)] = slot + C * alive[1]
+        odd = singles & 1
+        counts[0] = counts[0] + (both | (single & (1 - odd)))
+        counts[1] = counts[1] + (both | (single & odd))
+        singles = singles + single
+    return counts
+
+
 def pack_kernel(cols_ref, couple_ref, out_ref, lists):
     band = lax.axis_index("row")
     for i in range(STEP):
+        slots = lists.at[i]
+        counts = list_both(cols_ref, slots, pl.program_id(0) * STEP + i, band)
         for k in range(2):
-            slots = lists.at[i * 2 + k]
-            count = list_live(
-                cols_ref, slots, pl.program_id(0) * STEP + i, band, k, lambda quad, core, p: quad * 4 + p * C + core
-            )
             for j in range(CLASS):
-                out_ref[k, i, j] = couple_ref[i, jnp.where(j < count, slots[j], 0)]
+                out_ref[k, i, j] = couple_ref[i, jnp.where(j < counts[k], slots[k, j], 0)]
 
 
 def pack(win_cols, couple):
@@ -76,7 +90,7 @@
             pl.BlockSpec((STEP, GROUP, BS, BS), lambda i: (i, 0, 0, 0)),
         ],
         out_specs=pl.BlockSpec((2, STEP, CLASS, BS, BS), lambda i: (0, i, 0, 0, 0)),
-        scratch_shapes=[pltpu.SMEM((2 * STEP, CLASS + 1), jnp.int32)],
+        scratch_shapes=[pltpu.SMEM((STEP, 2, CLASS + 1), jnp.int32)],
         cost_estimate=pl.CostEstimate(flops=0, bytes_accessed=5 << 20, transcendentals=0),
         compiler_params=pltpu.CompilerParams(vmem_limit_bytes=56 << 20),
         name="pack",
@@ -126,7 +140,10 @@
     return product[:, :BS], product[:, BS:]
 
 
-def pick_kernel(cols_ref, own_ref, other_ref, left_ref, picks_ref, list_ref):
+def pick_kernel(cols_ref, own_ref, other_ref, left_ref, weights_ref, picks_ref, list_ref):
+    near = place()[3]
+    for p in range(2):
+        weights_ref[p] = jnp.full((1, BS), (near != p).astype(jnp.float32))
     list_picks(cols_ref, list_ref, picks_ref)
     left_ref[...] = picked(picks_ref, own_ref, other_ref)
 
@@ -139,23 +156,20 @@
 
 def partial_kernel(cols_ref, picks_ref, own_ref, other_ref, m_ref, keep_ref, send_ref):
     shares = multiply(cols_ref, picked(picks_ref, own_ref, other_ref), m_ref)
-    near = place()[3]
-    keep_ref[...] = jnp.where(near == 0, *shares)
-    send_ref[...] = jnp.where(near == 0, *shares[::-1])
-
-
-def square_kernel(shares_ref, square_ref, half_ref):
-    h = lax.rem(lax.axis_index("col") // (2 * C), 2)
-    square_ref[...] = shares_ref[2 * h] + shares_ref[2 * h + 1]
+    row, col, _, near = place()
+    keep = jnp.where(near == 0, *shares)
+    send = jnp.where(near == 0, *shares[::-1])
+    keep_ref[...] = jnp.where(cols_ref[row, col] >= 0, keep, 0.0)
+    send_ref[0] = jnp.where(cols_ref[row, col ^ C] >= 0, send, 0.0)
+
+
+def square_kernel(cols_ref, shares_ref, square_ref, half_ref):
+    row, col, _, _ = place()
+    h = lax.rem(col // (2 * C), 2)
+    total = shares_ref[2 * h] + shares_ref[2 * h + 1]
+    square_ref[...] = jnp.where(cols_ref[row, col] >= 0, total, 0.0)
     for pair in range(2):
         half_ref[pair] = (shares_ref[2 * pair] + shares_ref[2 * pair + 1]).astype(half_ref.dtype)
-
-
-def final_kernel(cols_ref, keep_ref, both_ref, square_ref, out_ref):
-    row, col, _, near = place()
-    cube = keep_ref[...] + both_ref[1 - near]
-    alive = cols_ref[row, col] >= 0
-    out_ref[...] = jnp.where(alive, 3.0 * square_ref[...] - 2.0 * cube, 0.0).astype(out_ref.dtype)
 
 
 def call(kernel, name, outs, arrays, scalars=(), grant=4, **options):
@@ -188,7 +202,7 @@
     block, cols = (BS, BS), (win_cols,)
     lists = dict(scratch_shapes=[pltpu.SMEM((CLASS + 1,), jnp.int32)])
     flops = lambda count: pl.CostEstimate(flops=count * BS**3, bytes_accessed=4 << 20, transcendentals=0)
-    shares = [(block, jnp.float32)] * 2
+    shares = [(block, jnp.float32), ((1,) + block, jnp.float32)]
 
     packed = pack(win_cols, couple_vals[0, 0])
     (line,) = call(copies_kernel, "copies", [((Y,) + block, jnp.bfloat16)], (win_vals[0],))
@@ -197,20 +211,20 @@
     held = exchange(packed.reshape((2 * BANDS, CLASS) + block), ("row", "col"), SPREAD)
     held = held.reshape(2, BANDS * CLASS * BS, BS)
     (line,) = call(choose_kernel, "choose", [((2,) + block, jnp.bfloat16)], (line,), cols)
-    outs = [((BS, BANDS * CLASS * BS), jnp.bfloat16), ((BANDS * CLASS,), jnp.int32)]
-    left, picks = call(pick_kernel, "pick", outs, lines(line), cols, 8, **lists)
+    outs = [((BS, BANDS * CLASS * BS), jnp.bfloat16), ((2, 1, BS), jnp.float32), ((BANDS * CLASS,), jnp.int32)]
+    left, weights, picks = call(pick_kernel, "pick", outs, lines(line), cols, 8, **lists)
     outs = [((Y,) + block, jnp.float32)]
     (sums,) = call(multiply_kernel, "multiply", outs, (left, held), cols, 16, cost_estimate=flops(128))
 
     outs = [(block, jnp.float32), ((2,) + block, jnp.bfloat16)]
-    square, half = call(square_kernel, "square", outs, (exchange(sums, "col", Y_LINES),))
+    square, half = call(square_kernel, "square", outs, (exchange(sums, "col", Y_LINES),), cols)
 
     line = lines(half)
     scalars = (win_cols, picks)
     keep, send = call(partial_kernel, "partials", shares, (*line, held), scalars, 16, cost_estimate=flops(128))
-    outs = [(block, jnp.bfloat16)]
-    (purified,) = call(final_kernel, "final", outs, (keep, gather(send[None], Y_NEAR), square), cols)
-    return purified[None, None]
+    both = gather(send, Y_NEAR)
+    cube = keep + weights[0] * both[0] + weights[1] * both[1]
+    return (3.0 * square - 2.0 * cube).astype(jnp.bfloat16)[None, None]
 
 
 def solution(mesh):

time: 129 us -> 129 us (level)
    pallas_call x7 -> x6, Pallas kernels: 7.11 us -> 6.47 us  [call(): pl.pallas_call(kernel, out_shape=[jax.ShapeDtypeStruct(shape, dtype) for...]
where the time goes in v13:
time: 129 us
  blocking collectives  93.4 us (72%)
  starting transfers between devices  17.5 us (14%)
  Pallas kernels  9.75 us (8%)
  waiting for transfers between devices  6.71 us (5%)
    all_gather x3, blocking collectives, gather(): lax.all_gather(value, 'col', axis=0, tiled=True, axis_index_groups=groups)  80.5 us
    all_to_all x2, starting transfers between devices, exchange(): lax.all_to_all(value, axis, split_axis=0, concat_axis=0, tiled=True, axis...  13.7 us
    all_to_all x1, blocking collectives, exchange(): lax.all_to_all(value, axis, split_axis=0, concat_axis=0, tiled=True, axis...  12.9 us
    pallas_call x6, Pallas kernels, call(): pl.pallas_call(kernel, out_shape=[jax.ShapeDtypeStruct(shape, dtype) for...  6.47 us
    ppermute x2, waiting for transfers between devices, lines(): return (own, lax.ppermute(own, 'col', SWAP))  4.49 us
    ppermute x2, starting transfers between devices, lines(): return (own, lax.ppermute(own, 'col', SWAP))  3.82 us
    pallas_call x1, Pallas kernels, pack(): pl.pallas_call(pack_kernel, out_shape=jax.ShapeDtypeStruct((2, BANDS, CLA...  3.28 us
  transfers between devices with their start and end apart: 4, of which 4 were waited for; matrix products, arithmetic and copies ran while one was open for 0% of the time, Pallas kernels for 5%

profile of v13, /device:TPU:1, one launch (start us, length us, event | category | flops | bytes accessed | tf_op | source)
XLA Modules:
  0.0 128.8 jit_solution(1715262862107939969)
XLA Ops:
  0.0 0.0 copy-start.1
  0.0 0.8 copy-done.1
  0.8 0.7 copies.1
  1.4 5.4 %all-to-all-start = ((bf16[4,128,128]{2,1,0:T(8,128)(2,1)}), bf16[4,128,128]{2,1,0:T(8,128)(2,1)S(1)}, u32[]{:S(2)}, u32[]{:S(2)}) async-start(bf16[4,128,128]{2,1,0:T(8,128)(2,1)} %copies.1), calls=%async_computation | async-start | bytes 262144 | tf_op jit(solution)/shard_map/all_to_all | solution.py:193
  6.8 3.3 %pack.1 = bf16[2,8,4,128,128]{4,3,2,1,0:T(8,128)(2,1)} custom-call(s32[8,96]{1,0:T(8,128)} %cols_ref.11, bf16[8,12,128,128]{3,2,1,0:T(8,128)(2,1)} %bitcast.38), custom_call_target="tpu_custom_call" | custom-call | bytes 5242880 | tf_op jit(solution)/shard_map/pack/pallas_call | solution.py:84
  10.1 1.5 %all-to-all-done.line_ref = bf16[4,128,128]{2,1,0:T(8,128)(2,1)S(1)} async-done(((bf16[4,128,128]{2,1,0:T(8,128)(2,1)}), bf16[4,128,128]{2,1,0:T(8,128)(2,1)S(1)}, u32[]{:S(2)}, u32[]{:S(2)}) %all-to-all-start) | async-done | bytes 131104 | tf_op jit(solution)/shard_map/all_to_all | solution.py:193
  11.6 0.0 copy-start
  11.6 8.3 %all-to-all-start.1 = ((bf16[16,4,128,128]{3,2,1,0:T(8,128)(2,1)}), bf16[16,4,128,128]{3,2,1,0:T(8,128)(2,1)S(1)}, u32[]{:S(2)}, u32[]{:S(2)}) async-start(bf16[16,4,128,128]{3,2,1,0:T(8,128)(2,1)} %bitcast.37), calls=%async_computation.1 | async-start | bytes 4194304 | tf_op jit(solution)/shard_map/all_to_all | solution.py:193
  19.9 0.0 copy-done
  19.9 0.6 choose.1
  20.5 36.7 %all_gather.9.own_ref = bf16[24,128,128]{2,1,0:T(8,128)(2,1)S(1)} all-gather(bf16[2,128,128]{2,1,0:T(8,128)(2,1)S(1)} %choose.1), channel_id=1, replica_groups={{0,9,16,25,32,41,48,57,64,73,80,89},{1,8,17,24,33,40,49,56,65,72,81,88}..., dimensions={0}, use_global_device_ids=true | all-gather | bytes 851968 | tf_op jit(solution)/shard_map/all_gather | solution.py:189
  57.2 1.9 %collective-permute-start = (bf16[24,128,128]{2,1,0:T(8,128)(2,1)S(1)}, bf16[24,128,128]{2,1,0:T(8,128)(2,1)S(1)}, u32[]{:S(2)}, u32[]{:S(2)}) collective-permute-start(bf16[24,128,128]{2,1,0:T(8,128)(2,1)S(1)} %all_gather.9.own_ref), channel_id=1, source_target_pairs={{0,1},{1,0},{2,3},{3,2},{4,5},{5,4},{6,7},{7,6},{8,9},{9,8},{10,11... | collective-permute-start | bytes 2359304 | tf_op jit(solution)/shard_map/ppermute | solution.py:198
  59.2 2.3 %collective-permute-done.other_ref = bf16[24,128,128]{2,1,0:T(8,128)(2,1)S(1)} collective-permute-done((bf16[24,128,128]{2,1,0:T(8,128)(2,1)S(1)}, bf16[24,128,128]{2,1,0:T(8,128)(2,1)S(1)}, u32[]{:S(2)}, u32[]{:S(2)}) %collective-permute-start) | collective-permute-done | bytes 786464 | tf_op jit(solution)/shard_map/ppermute | solution.py:198
  61.4 2.2 %pick.1 = (bf16[128,4096]{1,0:T(8,128)(2,1)S(1)}, f32[2,1,128]{2,1,0:T(1,128)S(1)}, s32[32]{0:T(128)S(1)}) custom-call(s32[8,96]{1,0:T(8,128)S(1)} %copy-done, bf16[24,128,128]{2,1,0:T(8,128)(2,1)S(1)} %all_gather.9.own_ref, bf16[24,128,128]{2,1,0:T(8,128)(2,1)S(1)} %collective-permute-done.other_ref), custom_call_target="tpu_custom_call" | custom-call | tf_op jit(solution)/shard_map/pick/pallas_call | solution.py:177
  63.6 0.7 all-to-all-done.1
  64.4 1.1 multiply.1
  65.5 12.9 %all_to_all.15.shares_ref = f32[4,128,128]{2,1,0:T(8,128)S(1)} all-to-all(f32[4,128,128]{2,1,0:T(8,128)S(1)} %multiply.1), channel_id=1, replica_groups={{0,2,4,6},{1,3,5,7},{8,10,12,14},{9,11,13,15},{16,18,20,22},{17,19,21,2..., dimensions={0} | all-to-all | bytes 524288 | tf_op jit(solution)/shard_map/all_to_all | solution.py:193
  78.4 0.6 square.1
  79.0 39.6 %all_gather.10.own_ref = bf16[24,128,128]{2,1,0:T(8,128)(2,1)S(1)} all-gather(bf16[2,128,128]{2,1,0:T(8,128)(2,1)S(1)} %get-tuple-element.19), channel_id=1, replica_groups={{0,9,16,25,32,41,48,57,64,73,80,89},{1,8,17,24,33,40,49,56,65,72,81,88}..., dimensions={0}, use_global_device_ids=true | all-gather | bytes 851968 | tf_op jit(solution)/shard_map/all_gather | solution.py:189
  118.6 1.9 %collective-permute-start.1 = (bf16[24,128,128]{2,1,0:T(8,128)(2,1)S(1)}, bf16[24,128,128]{2,1,0:T(8,128)(2,1)S(1)}, u32[]{:S(2)}, u32[]{:S(2)}) collective-permute-start(bf16[24,128,128]{2,1,0:T(8,128)(2,1)S(1)} %all_gather.10.own_ref), channel_id=1, source_target_pairs={{0,1},{1,0},{2,3},{3,2},{4,5},{5,4},{6,7},{7,6},{8,9},{9,8},{10,11... | collective-permute-start | bytes 2359304 | tf_op jit(solution)/shard_map/ppermute | solution.py:198
  120.5 2.2 %collective-permute-done.1.other_ref = bf16[24,128,128]{2,1,0:T(8,128)(2,1)S(1)} collective-permute-done((bf16[24,128,128]{2,1,0:T(8,128)(2,1)S(1)}, bf16[24,128,128]{2,1,0:T(8,128)(2,1)S(1)}, u32[]{:S(2)}, u32[]{:S(2)}) %collective-permute-start.1) | collective-permute-done | bytes 786464 | tf_op jit(solution)/shard_map/ppermute | solution.py:198
  122.8 1.2 partials.1
  124.0 4.2 %all_gather.11 = f32[2,128,128]{2,1,0:T(8,128)S(1)} all-gather(f32[1,128,128]{2,1,0:T(8,128)S(1)} %get-tuple-element.22), channel_id=1, replica_groups={{0,2},{1,3},{4,6},{5,7},{8,10},{9,11},{12,14},{13,15},{16,18},{17,19},{..., dimensions={0}, use_global_device_ids=true | all-gather | bytes 196608 | tf_op jit(solution)/shard_map/all_gather | solution.py:189
  128.2 0.6 fusion.7
  (1 shorter events, 0.0 us)
Async XLA Ops:
  0.0 0.8 copy-start.1
  1.4 10.2 %all-to-all-start = ((bf16[4,128,128]{2,1,0:T(8,128)(2,1)}), bf16[4,128,128]{2,1,0:T(8,128)(2,1)S(1)}, u32[]{:S(2)}, u32[]{:S(2)}) async-start(bf16[4,128,128]{2,1,0:T(8,128)(2,1)} %copies.1), calls=%async_computation | async-start | bytes 262144 | tf_op jit(solution)/shard_map/all_to_all | solution.py:193
  11.6 8.3 %copy-start = (s32[8,96]{1,0:T(8,128)S(1)}, s32[8,96]{1,0:T(8,128)}, u32[]{:S(2)}) copy-start(s32[8,96]{1,0:T(8,128)} %cols_ref.11) | copy-start | bytes 9220
  11.6 52.8 %all-to-all-start.1 = ((bf16[16,4,128,128]{3,2,1,0:T(8,128)(2,1)}), bf16[16,4,128,128]{3,2,1,0:T(8,128)(2,1)S(1)}, u32[]{:S(2)}, u32[]{:S(2)}) async-start(bf16[16,4,128,128]{3,2,1,0:T(8,128)(2,1)} %bitcast.37), calls=%async_computation.1 | async-start | bytes 4194304 | tf_op jit(solution)/shard_map/all_to_all | solution.py:193
  57.2 4.2 %collective-permute-start = (bf16[24,128,128]{2,1,0:T(8,128)(2,1)S(1)}, bf16[24,128,128]{2,1,0:T(8,128)(2,1)S(1)}, u32[]{:S(2)}, u32[]{:S(2)}) collective-permute-start(bf16[24,128,128]{2,1,0:T(8,128)(2,1)S(1)} %all_gather.9.own_ref), channel_id=1, source_target_pairs={{0,1},{1,0},{2,3},{3,2},{4,5},{5,4},{6,7},{7,6},{8,9},{9,8},{10,11... | collective-permute-start | bytes 2359304 | tf_op jit(solution)/shard_map/ppermute | solution.py:198
  118.6 4.2 %collective-permute-start.1 = (bf16[24,128,128]{2,1,0:T(8,128)(2,1)S(1)}, bf16[24,128,128]{2,1,0:T(8,128)(2,1)S(1)}, u32[]{:S(2)}, u32[]{:S(2)}) collective-permute-start(bf16[24,128,128]{2,1,0:T(8,128)(2,1)S(1)} %all_gather.10.own_ref), channel_id=1, source_target_pairs={{0,1},{1,0},{2,3},{3,2},{4,5},{5,4},{6,7},{7,6},{8,9},{9,8},{10,11... | collective-permute-start | bytes 2359304 | tf_op jit(solution)/shard_map/ppermute | solution.py:198

commit v14 on v13

--- a/solution.py
+++ b/solution.py
@@ -23,7 +23,7 @@
 
 Y_LINES = [[col_of(z, y, c) for y in range(Y)] for z in range(Z) for c in range(C)]
 Y_NEAR = [[col_of(z, 2 * h + p, c) for p in range(2)] for z in range(Z) for h in range(2) for c in range(C)]
-Z_LINES = [[col_of(z, y, (z + c) % C) for z in range(Z)] for y in range(Y) for c in range(C)]
+Z_LINES = [[col_of(z, y, (2 * z // Z + c) % C) for z in range(Z)] for y in range(Y) for c in range(C)]
 SWAP = [(s, s ^ 1) for s in range(N_COL)]
 SPREAD = [[row * N_COL + col for col in pair for row in range(BANDS)] for pair in Y_NEAR]
 
@@ -112,10 +112,10 @@
 
 def list_picks(cols_ref, list_ref, picks_ref):
     row, col, core, near = place()
-    line = lax.rem(col // (Y * C) + core, 2)
+    line = lax.rem(col // (N_COL // 2) + core, 2)
     for band in range(BANDS):
         where = lambda quad, c, _, band=band: (
-            band * 3 + quad + QUADS * lax.rem(line + c + (band * 3 + quad) // 2, 2)
+            band * 3 + quad + QUADS * lax.rem(line + c + 2 * (band * 3 + quad) // QUADS, 2)
         )
         count = list_live(cols_ref, list_ref, row, band, near, where)
         for j in range(CLASS):

time: 129 us -> 129 us (level)
    all_gather x3, blocking collectives: 80.5 us -> 82 us  [gather(): lax.all_gather(value, 'col', axis=0, tiled=True, axis_index_groups=groups)]
  transfers between devices with their start and end apart: 4 -> 4, of which waited for: 4 -> 3; matrix products, arithmetic and copies ran while one was open for 0% -> 0% of each run, Pallas kernels for 5% -> 5%
where the time goes in v14:
time: 129 us
  blocking collectives  94 us (73%)
  starting transfers between devices  17.5 us (14%)
  Pallas kernels  9.73 us (8%)
  waiting for transfers between devices  5.98 us (5%)
    all_gather x3, blocking collectives, gather(): lax.all_gather(value, 'col', axis=0, tiled=True, axis_index_groups=groups)  82 us
    all_to_all x2, starting transfers between devices, exchange(): lax.all_to_all(value, axis, split_axis=0, concat_axis=0, tiled=True, axis...  13.7 us
    all_to_all x1, blocking collectives, exchange(): lax.all_to_all(value, axis, split_axis=0, concat_axis=0, tiled=True, axis...  12 us
    pallas_call x6, Pallas kernels, call(): pl.pallas_call(kernel, out_shape=[jax.ShapeDtypeStruct(shape, dtype) for...  6.45 us
    ppermute x2, waiting for transfers between devices, lines(): return (own, lax.ppermute(own, 'col', SWAP))  4.49 us
    ppermute x2, starting transfers between devices, lines(): return (own, lax.ppermute(own, 'col', SWAP))  3.82 us
    pallas_call x1, Pallas kernels, pack(): pl.pallas_call(pack_kernel, out_shape=jax.ShapeDtypeStruct((2, BANDS, CLA...  3.28 us
  transfers between devices with their start and end apart: 4, of which 3 were waited for; matrix products, arithmetic and copies ran while one was open for 0% of the time, Pallas kernels for 5%

profile of v14, /device:TPU:1, one launch (start us, length us, event | category | flops | bytes accessed | tf_op | source)
XLA Modules:
  0.0 128.7 jit_solution(15464870773295536556)
XLA Ops:
  0.0 0.0 copy-start.1
  0.0 0.8 copy-done.1
  0.8 0.7 copies.1
  1.4 5.4 %all-to-all-start = ((bf16[4,128,128]{2,1,0:T(8,128)(2,1)}), bf16[4,128,128]{2,1,0:T(8,128)(2,1)S(1)}, u32[]{:S(2)}, u32[]{:S(2)}) async-start(bf16[4,128,128]{2,1,0:T(8,128)(2,1)} %copies.1), calls=%async_computation | async-start | bytes 262144 | tf_op jit(solution)/shard_map/all_to_all | solution.py:193
  6.8 3.3 %pack.1 = bf16[2,8,4,128,128]{4,3,2,1,0:T(8,128)(2,1)} custom-call(s32[8,96]{1,0:T(8,128)} %cols_ref.11, bf16[8,12,128,128]{3,2,1,0:T(8,128)(2,1)} %bitcast.38), custom_call_target="tpu_custom_call" | custom-call | bytes 5242880 | tf_op jit(solution)/shard_map/pack/pallas_call | solution.py:84
  10.1 1.5 %all-to-all-done.line_ref = bf16[4,128,128]{2,1,0:T(8,128)(2,1)S(1)} async-done(((bf16[4,128,128]{2,1,0:T(8,128)(2,1)}), bf16[4,128,128]{2,1,0:T(8,128)(2,1)S(1)}, u32[]{:S(2)}, u32[]{:S(2)}) %all-to-all-start) | async-done | bytes 131104 | tf_op jit(solution)/shard_map/all_to_all | solution.py:193
  11.6 0.0 copy-start
  11.6 8.3 %all-to-all-start.1 = ((bf16[16,4,128,128]{3,2,1,0:T(8,128)(2,1)}), bf16[16,4,128,128]{3,2,1,0:T(8,128)(2,1)S(1)}, u32[]{:S(2)}, u32[]{:S(2)}) async-start(bf16[16,4,128,128]{3,2,1,0:T(8,128)(2,1)} %bitcast.37), calls=%async_computation.1 | async-start | bytes 4194304 | tf_op jit(solution)/shard_map/all_to_all | solution.py:193
  19.9 0.0 copy-done
  19.9 0.6 choose.1
  20.5 38.4 %all_gather.9.own_ref = bf16[24,128,128]{2,1,0:T(8,128)(2,1)S(1)} all-gather(bf16[2,128,128]{2,1,0:T(8,128)(2,1)S(1)} %choose.1), channel_id=1, replica_groups={{0,8,16,24,32,40,49,57,65,73,81,89},{1,9,17,25,33,41,48,56,64,72,80,88}..., dimensions={0}, use_global_device_ids=true | all-gather | bytes 851968 | tf_op jit(solution)/shard_map/all_gather | solution.py:189
  58.9 1.9 %collective-permute-start = (bf16[24,128,128]{2,1,0:T(8,128)(2,1)S(1)}, bf16[24,128,128]{2,1,0:T(8,128)(2,1)S(1)}, u32[]{:S(2)}, u32[]{:S(2)}) collective-permute-start(bf16[24,128,128]{2,1,0:T(8,128)(2,1)S(1)} %all_gather.9.own_ref), channel_id=1, source_target_pairs={{0,1},{1,0},{2,3},{3,2},{4,5},{5,4},{6,7},{7,6},{8,9},{9,8},{10,11... | collective-permute-start | bytes 2359304 | tf_op jit(solution)/shard_map/ppermute | solution.py:198
  60.8 2.3 %collective-permute-done.other_ref = bf16[24,128,128]{2,1,0:T(8,128)(2,1)S(1)} collective-permute-done((bf16[24,128,128]{2,1,0:T(8,128)(2,1)S(1)}, bf16[24,128,128]{2,1,0:T(8,128)(2,1)S(1)}, u32[]{:S(2)}, u32[]{:S(2)}) %collective-permute-start) | collective-permute-done | bytes 786464 | tf_op jit(solution)/shard_map/ppermute | solution.py:198
  63.1 2.2 %pick.1 = (bf16[128,4096]{1,0:T(8,128)(2,1)S(1)}, f32[2,1,128]{2,1,0:T(1,128)S(1)}, s32[32]{0:T(128)S(1)}) custom-call(s32[8,96]{1,0:T(8,128)S(1)} %copy-done, bf16[24,128,128]{2,1,0:T(8,128)(2,1)S(1)} %all_gather.9.own_ref, bf16[24,128,128]{2,1,0:T(8,128)(2,1)S(1)} %collective-permute-done.other_ref), custom_call_target="tpu_custom_call" | custom-call | tf_op jit(solution)/shard_map/pick/pallas_call | solution.py:177
  65.3 0.0 all-to-all-done.1
  65.3 1.1 multiply.1
  66.4 12.0 %all_to_all.15.shares_ref = f32[4,128,128]{2,1,0:T(8,128)S(1)} all-to-all(f32[4,128,128]{2,1,0:T(8,128)S(1)} %multiply.1), channel_id=1, replica_groups={{0,2,4,6},{1,3,5,7},{8,10,12,14},{9,11,13,15},{16,18,20,22},{17,19,21,2..., dimensions={0} | all-to-all | bytes 524288 | tf_op jit(solution)/shard_map/all_to_all | solution.py:193
  78.4 0.6 square.1
  79.0 39.4 %all_gather.10.own_ref = bf16[24,128,128]{2,1,0:T(8,128)(2,1)S(1)} all-gather(bf16[2,128,128]{2,1,0:T(8,128)(2,1)S(1)} %get-tuple-element.19), channel_id=1, replica_groups={{0,8,16,24,32,40,49,57,65,73,81,89},{1,9,17,25,33,41,48,56,64,72,80,88}..., dimensions={0}, use_global_device_ids=true | all-gather | bytes 851968 | tf_op jit(solution)/shard_map/all_gather | solution.py:189
  118.4 1.9 %collective-permute-start.1 = (bf16[24,128,128]{2,1,0:T(8,128)(2,1)S(1)}, bf16[24,128,128]{2,1,0:T(8,128)(2,1)S(1)}, u32[]{:S(2)}, u32[]{:S(2)}) collective-permute-start(bf16[24,128,128]{2,1,0:T(8,128)(2,1)S(1)} %all_gather.10.own_ref), channel_id=1, source_target_pairs={{0,1},{1,0},{2,3},{3,2},{4,5},{5,4},{6,7},{7,6},{8,9},{9,8},{10,11... | collective-permute-start | bytes 2359304 | tf_op jit(solution)/shard_map/ppermute | solution.py:198
  120.4 2.2 %collective-permute-done.1.other_ref = bf16[24,128,128]{2,1,0:T(8,128)(2,1)S(1)} collective-permute-done((bf16[24,128,128]{2,1,0:T(8,128)(2,1)S(1)}, bf16[24,128,128]{2,1,0:T(8,128)(2,1)S(1)}, u32[]{:S(2)}, u32[]{:S(2)}) %collective-permute-start.1) | collective-permute-done | bytes 786464 | tf_op jit(solution)/shard_map/ppermute | solution.py:198
  122.6 1.2 partials.1
  123.8 4.2 %all_gather.11 = f32[2,128,128]{2,1,0:T(8,128)S(1)} all-gather(f32[1,128,128]{2,1,0:T(8,128)S(1)} %get-tuple-element.22), channel_id=1, replica_groups={{0,2},{1,3},{4,6},{5,7},{8,10},{9,11},{12,14},{13,15},{16,18},{17,19},{..., dimensions={0}, use_global_device_ids=true | all-gather | bytes 196608 | tf_op jit(solution)/shard_map/all_gather | solution.py:189
  128.1 0.6 fusion.7
  (1 shorter events, 0.0 us)
Async XLA Ops:
  0.0 0.8 copy-start.1
  1.4 10.2 %all-to-all-start = ((bf16[4,128,128]{2,1,0:T(8,128)(2,1)}), bf16[4,128,128]{2,1,0:T(8,128)(2,1)S(1)}, u32[]{:S(2)}, u32[]{:S(2)}) async-start(bf16[4,128,128]{2,1,0:T(8,128)(2,1)} %copies.1), calls=%async_computation | async-start | bytes 262144 | tf_op jit(solution)/shard_map/all_to_all | solution.py:193
  11.6 8.3 %copy-start = (s32[8,96]{1,0:T(8,128)S(1)}, s32[8,96]{1,0:T(8,128)}, u32[]{:S(2)}) copy-start(s32[8,96]{1,0:T(8,128)} %cols_ref.11) | copy-start | bytes 9220
  11.6 53.7 %all-to-all-start.1 = ((bf16[16,4,128,128]{3,2,1,0:T(8,128)(2,1)}), bf16[16,4,128,128]{3,2,1,0:T(8,128)(2,1)S(1)}, u32[]{:S(2)}, u32[]{:S(2)}) async-start(bf16[16,4,128,128]{3,2,1,0:T(8,128)(2,1)} %bitcast.37), calls=%async_computation.1 | async-start | bytes 4194304 | tf_op jit(solution)/shard_map/all_to_all | solution.py:193
  58.9 4.2 %collective-permute-start = (bf16[24,128,128]{2,1,0:T(8,128)(2,1)S(1)}, bf16[24,128,128]{2,1,0:T(8,128)(2,1)S(1)}, u32[]{:S(2)}, u32[]{:S(2)}) collective-permute-start(bf16[24,128,128]{2,1,0:T(8,128)(2,1)S(1)} %all_gather.9.own_ref), channel_id=1, source_target_pairs={{0,1},{1,0},{2,3},{3,2},{4,5},{5,4},{6,7},{7,6},{8,9},{9,8},{10,11... | collective-permute-start | bytes 2359304 | tf_op jit(solution)/shard_map/ppermute | solution.py:198
  118.4 4.2 %collective-permute-start.1 = (bf16[24,128,128]{2,1,0:T(8,128)(2,1)S(1)}, bf16[24,128,128]{2,1,0:T(8,128)(2,1)S(1)}, u32[]{:S(2)}, u32[]{:S(2)}) collective-permute-start(bf16[24,128,128]{2,1,0:T(8,128)(2,1)S(1)} %all_gather.10.own_ref), channel_id=1, source_target_pairs={{0,1},{1,0},{2,3},{3,2},{4,5},{5,4},{6,7},{7,6},{8,9},{9,8},{10,11... | collective-permute-start | bytes 2359304 | tf_op jit(solution)/shard_map/ppermute | solution.py:198

commit v15 on v14

--- a/solution.py
+++ b/solution.py
@@ -23,7 +23,8 @@
 
 Y_LINES = [[col_of(z, y, c) for y in range(Y)] for z in range(Z) for c in range(C)]
 Y_NEAR = [[col_of(z, 2 * h + p, c) for p in range(2)] for z in range(Z) for h in range(2) for c in range(C)]
-Z_LINES = [[col_of(z, y, (2 * z // Z + c) % C) for z in range(Z)] for y in range(Y) for c in range(C)]
+TURN = 7
+Z_LINES = [[col_of(z, y, (z // TURN + c) % C) for z in range(Z)] for y in range(Y) for c in range(C)]
 SWAP = [(s, s ^ 1) for s in range(N_COL)]
 SPREAD = [[row * N_COL + col for col in pair for row in range(BANDS)] for pair in Y_NEAR]
 
@@ -112,10 +113,10 @@
 
 def list_picks(cols_ref, list_ref, picks_ref):
     row, col, core, near = place()
-    line = lax.rem(col // (N_COL // 2) + core, 2)
+    line = lax.rem(col // (TURN * Y * C) + core, 2)
     for band in range(BANDS):
         where = lambda quad, c, _, band=band: (
-            band * 3 + quad + QUADS * lax.rem(line + c + 2 * (band * 3 + quad) // QUADS, 2)
+            band * 3 + quad + QUADS * lax.rem(line + c + (band * 3 + quad) // (2 * TURN), 2)
         )
         count = list_live(cols_ref, list_ref, row, band, near, where)
         for j in range(CLASS):

time: 129 us -> 130 us (level)
  no operation moved by 1% of the time
where the time goes in v15:
time: 130 us; the launch traced here: 129 us
  blocking collectives  94.4 us (73%)
  starting transfers between devices  17.5 us (13%)
  Pallas kernels  9.74 us (7%)
  waiting for transfers between devices  5.98 us (5%)
    all_gather x3, blocking collectives, gather(): lax.all_gather(value, 'col', axis=0, tiled=True, axis_index_groups=groups)  82.5 us
    all_to_all x2, starting transfers between devices, exchange(): lax.all_to_all(value, axis, split_axis=0, concat_axis=0, tiled=True, axis...  13.7 us
    all_to_all x1, blocking collectives, exchange(): lax.all_to_all(value, axis, split_axis=0, concat_axis=0, tiled=True, axis...  12 us
    pallas_call x6, Pallas kernels, call(): pl.pallas_call(kernel, out_shape=[jax.ShapeDtypeStruct(shape, dtype) for...  6.46 us
    ppermute x2, waiting for transfers between devices, lines(): return (own, lax.ppermute(own, 'col', SWAP))  4.49 us
    ppermute x2, starting transfers between devices, lines(): return (own, lax.ppermute(own, 'col', SWAP))  3.82 us
    pallas_call x1, Pallas kernels, pack(): pl.pallas_call(pack_kernel, out_shape=jax.ShapeDtypeStruct((2, BANDS, CLA...  3.28 us
  transfers between devices with their start and end apart: 4, of which 3 were waited for; matrix products, arithmetic and copies ran while one was open for 0% of the time, Pallas kernels for 5%

profile of v15, /device:TPU:1, one launch (start us, length us, event | category | flops | bytes accessed | tf_op | source)
XLA Modules:
  0.0 129.2 jit_solution(12092726360108523958)
XLA Ops:
  0.0 0.0 copy-start.1
  0.0 0.8 copy-done.1
  0.8 0.7 copies.1
  1.4 5.4 %all-to-all-start = ((bf16[4,128,128]{2,1,0:T(8,128)(2,1)}), bf16[4,128,128]{2,1,0:T(8,128)(2,1)S(1)}, u32[]{:S(2)}, u32[]{:S(2)}) async-start(bf16[4,128,128]{2,1,0:T(8,128)(2,1)} %copies.1), calls=%async_computation | async-start | bytes 262144 | tf_op jit(solution)/shard_map/all_to_all | solution.py:194
  6.8 3.3 %pack.1 = bf16[2,8,4,128,128]{4,3,2,1,0:T(8,128)(2,1)} custom-call(s32[8,96]{1,0:T(8,128)} %cols_ref.11, bf16[8,12,128,128]{3,2,1,0:T(8,128)(2,1)} %bitcast.38), custom_call_target="tpu_custom_call" | custom-call | bytes 5242880 | tf_op jit(solution)/shard_map/pack/pallas_call | solution.py:85
  10.1 1.5 %all-to-all-done.line_ref = bf16[4,128,128]{2,1,0:T(8,128)(2,1)S(1)} async-done(((bf16[4,128,128]{2,1,0:T(8,128)(2,1)}), bf16[4,128,128]{2,1,0:T(8,128)(2,1)S(1)}, u32[]{:S(2)}, u32[]{:S(2)}) %all-to-all-start) | async-done | bytes 131104 | tf_op jit(solution)/shard_map/all_to_all | solution.py:194
  11.6 0.0 copy-start
  11.6 8.3 %all-to-all-start.1 = ((bf16[16,4,128,128]{3,2,1,0:T(8,128)(2,1)}), bf16[16,4,128,128]{3,2,1,0:T(8,128)(2,1)S(1)}, u32[]{:S(2)}, u32[]{:S(2)}) async-start(bf16[16,4,128,128]{3,2,1,0:T(8,128)(2,1)} %bitcast.37), calls=%async_computation.1 | async-start | bytes 4194304 | tf_op jit(solution)/shard_map/all_to_all | solution.py:194
  19.9 0.0 copy-done
  19.9 0.6 choose.1
  20.5 38.4 %all_gather.9.own_ref = bf16[24,128,128]{2,1,0:T(8,128)(2,1)S(1)} all-gather(bf16[2,128,128]{2,1,0:T(8,128)(2,1)S(1)} %choose.1), channel_id=1, replica_groups={{0,8,16,24,32,40,48,57,65,73,81,89},{1,9,17,25,33,41,49,56,64,72,80,88}..., dimensions={0}, use_global_device_ids=true | all-gather | bytes 851968 | tf_op jit(solution)/shard_map/all_gather | solution.py:190
  58.9 1.9 %collective-permute-start = (bf16[24,128,128]{2,1,0:T(8,128)(2,1)S(1)}, bf16[24,128,128]{2,1,0:T(8,128)(2,1)S(1)}, u32[]{:S(2)}, u32[]{:S(2)}) collective-permute-start(bf16[24,128,128]{2,1,0:T(8,128)(2,1)S(1)} %all_gather.9.own_ref), channel_id=1, source_target_pairs={{0,1},{1,0},{2,3},{3,2},{4,5},{5,4},{6,7},{7,6},{8,9},{9,8},{10,11... | collective-permute-start | bytes 2359304 | tf_op jit(solution)/shard_map/ppermute | solution.py:199
  60.8 2.3 %collective-permute-done.other_ref = bf16[24,128,128]{2,1,0:T(8,128)(2,1)S(1)} collective-permute-done((bf16[24,128,128]{2,1,0:T(8,128)(2,1)S(1)}, bf16[24,128,128]{2,1,0:T(8,128)(2,1)S(1)}, u32[]{:S(2)}, u32[]{:S(2)}) %collective-permute-start) | collective-permute-done | bytes 786464 | tf_op jit(solution)/shard_map/ppermute | solution.py:199
  63.1 2.2 %pick.1 = (bf16[128,4096]{1,0:T(8,128)(2,1)S(1)}, f32[2,1,128]{2,1,0:T(1,128)S(1)}, s32[32]{0:T(128)S(1)}) custom-call(s32[8,96]{1,0:T(8,128)S(1)} %copy-done, bf16[24,128,128]{2,1,0:T(8,128)(2,1)S(1)} %all_gather.9.own_ref, bf16[24,128,128]{2,1,0:T(8,128)(2,1)S(1)} %collective-permute-done.other_ref), custom_call_target="tpu_custom_call" | custom-call | tf_op jit(solution)/shard_map/pick/pallas_call | solution.py:178
  65.3 0.0 all-to-all-done.1
  65.3 1.1 multiply.1
  66.4 12.0 %all_to_all.15.shares_ref = f32[4,128,128]{2,1,0:T(8,128)S(1)} all-to-all(f32[4,128,128]{2,1,0:T(8,128)S(1)} %multiply.1), channel_id=1, replica_groups={{0,2,4,6},{1,3,5,7},{8,10,12,14},{9,11,13,15},{16,18,20,22},{17,19,21,2..., dimensions={0} | all-to-all | bytes 524288 | tf_op jit(solution)/shard_map/all_to_all | solution.py:194
  78.4 0.6 square.1
  79.0 39.9 %all_gather.10.own_ref = bf16[24,128,128]{2,1,0:T(8,128)(2,1)S(1)} all-gather(bf16[2,128,128]{2,1,0:T(8,128)(2,1)S(1)} %get-tuple-element.19), channel_id=1, replica_groups={{0,8,16,24,32,40,48,57,65,73,81,89},{1,9,17,25,33,41,49,56,64,72,80,88}..., dimensions={0}, use_global_device_ids=true | all-gather | bytes 851968 | tf_op jit(solution)/shard_map/all_gather | solution.py:190
  118.9 1.9 %collective-permute-start.1 = (bf16[24,128,128]{2,1,0:T(8,128)(2,1)S(1)}, bf16[24,128,128]{2,1,0:T(8,128)(2,1)S(1)}, u32[]{:S(2)}, u32[]{:S(2)}) collective-permute-start(bf16[24,128,128]{2,1,0:T(8,128)(2,1)S(1)} %all_gather.10.own_ref), channel_id=1, source_target_pairs={{0,1},{1,0},{2,3},{3,2},{4,5},{5,4},{6,7},{7,6},{8,9},{9,8},{10,11... | collective-permute-start | bytes 2359304 | tf_op jit(solution)/shard_map/ppermute | solution.py:199
  120.8 2.2 %collective-permute-done.1.other_ref = bf16[24,128,128]{2,1,0:T(8,128)(2,1)S(1)} collective-permute-done((bf16[24,128,128]{2,1,0:T(8,128)(2,1)S(1)}, bf16[24,128,128]{2,1,0:T(8,128)(2,1)S(1)}, u32[]{:S(2)}, u32[]{:S(2)}) %collective-permute-start.1) | collective-permute-done | bytes 786464 | tf_op jit(solution)/shard_map/ppermute | solution.py:199
  123.1 1.2 partials.1
  124.3 4.2 %all_gather.11 = f32[2,128,128]{2,1,0:T(8,128)S(1)} all-gather(f32[1,128,128]{2,1,0:T(8,128)S(1)} %get-tuple-element.22), channel_id=1, replica_groups={{0,2},{1,3},{4,6},{5,7},{8,10},{9,11},{12,14},{13,15},{16,18},{17,19},{..., dimensions={0}, use_global_device_ids=true | all-gather | bytes 196608 | tf_op jit(solution)/shard_map/all_gather | solution.py:190
  128.5 0.6 fusion.7
  (1 shorter events, 0.0 us)
Async XLA Ops:
  0.0 0.8 copy-start.1
  1.4 10.2 %all-to-all-start = ((bf16[4,128,128]{2,1,0:T(8,128)(2,1)}), bf16[4,128,128]{2,1,0:T(8,128)(2,1)S(1)}, u32[]{:S(2)}, u32[]{:S(2)}) async-start(bf16[4,128,128]{2,1,0:T(8,128)(2,1)} %copies.1), calls=%async_computation | async-start | bytes 262144 | tf_op jit(solution)/shard_map/all_to_all | solution.py:194
  11.6 8.3 %copy-start = (s32[8,96]{1,0:T(8,128)S(1)}, s32[8,96]{1,0:T(8,128)}, u32[]{:S(2)}) copy-start(s32[8,96]{1,0:T(8,128)} %cols_ref.11) | copy-start | bytes 9220
  11.6 53.7 %all-to-all-start.1 = ((bf16[16,4,128,128]{3,2,1,0:T(8,128)(2,1)}), bf16[16,4,128,128]{3,2,1,0:T(8,128)(2,1)S(1)}, u32[]{:S(2)}, u32[]{:S(2)}) async-start(bf16[16,4,128,128]{3,2,1,0:T(8,128)(2,1)} %bitcast.37), calls=%async_computation.1 | async-start | bytes 4194304 | tf_op jit(solution)/shard_map/all_to_all | solution.py:194
  58.9 4.2 %collective-permute-start = (bf16[24,128,128]{2,1,0:T(8,128)(2,1)S(1)}, bf16[24,128,128]{2,1,0:T(8,128)(2,1)S(1)}, u32[]{:S(2)}, u32[]{:S(2)}) collective-permute-start(bf16[24,128,128]{2,1,0:T(8,128)(2,1)S(1)} %all_gather.9.own_ref), channel_id=1, source_target_pairs={{0,1},{1,0},{2,3},{3,2},{4,5},{5,4},{6,7},{7,6},{8,9},{9,8},{10,11... | collective-permute-start | bytes 2359304 | tf_op jit(solution)/shard_map/ppermute | solution.py:199
  118.9 4.2 %collective-permute-start.1 = (bf16[24,128,128]{2,1,0:T(8,128)(2,1)S(1)}, bf16[24,128,128]{2,1,0:T(8,128)(2,1)S(1)}, u32[]{:S(2)}, u32[]{:S(2)}) collective-permute-start(bf16[24,128,128]{2,1,0:T(8,128)(2,1)S(1)} %all_gather.10.own_ref), channel_id=1, source_target_pairs={{0,1},{1,0},{2,3},{3,2},{4,5},{5,4},{6,7},{7,6},{8,9},{9,8},{10,11... | collective-permute-start | bytes 2359304 | tf_op jit(solution)/shard_map/ppermute | solution.py:199

commit v16 on v14

--- a/solution.py
+++ b/solution.py
@@ -205,7 +205,7 @@
     shares = [(block, jnp.float32), ((1,) + block, jnp.float32)]
 
     packed = pack(win_cols, couple_vals[0, 0])
-    (line,) = call(copies_kernel, "copies", [((Y,) + block, jnp.bfloat16)], (win_vals[0],))
+    line = jnp.broadcast_to(win_vals[0], (Y,) + block)
     line = exchange(line, "col", Y_LINES)
     line, packed = lax.optimization_barrier((line, packed))
     held = exchange(packed.reshape((2 * BANDS, CLASS) + block), ("row", "col"), SPREAD)

time: 129 us -> 129 us (level)
    broadcast_in_dim x0 -> x1, local copies, waits for them, and re-layouts: none -> 1.43 us  [on_device(): line = jnp.broadcast_to(win_vals[0], (Y,) + block)]
    pallas_call x6 -> x5, Pallas kernels: 6.45 us -> 5.79 us  [call(): pl.pallas_call(kernel, out_shape=[jax.ShapeDtypeStruct(shape, dtype) for...]
where the time goes in v16:
time: 129 us
  blocking collectives  94 us (73%)
  starting transfers between devices  17.5 us (14%)
  Pallas kernels  9.07 us (7%)
  waiting for transfers between devices  5.98 us (5%)
  local copies, waits for them, and re-layouts  1.43 us (1%)
    all_gather x3, blocking collectives, gather(): lax.all_gather(value, 'col', axis=0, tiled=True, axis_index_groups=groups)  82 us
    all_to_all x2, starting transfers between devices, exchange(): lax.all_to_all(value, axis, split_axis=0, concat_axis=0, tiled=True, axis...  13.7 us
    all_to_all x1, blocking collectives, exchange(): lax.all_to_all(value, axis, split_axis=0, concat_axis=0, tiled=True, axis...  12 us
    pallas_call x5, Pallas kernels, call(): pl.pallas_call(kernel, out_shape=[jax.ShapeDtypeStruct(shape, dtype) for...  5.79 us
    ppermute x2, waiting for transfers between devices, lines(): return (own, lax.ppermute(own, 'col', SWAP))  4.49 us
    ppermute x2, starting transfers between devices, lines(): return (own, lax.ppermute(own, 'col', SWAP))  3.82 us
    pallas_call x1, Pallas kernels, pack(): pl.pallas_call(pack_kernel, out_shape=jax.ShapeDtypeStruct((2, BANDS, CLA...  3.28 us
  transfers between devices with their start and end apart: 4, of which 3 were waited for; matrix products, arithmetic and copies ran while one was open for 0% of the time, Pallas kernels for 5%

profile of v16, /device:TPU:1, one launch (start us, length us, event | category | flops | bytes accessed | tf_op | source)
XLA Modules:
  0.0 128.7 jit_solution(15434743173439141886)
XLA Ops:
  0.0 1.4 %broadcast_in_dim.11 = bf16[4,128,128]{2,1,0:T(8,128)(2,1)} broadcast(bf16[128,128]{1,0:T(8,128)(2,1)} %bitcast.38), dimensions={1,2} | broadcast | bytes 163840 | tf_op jit(solution)/shard_map/broadcast_in_dim | solution.py:208
  1.4 5.4 %all-to-all-start = ((bf16[4,128,128]{2,1,0:T(8,128)(2,1)}), bf16[4,128,128]{2,1,0:T(8,128)(2,1)S(1)}, u32[]{:S(2)}, u32[]{:S(2)}) async-start(bf16[4,128,128]{2,1,0:T(8,128)(2,1)} %broadcast_in_dim.11), calls=%async_computation | async-start | bytes 262144 | tf_op jit(solution)/shard_map/all_to_all | solution.py:193
  6.8 3.3 %pack.1 = bf16[2,8,4,128,128]{4,3,2,1,0:T(8,128)(2,1)} custom-call(s32[8,96]{1,0:T(8,128)} %cols_ref.11, bf16[8,12,128,128]{3,2,1,0:T(8,128)(2,1)} %bitcast.37), custom_call_target="tpu_custom_call" | custom-call | bytes 5242880 | tf_op jit(solution)/shard_map/pack/pallas_call | solution.py:84
  10.1 1.5 %all-to-all-done.line_ref = bf16[4,128,128]{2,1,0:T(8,128)(2,1)S(1)} async-done(((bf16[4,128,128]{2,1,0:T(8,128)(2,1)}), bf16[4,128,128]{2,1,0:T(8,128)(2,1)S(1)}, u32[]{:S(2)}, u32[]{:S(2)}) %all-to-all-start) | async-done | bytes 131104 | tf_op jit(solution)/shard_map/all_to_all | solution.py:193
  11.6 0.0 copy-start
  11.6 8.3 %all-to-all-start.1 = ((bf16[16,4,128,128]{3,2,1,0:T(8,128)(2,1)}), bf16[16,4,128,128]{3,2,1,0:T(8,128)(2,1)S(1)}, u32[]{:S(2)}, u32[]{:S(2)}) async-start(bf16[16,4,128,128]{3,2,1,0:T(8,128)(2,1)} %bitcast.36), calls=%async_computation.1 | async-start | bytes 4194304 | tf_op jit(solution)/shard_map/all_to_all | solution.py:193
  19.9 0.0 copy-done
  19.9 0.6 choose.1
  20.5 38.4 %all_gather.9.own_ref = bf16[24,128,128]{2,1,0:T(8,128)(2,1)S(1)} all-gather(bf16[2,128,128]{2,1,0:T(8,128)(2,1)S(1)} %choose.1), channel_id=1, replica_groups={{0,8,16,24,32,40,49,57,65,73,81,89},{1,9,17,25,33,41,48,56,64,72,80,88}..., dimensions={0}, use_global_device_ids=true | all-gather | bytes 851968 | tf_op jit(solution)/shard_map/all_gather | solution.py:189
  58.9 1.9 %collective-permute-start = (bf16[24,128,128]{2,1,0:T(8,128)(2,1)S(1)}, bf16[24,128,128]{2,1,0:T(8,128)(2,1)S(1)}, u32[]{:S(2)}, u32[]{:S(2)}) collective-permute-start(bf16[24,128,128]{2,1,0:T(8,128)(2,1)S(1)} %all_gather.9.own_ref), channel_id=1, source_target_pairs={{0,1},{1,0},{2,3},{3,2},{4,5},{5,4},{6,7},{7,6},{8,9},{9,8},{10,11... | collective-permute-start | bytes 2359304 | tf_op jit(solution)/shard_map/ppermute | solution.py:198
  60.8 2.3 %collective-permute-done.other_ref = bf16[24,128,128]{2,1,0:T(8,128)(2,1)S(1)} collective-permute-done((bf16[24,128,128]{2,1,0:T(8,128)(2,1)S(1)}, bf16[24,128,128]{2,1,0:T(8,128)(2,1)S(1)}, u32[]{:S(2)}, u32[]{:S(2)}) %collective-permute-start) | collective-permute-done | bytes 786464 | tf_op jit(solution)/shard_map/ppermute | solution.py:198
  63.1 2.2 %pick.1 = (bf16[128,4096]{1,0:T(8,128)(2,1)S(1)}, f32[2,1,128]{2,1,0:T(1,128)S(1)}, s32[32]{0:T(128)S(1)}) custom-call(s32[8,96]{1,0:T(8,128)S(1)} %copy-done, bf16[24,128,128]{2,1,0:T(8,128)(2,1)S(1)} %all_gather.9.own_ref, bf16[24,128,128]{2,1,0:T(8,128)(2,1)S(1)} %collective-permute-done.other_ref), custom_call_target="tpu_custom_call" | custom-call | tf_op jit(solution)/shard_map/pick/pallas_call | solution.py:177
  65.3 0.0 all-to-all-done.1
  65.3 1.1 multiply.1
  66.4 12.0 %all_to_all.15.shares_ref = f32[4,128,128]{2,1,0:T(8,128)S(1)} all-to-all(f32[4,128,128]{2,1,0:T(8,128)S(1)} %multiply.1), channel_id=1, replica_groups={{0,2,4,6},{1,3,5,7},{8,10,12,14},{9,11,13,15},{16,18,20,22},{17,19,21,2..., dimensions={0} | all-to-all | bytes 524288 | tf_op jit(solution)/shard_map/all_to_all | solution.py:193
  78.4 0.6 square.1
  79.0 39.4 %all_gather.10.own_ref = bf16[24,128,128]{2,1,0:T(8,128)(2,1)S(1)} all-gather(bf16[2,128,128]{2,1,0:T(8,128)(2,1)S(1)} %get-tuple-element.19), channel_id=1, replica_groups={{0,8,16,24,32,40,49,57,65,73,81,89},{1,9,17,25,33,41,48,56,64,72,80,88}..., dimensions={0}, use_global_device_ids=true | all-gather | bytes 851968 | tf_op jit(solution)/shard_map/all_gather | solution.py:189
  118.4 1.9 %collective-permute-start.1 = (bf16[24,128,128]{2,1,0:T(8,128)(2,1)S(1)}, bf16[24,128,128]{2,1,0:T(8,128)(2,1)S(1)}, u32[]{:S(2)}, u32[]{:S(2)}) collective-permute-start(bf16[24,128,128]{2,1,0:T(8,128)(2,1)S(1)} %all_gather.10.own_ref), channel_id=1, source_target_pairs={{0,1},{1,0},{2,3},{3,2},{4,5},{5,4},{6,7},{7,6},{8,9},{9,8},{10,11... | collective-permute-start | bytes 2359304 | tf_op jit(solution)/shard_map/ppermute | solution.py:198
  120.4 2.2 %collective-permute-done.1.other_ref = bf16[24,128,128]{2,1,0:T(8,128)(2,1)S(1)} collective-permute-done((bf16[24,128,128]{2,1,0:T(8,128)(2,1)S(1)}, bf16[24,128,128]{2,1,0:T(8,128)(2,1)S(1)}, u32[]{:S(2)}, u32[]{:S(2)}) %collective-permute-start.1) | collective-permute-done | bytes 786464 | tf_op jit(solution)/shard_map/ppermute | solution.py:198
  122.6 1.2 partials.1
  123.8 4.2 %all_gather.11 = f32[2,128,128]{2,1,0:T(8,128)S(1)} all-gather(f32[1,128,128]{2,1,0:T(8,128)S(1)} %get-tuple-element.22), channel_id=1, replica_groups={{0,2},{1,3},{4,6},{5,7},{8,10},{9,11},{12,14},{13,15},{16,18},{17,19},{..., dimensions={0}, use_global_device_ids=true | all-gather | bytes 196608 | tf_op jit(solution)/shard_map/all_gather | solution.py:189
  128.0 0.6 fusion.7
  (1 shorter events, 0.0 us)
Async XLA Ops:
  1.4 10.2 %all-to-all-start = ((bf16[4,128,128]{2,1,0:T(8,128)(2,1)}), bf16[4,128,128]{2,1,0:T(8,128)(2,1)S(1)}, u32[]{:S(2)}, u32[]{:S(2)}) async-start(bf16[4,128,128]{2,1,0:T(8,128)(2,1)} %broadcast_in_dim.11), calls=%async_computation | async-start | bytes 262144 | tf_op jit(solution)/shard_map/all_to_all | solution.py:193
  11.6 8.3 %copy-start = (s32[8,96]{1,0:T(8,128)S(1)}, s32[8,96]{1,0:T(8,128)}, u32[]{:S(2)}) copy-start(s32[8,96]{1,0:T(8,128)} %cols_ref.11) | copy-start | bytes 9220
  11.6 53.7 %all-to-all-start.1 = ((bf16[16,4,128,128]{3,2,1,0:T(8,128)(2,1)}), bf16[16,4,128,128]{3,2,1,0:T(8,128)(2,1)S(1)}, u32[]{:S(2)}, u32[]{:S(2)}) async-start(bf16[16,4,128,128]{3,2,1,0:T(8,128)(2,1)} %bitcast.36), calls=%async_computation.1 | async-start | bytes 4194304 | tf_op jit(solution)/shard_map/all_to_all | solution.py:193
  58.9 4.2 %collective-permute-start = (bf16[24,128,128]{2,1,0:T(8,128)(2,1)S(1)}, bf16[24,128,128]{2,1,0:T(8,128)(2,1)S(1)}, u32[]{:S(2)}, u32[]{:S(2)}) collective-permute-start(bf16[24,128,128]{2,1,0:T(8,128)(2,1)S(1)} %all_gather.9.own_ref), channel_id=1, source_target_pairs={{0,1},{1,0},{2,3},{3,2},{4,5},{5,4},{6,7},{7,6},{8,9},{9,8},{10,11... | collective-permute-start | bytes 2359304 | tf_op jit(solution)/shard_map/ppermute | solution.py:198
  118.4 4.2 %collective-permute-start.1 = (bf16[24,128,128]{2,1,0:T(8,128)(2,1)S(1)}, bf16[24,128,128]{2,1,0:T(8,128)(2,1)S(1)}, u32[]{:S(2)}, u32[]{:S(2)}) collective-permute-start(bf16[24,128,128]{2,1,0:T(8,128)(2,1)S(1)} %all_gather.10.own_ref), channel_id=1, source_target_pairs={{0,1},{1,0},{2,3},{3,2},{4,5},{5,4},{6,7},{7,6},{8,9},{9,8},{10,11... | collective-permute-start | bytes 2359304 | tf_op jit(solution)/shard_map/ppermute | solution.py:198
